TPU v7x, 512 devices: a whole 4x4x16 slice. The times are simulated.
512 devices in a mesh: vocab: 32 (over x, y, core), dp: 16 (over z).
Axes of the slice: x: 4, y: 4, z: 16, core: 2. Of those that a mesh axis runs over, the one named last changes fastest.
Arguments:
- hidden: bfloat16 [2048, 2048], P('dp', 'vocab')
- head_weight: bfloat16 [2048, 65536], P('dp', 'vocab')
- teacher_logits: bfloat16 [2048, 65536], P('dp', 'vocab')
- target_ids: int32 [2048], P('dp'), may hold values from 0 to 65535
- segment_ids: int32 [16, 128], P('dp'), may hold values from 0 to 15, never falling along the last dimension, each value on 1 to 16 neighbouring positions
- pair_order: int32 [16, 16], P('dp'), may hold values from 0 to 15, each once within a row
Outputs:
- hidden_grad: bfloat16 [2048, 2048], P('dp', 'vocab')
- head_grad: float32 [2048, 65536], P('dp', 'vocab')
- loss: float32 [], replicated
Inputs may be any that keep to these rules, and one draw needn't show every extreme that they name: `segment_ids`: in each group the row's sequence number never falls along the rows, and every sequence has 1 to 16 rows. `pair_order`: each group's row is a permutation of its 16 sequences; pair p is entry 2p (chosen) and entry 2p + 1 (rejected).
All inputs are finite; a program needn't handle non-finite values.
Results may differ from a plain program's by a relative error of at most 0.018.
Values may be sent and summed in bfloat16 or wider, within the bound.
No kernel may reach another device: no remote copies, remote signals or barrier semaphores. Data moves between devices by JAX's collectives and lax.ppermute only.
A program may use at most 64 MiB of HBM per device.

v0:
```python
import jax
import jax.numpy as jnp
from jax import lax
from jax.sharding import PartitionSpec as P

dpo_beta = 0.1
dpo_gamma = 4.0


def pair_weights(log_ratio, segments, ordering):
    seq_count = ordering.shape[0]
    labels = lax.broadcasted_iota(jnp.int32, (1, seq_count), 1)
    seq_hot = (segments[:, None] == labels).astype(jnp.float32)
    seq_ratio = jnp.sum(seq_hot * log_ratio[:, None], axis=0)
    chosen = ordering[0::2]
    rejected = ordering[1::2]
    chosen_hot = (chosen[:, None] == labels).astype(jnp.float32)
    rejected_hot = (rejected[:, None] == labels).astype(jnp.float32)
    margin = dpo_beta * (
        jnp.sum(chosen_hot * seq_ratio[None, :], axis=1)
        - jnp.sum(rejected_hot * seq_ratio[None, :], axis=1)
    )
    strength = dpo_gamma * dpo_beta * jax.nn.sigmoid(-margin)
    coeffs = jnp.sum((rejected_hot - chosen_hot) * strength[:, None], axis=0)
    row_weight = jnp.sum(seq_hot * coeffs[None, :], axis=1)
    return (row_weight, jnp.sum(jax.nn.softplus(-margin)))


def on_device(hidden, head_weight, teacher_logits, target_ids, segment_ids, pair_order):
    rows_full = lax.all_gather(hidden, "vocab", axis=1, tiled=True)
    weight_full = lax.all_gather(head_weight, "dp", axis=0, tiled=True)
    student = jnp.dot(rows_full, weight_full, preferred_element_type=jnp.float32)
    teacher = teacher_logits.astype(jnp.float32)
    shard_width = student.shape[1]
    offset = lax.axis_index("vocab") * shard_width
    column = lax.broadcasted_iota(jnp.int32, student.shape, 1) + offset
    is_target = column == target_ids[:, None]
    local_target = jnp.sum(jnp.where(is_target, student, 0.0), axis=1)
    local_tgt_teach = jnp.sum(jnp.where(is_target, teacher, 0.0), axis=1)
    local_max = jnp.max(student, axis=1)
    local_tmax = jnp.max(teacher, axis=1)
    max_student, max_teacher = lax.pmax((local_max, local_tmax), "vocab")
    exp_student = jnp.exp(student - max_student[:, None])
    exp_teacher = jnp.exp(teacher - max_teacher[:, None])
    sum_student, sum_teacher, cross, target_student, target_teacher = lax.psum(
        (
            jnp.sum(exp_student, axis=1),
            jnp.sum(exp_teacher, axis=1),
            jnp.sum(exp_teacher * (teacher - student), axis=1),
            local_target,
            local_tgt_teach,
        ),
        "vocab",
    )
    lse_student = max_student + jnp.log(sum_student)
    lse_teacher = max_teacher + jnp.log(sum_teacher)
    kl_rows = cross / sum_teacher - lse_teacher + lse_student
    log_ratio = target_student - lse_student - (target_teacher - lse_teacher)
    row_weight, dpo_sum = pair_weights(log_ratio, segment_ids[0], pair_order[0])
    group_objective = jnp.sum(kl_rows) + dpo_gamma * dpo_sum
    summed_objective = lax.psum(group_objective, "dp")
    loss_value = summed_objective / (rows_full.shape[0] * lax.axis_size("dp"))
    prob_student = exp_student / sum_student[:, None]
    prob_teacher = exp_teacher / sum_teacher[:, None]
    logit_grad = (
        prob_student
        - prob_teacher
        + row_weight[:, None] * (is_target.astype(jnp.float32) - prob_student)
    ).astype(jnp.bfloat16)
    hidden_term = lax.dot_general(
        logit_grad, weight_full, (((1,), (1,)), ((), ())), preferred_element_type=jnp.float32
    )
    hidden_grad = lax.psum_scatter(
        hidden_term.astype(jnp.bfloat16), "vocab", scatter_dimension=1, tiled=True
    )
    grad_cols = lax.all_to_all(rows_full, "dp", split_axis=1, concat_axis=0, tiled=True)
    head_grad = lax.dot_general(
        grad_cols,
        lax.all_gather(logit_grad, "dp", axis=0, tiled=True),
        (((0,), (0,)), ((), ())),
        preferred_element_type=jnp.float32,
    )
    return (hidden_grad, head_grad, loss_value)


def solution(mesh):
    return jax.shard_map(
        on_device,
        mesh=mesh,
        in_specs=(
            P("dp", "vocab"),
            P("dp", "vocab"),
            P("dp", "vocab"),
            P("dp"),
            P("dp", None),
            P("dp", None),
        ),
        out_specs=(P("dp", "vocab"), P("dp", "vocab"), P()),
        check_vma=False,
    )
```

profile of v0, /device:TPU:2, one launch (start us, length us, event | category | flops | bytes accessed | tf_op | source)
XLA Modules:
  0.0 486.9 jit_solution(1537256044486397161)
XLA Ops:
  7.2 0.7 all-gather.3.cloned.1.call-update
  8.0 0.8 slice.7
  8.8 0.7 slice.6
  9.5 1.2 reduce_max.24
  10.7 29.9 %all_gather.9 = bf16[128,2048]{0,1:T(8,128)(2,1)} all-gather(bf16[128,64]{0,1:T(8,128)(2,1)} %param.6), channel_id=1, replica_groups=mesh['vocab'=32,'dp'=16] {'vocab'}, dimensions={1}, use_global_device_ids=true | all-gather | bytes 540672 | tf_op jit(solution)/shard_map/all_gather | solution.py:30
  40.6 79.9 %all-gather.3.cloned.1.call-done = bf16[2048,2048]{1,0:T(8,128)(2,1)} async-done(((bf16[128,2048]{1,0:T(8,128)(2,1)}), bf16[2048,2048]{1,0:T(8,128)(2,1)}) %all-gather.3.cloned.1.call-update) | async-done | bytes 8388624 | tf_op jit(solution)/shard_map/all_gather | solution.py:31
  120.5 4.9 %fusion.14 = (f32[128]{0:T(128)S(1)}, f32[128,2048]{1,0:T(8,128)S(1)}) fusion(bf16[128,2048]{0,1:T(8,128)(2,1)} %all_gather.9, bf16[2048,2048]{1,0:T(8,128)(2,1)} %all-gather.3.cloned.1.call-done), kind=kOutput, calls=%fused_computation.38 | convolution fusion | flops 1074003840 | bytes 9961984 | tf_op jit(solution)/shard_map/dot_general | solution.py:32
  125.4 56.2 %all-reduce.1 = (f32[128]{0:T(128)S(1)}, f32[128]{0:T(128)S(1)}) all-reduce(bf16[128]{0:T(256)(128)(2,1)S(1)} %reduce_max.24, f32[128]{0:T(128)S(1)} %get-tuple-element.33), channel_id=1, replica_groups=mesh['vocab'=32,'dp'=16] {'vocab'}, use_global_device_ids=true, to_apply=%region_5.6 | all-reduce | flops 256 | bytes 1792 | tf_op jit(solution)/shard_map/pmax | solution.py:42
  181.6 0.8 fusion.6
  182.4 56.8 %all-reduce = (f32[128]{0:T(128)S(1)}, f32[128]{0:T(128)S(1)}, f32[128]{0:T(128)S(1)}, f32[128]{0:T(128)S(1)}, f32[128]{0:T(128)S(1)}) all-reduce(f32[128]{0:T(128)S(1)} %get-tuple-element.18, f32[128]{0:T(128)S(1)} %get-tuple-element.16, f32[128]{0:T(128)S(1)} %get-tuple-element.19, ...), channel_id=1, replica_groups=mesh['vocab'=32,'dp'=16] {'vocab'}, use_global_device_ids=true, to_apply=%region_11.12 | all-reduce | flops 640 | bytes 5120 | tf_op jit(solution)/shard_map/psum | solution.py:45
  239.2 0.6 add_reduce_fusion
  239.9 0.1 select_reduce_fusion.1
  240.0 0.2 select_reduce_fusion.2
  240.2 0.6 fusion.13
  241.0 1.4 fusion.11
  242.4 8.9 %all-to-all-start = ((bf16[128,16,128]{0,2,1:T(8,128)(2,1)}), bf16[128,16,128]{0,2,1:T(8,128)(2,1)S(1)}, u32[]{:S(2)}, u32[]{:S(2)}) async-start(bf16[128,16,128]{0,2,1:T(8,128)(2,1)} %bitcast.2), calls=%async_computation.1 | async-start | bytes 1048576 | tf_op jit(solution)/shard_map/all_to_all | solution.py:76
  251.4 6.7 %convolution_convert_fusion = bf16[128,2048]{0,1:T(8,128)(2,1)} fusion(bf16[128,2048]{1,0:T(8,128)(2,1)} %fusion.11, bf16[2048,2048]{1,0:T(8,128)(2,1)} %all-gather.3.cloned.1.call-done), kind=kOutput, calls=%fused_computation.1 | convolution fusion | flops 1074003968 | bytes 9437184 | tf_op jit(solution)/shard_map/dot_general | solution.py:70
  259.3 21.5 %all-to-all-done = bf16[128,16,128]{0,2,1:T(8,128)(2,1)S(1)} async-done(((bf16[128,16,128]{0,2,1:T(8,128)(2,1)}), bf16[128,16,128]{0,2,1:T(8,128)(2,1)S(1)}, u32[]{:S(2)}, u32[]{:S(2)}) %all-to-all-start) | async-done | bytes 524320 | tf_op jit(solution)/shard_map/all_to_all | solution.py:76
  280.9 0.3 copy.13
  281.1 32.6 %psum.47 = f32[]{:T(128)} all-reduce(f32[]{:T(128)S(6)} %add.55), channel_id=1, replica_groups=mesh['vocab'=32,'dp'=16] {'dp'}, use_global_device_ids=true, to_apply=%region_22.23 | all-reduce | flops 1 | bytes 8 | tf_op jit(solution)/shard_map/psum | solution.py:61
  314.4 48.8 %all-gather.5.cloned.1.call-done = bf16[2048,2048]{1,0:T(8,128)(2,1)} async-done(((bf16[128,2048]{1,0:T(8,128)(2,1)}), bf16[2048,2048]{1,0:T(8,128)(2,1)}) %all-gather.5.cloned.1.call-update) | async-done | bytes 8388624 | tf_op jit(solution)/shard_map/all_gather | solution.py:79
  363.2 5.8 %convolution_bitcast_fusion = f32[128,2048]{0,1:T(8,128)S(1)} fusion(bf16[2048,2048]{1,0:T(8,128)(2,1)} %all-gather.5.cloned.1.call-done, bf16[2048,128]{1,0:T(8,128)(2,1)S(1)} %bitcast.14), kind=kOutput, calls=%fused_computation | convolution fusion | flops 1073741824 | bytes 9961472 | tf_op jit(solution)/shard_map/dot_general | solution.py:77
  369.0 1.3 copy.14
  370.3 109.0 %reduce-scatter.2.cloned.1.call-done = bf16[128,64]{0,1:T(8,128)(2,1)} async-done(((bf16[128,2048]{0,1:T(8,128)(2,1)}), bf16[128,64]{0,1:T(8,128)(2,1)}) %reduce-scatter.2.cloned.1.call-update) | async-done | bytes 16400 | tf_op jit(solution)/shard_map/reduce_scatter | solution.py:73
  (14 shorter events, 0.3 us)
Async XLA Ops:
  7.2 113.3 %all-gather.3.cloned.1.call-start = ((), (), s32[]{:S(2)}) async-start(), calls=%async_computation.2 | async-start | bytes 8912896 | tf_op jit(solution)/shard_map/all_gather | solution.py:31
  7.9 173.7 %copy-start = (bf16[128,2048]{1,0:T(8,128)(2,1)S(1)}, bf16[128,2048]{1,0:T(8,128)(2,1)}, u32[]{:S(2)}) copy-start(bf16[128,2048]{1,0:T(8,128)(2,1)} %param.8) | copy-start | bytes 1572868
  7.9 173.7 %copy-start.1 = (s32[128]{0:T(128)S(1)}, s32[128]{0:T(128)}, u32[]{:S(2)}) copy-start(s32[128]{0:T(128)} %param.9) | copy-start | bytes 1540
  7.9 355.3 %all-gather.5.cloned.1.call-start = ((), (), s32[]{:S(2)}) async-start(), calls=%async_computation.4 | async-start | bytes 8912896 | tf_op jit(solution)/shard_map/all_gather | solution.py:79
  40.6 199.2 %copy-start.2 = (s32[1,128]{1,0:T(1,128)S(1)}, s32[1,128]{1,0:T(1,128)}, u32[]{:S(2)}) copy-start(s32[1,128]{1,0:T(1,128)} %param.10) | copy-start | bytes 1540
  242.4 38.4 %all-to-all-start = ((bf16[128,16,128]{0,2,1:T(8,128)(2,1)}), bf16[128,16,128]{0,2,1:T(8,128)(2,1)S(1)}, u32[]{:S(2)}, u32[]{:S(2)}) async-start(bf16[128,16,128]{0,2,1:T(8,128)(2,1)} %bitcast.2), calls=%async_computation.1 | async-start | bytes 1048576 | tf_op jit(solution)/shard_map/all_to_all | solution.py:76
  251.3 227.9 %reduce-scatter.2.cloned.1.call-start = ((), (), s32[]{:S(2)}) async-start(), calls=%async_computation.3 | async-start | bytes 540672 | tf_op jit(solution)/shard_map/reduce_scatter | solution.py:73
Sparse Core Ops, SparseCore 0:
  10.1 110.3 all-gather.2
  242.6 120.6 all-gather.4
  368.1 111.0 reduce-scatter.1
where the time goes:
time: 487 us
  waiting for transfers between devices  260 us (53%)
  blocking collectives  175 us (36%)
  matrix products  17.4 us (4%)
  between operations  16.8 us (3%)
  starting transfers between devices  9 us (2%)
  other arithmetic  5.2 us (1%)
    reduce_scatter x1, waiting for transfers between devices, on_device(): lax.psum_scatter(hidden_term.astype(jnp.bfloat16), 'vocab', scatter_dimen...  109 us
    all_gather x1, waiting for transfers between devices, on_device(): weight_full = lax.all_gather(head_weight, 'dp', axis=0, tiled=True)  79.9 us
    psum x1, blocking collectives, on_device(): lax.psum((jnp.sum(exp_student, axis=1), jnp.sum(exp_teacher, axis=1), jnp...  56.8 us
    pmax x1, blocking collectives, on_device(): max_student, max_teacher = lax.pmax((local_max, local_tmax), 'vocab')  56.2 us
    all_gather x1, waiting for transfers between devices, on_device(): lax.all_gather(logit_grad, 'dp', axis=0, tiled=True)  48.8 us
    psum x1, blocking collectives, on_device(): summed_objective = lax.psum(group_objective, 'dp')  32.6 us
    all_gather x1, blocking collectives, on_device(): rows_full = lax.all_gather(hidden, 'vocab', axis=1, tiled=True)  29.9 us
    all_to_all x1, waiting for transfers between devices, on_device(): lax.all_to_all(rows_full, 'dp', split_axis=1, concat_axis=0, tiled=True)  21.5 us
  transfers between devices with their start and end apart: 4, of which 4 were waited for; matrix products, arithmetic and copies ran while one was open for 3% of the time, Pallas kernels for 0%

commit v1 on v0

v1 whole, which is shorter than its diff:
```python
import jax
import jax.numpy as jnp
from jax import lax
from jax.sharding import PartitionSpec as P

dpo_beta = 0.1
dpo_gamma = 4.0


def pair_weights(log_ratio, segments, ordering):
    seq_count = ordering.shape[0]
    labels = lax.broadcasted_iota(jnp.int32, (1, seq_count), 1)
    seq_hot = (segments[:, None] == labels).astype(jnp.float32)
    seq_ratio = jnp.sum(seq_hot * log_ratio[:, None], axis=0)
    chosen = ordering[0::2]
    rejected = ordering[1::2]
    chosen_hot = (chosen[:, None] == labels).astype(jnp.float32)
    rejected_hot = (rejected[:, None] == labels).astype(jnp.float32)
    margin = dpo_beta * (
        jnp.sum(chosen_hot * seq_ratio[None, :], axis=1)
        - jnp.sum(rejected_hot * seq_ratio[None, :], axis=1)
    )
    strength = dpo_gamma * dpo_beta * jax.nn.sigmoid(-margin)
    coeffs = jnp.sum((rejected_hot - chosen_hot) * strength[:, None], axis=0)
    row_weight = jnp.sum(seq_hot * coeffs[None, :], axis=1)
    return (row_weight, jnp.sum(jax.nn.softplus(-margin)))


def to_all(block, axis):
    count = lax.axis_size(axis)
    copies = jnp.broadcast_to(block[None], (count,) + block.shape)
    return lax.all_to_all(copies, axis, 0, 0, tiled=True)


def on_device(hidden, head_weight, teacher_logits, target_ids, segment_ids, pair_order):
    f32, bf16 = jnp.float32, jnp.bfloat16
    rows_full = lax.all_gather(hidden, "vocab", axis=1, tiled=True)
    width = head_weight.shape[1]
    half = width // 2
    weight_lo = lax.all_gather(head_weight[:, :half], "dp", axis=0, tiled=True)
    weight_hi = lax.all_gather(head_weight[:, half:], "dp", axis=0, tiled=True)
    student = jnp.concatenate(
        [
            jnp.dot(rows_full, weight_lo, preferred_element_type=f32),
            jnp.dot(rows_full, weight_hi, preferred_element_type=f32),
        ],
        axis=1,
    )
    teacher = teacher_logits.astype(f32)
    n_vocab = lax.axis_size("vocab")
    n_dp = lax.axis_size("dp")
    rows = student.shape[0]
    offset = lax.axis_index("vocab") * width
    column = lax.broadcasted_iota(jnp.int32, student.shape, 1) + offset
    is_target = column == target_ids[:, None]
    own_max = jnp.max(student, axis=1)
    own_tmax = jnp.max(teacher, axis=1)
    own_exp = jnp.exp(student - own_max[:, None])
    own_texp = jnp.exp(teacher - own_tmax[:, None])
    stats = jnp.stack(
        [
            own_max,
            own_tmax,
            jnp.sum(own_exp, axis=1),
            jnp.sum(own_texp, axis=1),
            jnp.sum(own_texp * (teacher - student), axis=1),
            jnp.sum(jnp.where(is_target, student, 0.0), axis=1),
            jnp.sum(jnp.where(is_target, teacher, 0.0), axis=1),
            jnp.zeros((rows,), f32),
        ]
    )
    every = to_all(stats, "vocab").reshape(n_vocab, 8, rows)
    max_student = jnp.max(every[:, 0], axis=0)
    max_teacher = jnp.max(every[:, 1], axis=0)
    scale_s = jnp.exp(every[:, 0] - max_student[None])
    scale_t = jnp.exp(every[:, 1] - max_teacher[None])
    sum_student = jnp.sum(every[:, 2] * scale_s, axis=0)
    sum_teacher = jnp.sum(every[:, 3] * scale_t, axis=0)
    cross = jnp.sum(every[:, 4] * scale_t, axis=0)
    target_student = jnp.sum(every[:, 5], axis=0)
    target_teacher = jnp.sum(every[:, 6], axis=0)
    lse_student = max_student + jnp.log(sum_student)
    lse_teacher = max_teacher + jnp.log(sum_teacher)
    kl_rows = cross / sum_teacher - lse_teacher + lse_student
    log_ratio = target_student - lse_student - (target_teacher - lse_teacher)
    row_weight, dpo_sum = pair_weights(log_ratio, segment_ids[0], pair_order[0])
    group_objective = jnp.sum(kl_rows) + dpo_gamma * dpo_sum
    exp_student = jnp.exp(student - max_student[:, None])
    exp_teacher = jnp.exp(teacher - max_teacher[:, None])
    prob_student = exp_student / sum_student[:, None]
    prob_teacher = exp_teacher / sum_teacher[:, None]
    logit_grad = (
        prob_student
        - prob_teacher
        + row_weight[:, None] * (is_target.astype(f32) - prob_student)
    ).astype(bf16)
    grad_lo = logit_grad[:, :half]
    grad_hi = logit_grad[:, half:]
    all_lo = lax.all_gather(grad_lo, "dp", axis=0, tiled=True)
    all_hi = lax.all_gather(grad_hi, "dp", axis=0, tiled=True)
    nt = (((1,), (1,)), ((), ()))
    hidden_term = (
        lax.dot_general(grad_lo, weight_lo, nt, preferred_element_type=f32)
        + lax.dot_general(grad_hi, weight_hi, nt, preferred_element_type=f32)
    ).astype(bf16)
    feats = hidden_term.shape[1] // n_vocab
    terms = hidden_term.reshape(rows, n_vocab, feats).swapaxes(0, 1)
    terms = lax.all_to_all(terms, "vocab", 0, 0, tiled=True)
    hidden_grad = jnp.sum(terms.astype(f32), axis=0).astype(bf16)
    objectives = to_all(jnp.full((8, 128), group_objective, f32), "dp").reshape(n_dp, 8, 128)
    loss_value = jnp.sum(objectives[:, 0, 0]) / (rows * n_dp)
    grad_cols = lax.all_to_all(rows_full, "dp", split_axis=1, concat_axis=0, tiled=True)
    tn = (((0,), (0,)), ((), ()))
    head_grad = jnp.concatenate(
        [
            lax.dot_general(grad_cols, all_lo, tn, preferred_element_type=f32),
            lax.dot_general(grad_cols, all_hi, tn, preferred_element_type=f32),
        ],
        axis=1,
    )
    return (hidden_grad, head_grad, loss_value)


def solution(mesh):
    return jax.shard_map(
        on_device,
        mesh=mesh,
        in_specs=(
            P("dp", "vocab"),
            P("dp", "vocab"),
            P("dp", "vocab"),
            P("dp"),
            P("dp", None),
            P("dp", None),
        ),
        out_specs=(P("dp", "vocab"), P("dp", "vocab"), P()),
        check_vma=False,
    )
```

time: 487 us -> 375 us (0.77)
  blocking collectives: 175 us -> 29.9 us
  starting transfers between devices: 9 us -> 26.5 us
  waiting for transfers between devices: 260 us -> 268 us
    reduce_scatter x1 -> x0, waiting for transfers between devices: 109 us -> none  [on_device(): lax.psum_scatter(hidden_term.astype(jnp.bfloat16), 'vocab', scatter_dimen...]
    psum x2 -> x0, blocking collectives: 89.4 us -> none  [the longest x1 56.8 us: on_device(): lax.psum((jnp.sum(exp_student, axis=1), jnp.sum(exp_teacher, axis=1), jnp...]
    all_gather x2 -> x4, waiting for transfers between devices: 129 us -> 214 us  [the longest x1 74.8 us: on_device(): weight_hi = lax.all_gather(head_weight[:, half:], 'dp', axis=0, tiled=True)]
    pmax x1 -> x0, blocking collectives: 56.2 us -> none  [on_device(): max_student, max_teacher = lax.pmax((local_max, local_tmax), 'vocab')]
    all_to_all x0 -> x3, waiting for transfers between devices: none -> 23.4 us  [the longest x2 15.2 us: to_all(): return lax.all_to_all(copies, axis, 0, 0, tiled=True)]
    all_to_all x0 -> x3, starting transfers between devices: none -> 18.9 us  [the longest x2 13.8 us: to_all(): return lax.all_to_all(copies, axis, 0, 0, tiled=True)]
    all_to_all x1, waiting for transfers between devices: 21.5 us -> 29.5 us  [on_device(): lax.all_to_all(rows_full, 'dp', split_axis=1, concat_axis=0, tiled=True)]
    dot_general x3 -> x6, matrix products: 17.4 us -> 20.8 us  [the longest x1 3.78 us: on_device(): lax.dot_general(grad_lo, weight_lo, nt, preferred_element_type=f32)]
  transfers between devices with their start and end apart: 4 -> 8, of which waited for: 4 -> 8; matrix products, arithmetic and copies ran while one was open for 3% -> 5% of each run, Pallas kernels for 0% -> 0%
where the time goes in v1:
time: 375 us
  waiting for transfers between devices  268 us (71%)
  blocking collectives  29.9 us (8%)
  starting transfers between devices  26.5 us (7%)
  matrix products  20.8 us (6%)
  between operations  17 us (5%)
  local copies, waits for them, and re-layouts  6.89 us (2%)
  other arithmetic  5.88 us (2%)
    all_gather x1, waiting for transfers between devices, on_device(): weight_hi = lax.all_gather(head_weight[:, half:], 'dp', axis=0, tiled=True)  74.8 us
    all_gather x1, waiting for transfers between devices, on_device(): all_hi = lax.all_gather(grad_hi, 'dp', axis=0, tiled=True)  70.6 us
    all_gather x1, waiting for transfers between devices, on_device(): weight_lo = lax.all_gather(head_weight[:, :half], 'dp', axis=0, tiled=True)  52.3 us
    all_gather x1, blocking collectives, on_device(): rows_full = lax.all_gather(hidden, 'vocab', axis=1, tiled=True)  29.9 us
    all_to_all x1, waiting for transfers between devices, on_device(): lax.all_to_all(rows_full, 'dp', split_axis=1, concat_axis=0, tiled=True)  29.5 us
    all_gather x1, waiting for transfers between devices, on_device(): all_lo = lax.all_gather(grad_lo, 'dp', axis=0, tiled=True)  15.8 us
    all_to_all x2, waiting for transfers between devices, to_all(): return lax.all_to_all(copies, axis, 0, 0, tiled=True)  15.2 us
    all_to_all x2, starting transfers between devices, to_all(): return lax.all_to_all(copies, axis, 0, 0, tiled=True)  13.8 us
  transfers between devices with their start and end apart: 8, of which 8 were waited for; matrix products, arithmetic and copies ran while one was open for 5% of the time, Pallas kernels for 0%

profile of v1, /device:TPU:2, one launch (start us, length us, event | category | flops | bytes accessed | tf_op | source)
XLA Modules:
  0.0 374.6 jit_solution(1377167011678018934)
XLA Ops:
  7.2 1.8 fusion.19
  9.8 1.2 reduce_max.71
  11.0 29.9 %all_gather.15 = bf16[128,2048]{0,1:T(8,128)(2,1)} all-gather(bf16[128,64]{0,1:T(8,128)(2,1)} %param.6), channel_id=1, replica_groups=mesh['vocab'=32,'dp'=16] {'vocab'}, dimensions={1}, use_global_device_ids=true | all-gather | bytes 540672 | tf_op jit(solution)/shard_map/all_gather | solution.py:37
  40.9 52.3 %all-gather.5.cloned.1.call-done = bf16[2048,1024]{1,0:T(8,128)(2,1)} async-done(((bf16[128,1024]{1,0:T(8,128)(2,1)}), bf16[2048,1024]{1,0:T(8,128)(2,1)}) %all-gather.5.cloned.1.call-update) | async-done | bytes 4194320 | tf_op jit(solution)/shard_map/all_gather | solution.py:40
  93.3 3.2 fusion.22
  96.5 74.8 %all-gather.7.cloned.1.call-done = bf16[2048,1024]{1,0:T(8,128)(2,1)} async-done(((bf16[128,1024]{1,0:T(8,128)(2,1)}), bf16[2048,1024]{1,0:T(8,128)(2,1)}) %all-gather.7.cloned.1.call-update) | async-done | bytes 4194320 | tf_op jit(solution)/shard_map/all_gather | solution.py:41
  171.3 3.2 fusion.23
  176.0 7.4 %all-to-all-start = ((f32[32,8,128]{2,1,0:T(8,128)}), f32[32,8,128]{2,1,0:T(8,128)S(1)}, u32[]{:S(2)}, u32[]{:S(2)}) async-start(f32[32,8,128]{2,1,0:T(8,128)} %broadcast_in_dim.8), calls=%async_computation | async-start | bytes 262144 | tf_op jit(solution)/shard_map/all_to_all | solution.py:32
  183.7 6.4 %all-to-all-done = f32[32,8,128]{2,1,0:T(8,128)S(1)} async-done(((f32[32,8,128]{2,1,0:T(8,128)}), f32[32,8,128]{2,1,0:T(8,128)S(1)}, u32[]{:S(2)}, u32[]{:S(2)}) %all-to-all-start) | async-done | bytes 131104 | tf_op jit(solution)/shard_map/all_to_all | solution.py:32
  192.7 0.9 fusion.18
  194.1 7.4 %all-to-all-start.2 = ((bf16[128,16,128]{0,2,1:T(8,128)(2,1)}), bf16[128,16,128]{0,2,1:T(8,128)(2,1)S(1)}, u32[]{:S(2)}, u32[]{:S(2)}) async-start(bf16[128,16,128]{0,2,1:T(8,128)(2,1)} %bitcast.17), calls=%async_computation.2 | async-start | bytes 1048576 | tf_op jit(solution)/shard_map/all_to_all | solution.py:112
  202.9 3.8 %fusion.16 = f32[128,2048]{1,0:T(8,128)S(1)} fusion(bf16[2048,1024]{1,0:T(8,128)(2,1)} %all-gather.5.cloned.1.call-done, bf16[128,2048]{1,0:T(8,128)(2,1)S(1)} %fusion.5), kind=kOutput, calls=%fused_computation.50 | convolution fusion | flops 536870912 | bytes 5505024 | tf_op jit(solution)/shard_map/dot_general | solution.py:103
  206.7 29.5 %all-to-all-done.2 = bf16[128,16,128]{0,2,1:T(8,128)(2,1)S(1)} async-done(((bf16[128,16,128]{0,2,1:T(8,128)(2,1)}), bf16[128,16,128]{0,2,1:T(8,128)(2,1)S(1)}, u32[]{:S(2)}, u32[]{:S(2)}) %all-to-all-start.2) | async-done | bytes 524320 | tf_op jit(solution)/shard_map/all_to_all | solution.py:112
  236.8 6.4 %all-to-all-start.3 = ((f32[16,8,128]{2,1,0:T(8,128)}), f32[16,8,128]{2,1,0:T(8,128)S(1)}, u32[]{:S(2)}, u32[]{:S(2)}) async-start(f32[16,8,128]{2,1,0:T(8,128)} %broadcast_in_dim_broadcast_in_dim_broadcast_in_dim.3), calls=%async_computation.3 | async-start | bytes 131072 | tf_op jit(solution)/shard_map/all_to_all | solution.py:32
  243.2 3.7 fusion
  246.9 1.0 copy.32
  247.9 8.8 %all-to-all-done.3 = f32[16,8,128]{2,1,0:T(8,128)S(1)} async-done(((f32[16,8,128]{2,1,0:T(8,128)}), f32[16,8,128]{2,1,0:T(8,128)S(1)}, u32[]{:S(2)}, u32[]{:S(2)}) %all-to-all-start.3) | async-done | bytes 65568 | tf_op jit(solution)/shard_map/all_to_all | solution.py:32
  256.8 5.0 %all-to-all-start.1 = ((bf16[32,128,64]{1,2,0:T(8,128)(2,1)}), bf16[32,128,64]{1,2,0:T(8,128)(2,1)S(1)}, u32[]{:S(2)}, u32[]{:S(2)}) async-start(bf16[32,128,64]{1,2,0:T(8,128)(2,1)} %bitcast.16), calls=%async_computation.1 | async-start | bytes 1048576 | tf_op jit(solution)/shard_map/all_to_all | solution.py:108
  263.4 8.2 %all-to-all-done.1 = bf16[32,128,64]{1,2,0:T(8,128)(2,1)S(1)} async-done(((bf16[32,128,64]{1,2,0:T(8,128)(2,1)}), bf16[32,128,64]{1,2,0:T(8,128)(2,1)S(1)}, u32[]{:S(2)}, u32[]{:S(2)}) %all-to-all-start.1) | async-done | bytes 524320 | tf_op jit(solution)/shard_map/all_to_all | solution.py:108
  272.2 15.8 %all-gather.9.cloned.1.call-done = bf16[2048,1024]{1,0:T(8,128)(2,1)} async-done(((bf16[128,1024]{1,0:T(8,128)(2,1)}), bf16[2048,1024]{1,0:T(8,128)(2,1)}) %all-gather.9.cloned.1.call-update) | async-done | bytes 4194320 | tf_op jit(solution)/shard_map/all_gather | solution.py:99
  288.0 3.5 convolution_bitcast_fusion.1
  291.5 70.6 %all-gather.11.cloned.1.call-done = bf16[2048,1024]{1,0:T(8,128)(2,1)} async-done(((bf16[128,1024]{1,0:T(8,128)(2,1)}), bf16[2048,1024]{1,0:T(8,128)(2,1)}) %all-gather.11.cloned.1.call-update) | async-done | bytes 4194320 | tf_op jit(solution)/shard_map/all_gather | solution.py:100
  362.1 3.5 convolution_bitcast_fusion
  365.6 1.3 copy.35
  (43 shorter events, 8.0 us)
Async XLA Ops:
  7.2 86.1 %all-gather.5.cloned.1.call-start = ((), (), s32[]{:S(2)}) async-start(), calls=%async_computation.4 | async-start | bytes 4456448 | tf_op jit(solution)/shard_map/all_gather | solution.py:40
  9.1 162.2 %all-gather.7.cloned.1.call-start = ((), (), s32[]{:S(2)}) async-start(), calls=%async_computation.5 | async-start | bytes 4456448 | tf_op jit(solution)/shard_map/all_gather | solution.py:41
  40.9 133.6 %copy-start = (bf16[128,2048]{1,0:T(8,128)(2,1)S(1)}, bf16[128,2048]{1,0:T(8,128)(2,1)}, u32[]{:S(2)}) copy-start(bf16[128,2048]{1,0:T(8,128)(2,1)} %param.8) | copy-start | bytes 1572868
  40.9 133.6 %copy-start.1 = (s32[128]{0:T(128)S(1)}, s32[128]{0:T(128)}, u32[]{:S(2)}) copy-start(s32[128]{0:T(128)} %param.9) | copy-start | bytes 1540
  96.4 87.1 %copy-start.2 = (s32[1,16]{1,0:T(1,128)S(1)}, s32[1,16]{1,0:T(1,128)}, u32[]{:S(2)}) copy-start(s32[1,16]{1,0:T(1,128)} %param.11) | copy-start | bytes 196
  96.5 94.5 %copy-start.3 = (s32[1,128]{1,0:T(1,128)S(1)}, s32[1,128]{1,0:T(1,128)}, u32[]{:S(2)}) copy-start(s32[1,128]{1,0:T(1,128)} %param.10) | copy-start | bytes 1540
  176.0 14.1 %all-to-all-start = ((f32[32,8,128]{2,1,0:T(8,128)}), f32[32,8,128]{2,1,0:T(8,128)S(1)}, u32[]{:S(2)}, u32[]{:S(2)}) async-start(f32[32,8,128]{2,1,0:T(8,128)} %broadcast_in_dim.8), calls=%async_computation | async-start | bytes 262144 | tf_op jit(solution)/shard_map/all_to_all | solution.py:32
  183.5 104.5 %all-gather.9.cloned.1.call-start = ((), (), s32[]{:S(2)}) async-start(), calls=%async_computation.6 | async-start | bytes 4456448 | tf_op jit(solution)/shard_map/all_gather | solution.py:99
  193.6 168.5 %all-gather.11.cloned.1.call-start = ((), (), s32[]{:S(2)}) async-start(), calls=%async_computation.7 | async-start | bytes 4456448 | tf_op jit(solution)/shard_map/all_gather | solution.py:100
  194.1 42.0 %all-to-all-start.2 = ((bf16[128,16,128]{0,2,1:T(8,128)(2,1)}), bf16[128,16,128]{0,2,1:T(8,128)(2,1)S(1)}, u32[]{:S(2)}, u32[]{:S(2)}) async-start(bf16[128,16,128]{0,2,1:T(8,128)(2,1)} %bitcast.17), calls=%async_computation.2 | async-start | bytes 1048576 | tf_op jit(solution)/shard_map/all_to_all | solution.py:112
  236.8 20.0 %all-to-all-start.3 = ((f32[16,8,128]{2,1,0:T(8,128)}), f32[16,8,128]{2,1,0:T(8,128)S(1)}, u32[]{:S(2)}, u32[]{:S(2)}) async-start(f32[16,8,128]{2,1,0:T(8,128)} %broadcast_in_dim_broadcast_in_dim_broadcast_in_dim.3), calls=%async_computation.3 | async-start | bytes 131072 | tf_op jit(solution)/shard_map/all_to_all | solution.py:32
  256.8 14.8 %all-to-all-start.1 = ((bf16[32,128,64]{1,2,0:T(8,128)(2,1)}), bf16[32,128,64]{1,2,0:T(8,128)(2,1)S(1)}, u32[]{:S(2)}, u32[]{:S(2)}) async-start(bf16[32,128,64]{1,2,0:T(8,128)(2,1)} %bitcast.16), calls=%async_computation.1 | async-start | bytes 1048576 | tf_op jit(solution)/shard_map/all_to_all | solution.py:108
Sparse Core Ops, SparseCore 0:
  10.1 83.1 all-gather.4
  95.9 75.3 all-gather.6
  193.7 94.2 all-gather.8
  289.9 72.1 all-gather.10

commit v2 on v1

--- a/solution.py
+++ b/solution.py
@@ -1,6 +1,8 @@
 import jax
 import jax.numpy as jnp
 from jax import lax
+from jax.experimental import pallas as pl
+from jax.experimental.pallas import tpu as pltpu
 from jax.sharding import PartitionSpec as P
 
 dpo_beta = 0.1
@@ -26,30 +28,117 @@
     return (row_weight, jnp.sum(jax.nn.softplus(-margin)))
 
 
-def to_all(block, axis):
-    count = lax.axis_size(axis)
+def to_all(block, axis, groups=None):
+    count = lax.axis_size(axis) if groups is None else len(groups[0])
     copies = jnp.broadcast_to(block[None], (count,) + block.shape)
-    return lax.all_to_all(copies, axis, 0, 0, tiled=True)
+    return lax.all_to_all(copies, axis, 0, 0, axis_index_groups=groups, tiled=True)
+
+
+def head_kernel(core_ref, objective_ref, own_ref, other_ref, grad_ref, out_ref):
+    f32, bf16 = jnp.float32, jnp.bfloat16
+    grad = grad_ref[...]
+    own = jnp.dot(own_ref[...], grad, preferred_element_type=f32).astype(bf16)
+    other = jnp.dot(other_ref[...], grad, preferred_element_type=f32).astype(bf16)
+    blocks, tall, _ = out_ref.shape
+    feats = own.shape[0] // blocks
+    extra = tall - 2 * feats
+    value = jnp.full((extra, own.shape[1]), objective_ref[0], f32)
+    high = value.astype(bf16).astype(f32)
+    middle = (value - high).astype(bf16).astype(f32)
+    low = value - high - middle
+    line = lax.broadcasted_iota(jnp.int32, value.shape, 0)
+    pieces = jnp.where(line == 0, high, jnp.where(line == 1, middle, jnp.where(line == 2, low, 0.0)))
+    pieces = pieces.astype(bf16)
+
+    def store(first, second):
+        for j in range(blocks):
+            out_ref[j, :feats] = first[j * feats : (j + 1) * feats]
+            out_ref[j, feats : 2 * feats] = second[j * feats : (j + 1) * feats]
+            out_ref[j, 2 * feats :] = pieces
+
+    @pl.when(core_ref[0] == 0)
+    def _():
+        store(own, other)
+
+    @pl.when(core_ref[0] != 0)
+    def _():
+        store(other, own)
+
+
+def head_partial(core, objective, own, other, grad, blocks, extra):
+    tall, rows = own.shape
+    cols = grad.shape[1]
+    steps = 4
+    per = blocks // steps
+    feats = tall // blocks
+    return pl.pallas_call(
+        head_kernel,
+        out_shape=jax.ShapeDtypeStruct((blocks, 2 * feats + extra, cols), jnp.bfloat16),
+        grid=(steps,),
+        in_specs=[
+            pl.BlockSpec(memory_space=pltpu.SMEM),
+            pl.BlockSpec(memory_space=pltpu.SMEM),
+            pl.BlockSpec((tall // steps, rows), lambda i: (i, 0)),
+            pl.BlockSpec((tall // steps, rows), lambda i: (i, 0)),
+            pl.BlockSpec((rows, cols), lambda i: (0, 0)),
+        ],
+        out_specs=pl.BlockSpec((per, 2 * feats + extra, cols), lambda i: (i, 0, 0)),
+        compiler_params=pltpu.CompilerParams(vmem_limit_bytes=32 * 1024 * 1024),
+        cost_estimate=pl.CostEstimate(
+            flops=4 * tall * rows * cols,
+            bytes_accessed=4 * tall * rows + 2 * rows * cols + 4 * tall * cols,
+            transcendentals=0,
+        ),
+    )(core, objective, own, other, grad)
+
+
+def unpack_kernel(parts_ref, grad_ref, total_ref):
+    f32 = jnp.float32
+    count, _, cols = parts_ref.shape
+    tall = grad_ref.shape[0]
+    for j in range(count):
+        grad_ref[:, j * cols : (j + 1) * cols] = parts_ref[j, :tall].astype(f32)
+    lines = jnp.sum(parts_ref[:, tall:].astype(f32), axis=0)
+    total_ref[0] = jnp.sum(lines[:3, :1])
+
+
+def unpack(parts, tall):
+    count, _, cols = parts.shape
+    return pl.pallas_call(
+        unpack_kernel,
+        out_shape=(
+            jax.ShapeDtypeStruct((tall, count * cols), jnp.float32),
+            jax.ShapeDtypeStruct((1,), jnp.float32),
+        ),
+        out_specs=(pl.BlockSpec(memory_space=pltpu.VMEM), pl.BlockSpec(memory_space=pltpu.SMEM)),
+        compiler_params=pltpu.CompilerParams(vmem_limit_bytes=16 * 1024 * 1024),
+    )(parts)
 
 
 def on_device(hidden, head_weight, teacher_logits, target_ids, segment_ids, pair_order):
     f32, bf16 = jnp.float32, jnp.bfloat16
-    rows_full = lax.all_gather(hidden, "vocab", axis=1, tiled=True)
-    width = head_weight.shape[1]
-    half = width // 2
-    weight_lo = lax.all_gather(head_weight[:, :half], "dp", axis=0, tiled=True)
-    weight_hi = lax.all_gather(head_weight[:, half:], "dp", axis=0, tiled=True)
-    student = jnp.concatenate(
-        [
-            jnp.dot(rows_full, weight_lo, preferred_element_type=f32),
-            jnp.dot(rows_full, weight_hi, preferred_element_type=f32),
-        ],
-        axis=1,
-    )
-    teacher = teacher_logits.astype(f32)
     n_vocab = lax.axis_size("vocab")
     n_dp = lax.axis_size("dp")
-    rows = student.shape[0]
+    rows, feats = hidden.shape
+    width = head_weight.shape[1]
+    pairs = n_vocab // 2
+    core = lax.axis_index("vocab") % 2
+    same_core = [[2 * j + c for j in range(pairs)] for c in range(2)]
+    swap = [(i, i ^ 1) for i in range(n_vocab)]
+    weight_full = lax.all_gather(head_weight, "dp", axis=0, tiled=True)
+    by_group = to_all(hidden.T, "dp").reshape(n_dp, feats, rows)
+    by_pair = to_all(by_group, "vocab", same_core).reshape(pairs, n_dp, feats, rows)
+    mine = lax.dynamic_index_in_dim(by_pair, lax.axis_index("dp"), 1, keepdims=False)
+    theirs = lax.ppermute(mine, "vocab", swap)
+    rows_t = jnp.stack(
+        [jnp.where(core == 0, mine, theirs), jnp.where(core == 0, theirs, mine)], axis=1
+    ).reshape(n_vocab * feats, rows)
+    own_t = by_pair.swapaxes(1, 2).reshape(pairs * feats, n_dp * rows)
+    other_t = lax.ppermute(own_t, "vocab", swap)
+    tn = (((0,), (0,)), ((), ()))
+    nt = (((1,), (1,)), ((), ()))
+    student = lax.dot_general(rows_t, weight_full, tn, preferred_element_type=f32)
+    teacher = teacher_logits.astype(f32)
     offset = lax.axis_index("vocab") * width
     column = lax.broadcasted_iota(jnp.int32, student.shape, 1) + offset
     is_target = column == target_ids[:, None]
@@ -94,30 +183,27 @@
         - prob_teacher
         + row_weight[:, None] * (is_target.astype(f32) - prob_student)
     ).astype(bf16)
-    grad_lo = logit_grad[:, :half]
-    grad_hi = logit_grad[:, half:]
-    all_lo = lax.all_gather(grad_lo, "dp", axis=0, tiled=True)
-    all_hi = lax.all_gather(grad_hi, "dp", axis=0, tiled=True)
-    nt = (((1,), (1,)), ((), ()))
-    hidden_term = (
-        lax.dot_general(grad_lo, weight_lo, nt, preferred_element_type=f32)
-        + lax.dot_general(grad_hi, weight_hi, nt, preferred_element_type=f32)
-    ).astype(bf16)
-    feats = hidden_term.shape[1] // n_vocab
-    terms = hidden_term.reshape(rows, n_vocab, feats).swapaxes(0, 1)
+    chunk = width // n_dp
+    chunks = logit_grad.reshape(rows, n_dp, chunk).swapaxes(0, 1)
+    chunks = lax.all_to_all(chunks, "dp", 0, 0, tiled=True)
+    hidden_term = lax.dot_general(logit_grad, weight_full, nt, preferred_element_type=f32)
+    terms = hidden_term.astype(bf16).reshape(rows, n_vocab, feats).swapaxes(0, 1)
+    chunks, terms = lax.optimization_barrier((chunks, terms))
+    partial = head_partial(
+        core.astype(jnp.int32).reshape(1),
+        group_objective.reshape(1),
+        own_t,
+        other_t,
+        chunks.reshape(n_dp * rows, chunk),
+        pairs,
+        16,
+    )
     terms = lax.all_to_all(terms, "vocab", 0, 0, tiled=True)
     hidden_grad = jnp.sum(terms.astype(f32), axis=0).astype(bf16)
-    objectives = to_all(jnp.full((8, 128), group_objective, f32), "dp").reshape(n_dp, 8, 128)
-    loss_value = jnp.sum(objectives[:, 0, 0]) / (rows * n_dp)
-    grad_cols = lax.all_to_all(rows_full, "dp", split_axis=1, concat_axis=0, tiled=True)
-    tn = (((0,), (0,)), ((), ()))
-    head_grad = jnp.concatenate(
-        [
-            lax.dot_general(grad_cols, all_lo, tn, preferred_element_type=f32),
-            lax.dot_general(grad_cols, all_hi, tn, preferred_element_type=f32),
-        ],
-        axis=1,
-    )
+    partial, hidden_grad = lax.optimization_barrier((partial, hidden_grad))
+    parts = lax.all_to_all(partial, "dp", 0, 0, tiled=True)
+    head_grad, total = unpack(parts, 2 * feats)
+    loss_value = total[0] / (rows * n_dp)
     return (hidden_grad, head_grad, loss_value)
 
 

time: 375 us -> 263 us (0.70)
  the two profiles are of different devices: /device:TPU:2 before, /device:TPU:1 now
where the time goes in v2:
time: 263 us
  waiting for transfers between devices  84.7 us (32%)
  blocking collectives  68.9 us (26%)
  starting transfers between devices  51.4 us (20%)
  local copies, waits for them, and re-layouts  17.5 us (7%)
  between operations  17.2 us (7%)
  matrix products  11 us (4%)
  Pallas kernels  6.5 us (2%)
  other arithmetic  5.19 us (2%)
    all_to_all x2, waiting for transfers between devices, to_all(): lax.all_to_all(copies, axis, 0, 0, axis_index_groups=groups, tiled=True)  44.7 us
    all_to_all x1, blocking collectives, on_device(): parts = lax.all_to_all(partial, 'dp', 0, 0, tiled=True)  40.2 us
    all_to_all x1, blocking collectives, to_all(): lax.all_to_all(copies, axis, 0, 0, axis_index_groups=groups, tiled=True)  28.7 us
    all_gather x1, waiting for transfers between devices, on_device(): weight_full = lax.all_gather(head_weight, 'dp', axis=0, tiled=True)  18.1 us
    all_to_all x1, waiting for transfers between devices, on_device(): chunks = lax.all_to_all(chunks, 'dp', 0, 0, tiled=True)  15.4 us
    all_to_all x2, starting transfers between devices, to_all(): lax.all_to_all(copies, axis, 0, 0, axis_index_groups=groups, tiled=True)  14.3 us
    all_to_all x1, starting transfers between devices, on_device(): terms = lax.all_to_all(terms, 'vocab', 0, 0, tiled=True)  14.3 us
    ppermute x1, starting transfers between devices, on_device(): theirs = lax.ppermute(mine, 'vocab', swap)  11.4 us
  transfers between devices with their start and end apart: 7, of which 5 were waited for; matrix products, arithmetic and copies ran while one was open for 10% of the time, Pallas kernels for 2%

profile of v2, /device:TPU:1, one launch (start us, length us, event | category | flops | bytes accessed | tf_op | source)
XLA Modules:
  0.0 262.5 jit_solution(15758901834401224466)
XLA Ops:
  8.7 28.7 %all_to_all.30 = bf16[16,64,128]{2,1,0:T(8,128)(2,1)S(1)} all-to-all(bf16[16,64,128]{2,1,0:T(8,128)(2,1)S(1)} %broadcast_in_dim.10), channel_id=1, replica_groups=mesh['vocab'=32,'dp'=16] {'dp'}, dimensions={0} | all-to-all | bytes 524288 | tf_op jit(solution)/shard_map/all_to_all | solution.py:34
  37.4 3.0 %broadcast_in_dim.11 = bf16[16,16,64,128]{3,2,1,0:T(8,128)(2,1)} broadcast(bf16[16,64,128]{2,1,0:T(8,128)(2,1)S(1)} %all_to_all.30), dimensions={1,2,3} | broadcast | bytes 4456448 | tf_op jit(solution)/shard_map/broadcast_in_dim | solution.py:33
  40.4 6.8 %all-to-all-start.1 = ((bf16[16,16,64,128]{3,2,1,0:T(8,128)(2,1)}), bf16[16,16,64,128]{3,2,1,0:T(8,128)(2,1)}, u32[]{:S(2)}, u32[]{:S(2)}) async-start(bf16[16,16,64,128]{3,2,1,0:T(8,128)(2,1)} %broadcast_in_dim.11), calls=%async_computation.1 | async-start | bytes 8388608 | tf_op jit(solution)/shard_map/all_to_all | solution.py:34
  47.2 44.7 %all-to-all-done.1 = bf16[16,16,64,128]{3,2,1,0:T(8,128)(2,1)} async-done(((bf16[16,16,64,128]{3,2,1,0:T(8,128)(2,1)}), bf16[16,16,64,128]{3,2,1,0:T(8,128)(2,1)}, u32[]{:S(2)}, u32[]{:S(2)}) %all-to-all-start.1) | async-done | bytes 4194336 | tf_op jit(solution)/shard_map/all_to_all | solution.py:34
  91.9 1.0 dynamic-slice_bitcast_fusion
  92.9 11.4 %collective-permute-start = (bf16[16,64,128]{2,1,0:T(8,128)(2,1)S(1)}, bf16[16,64,128]{2,1,0:T(8,128)(2,1)S(1)}, u32[]{:S(2)}, u32[]{:S(2)}) collective-permute-start(bf16[16,64,128]{2,1,0:T(8,128)(2,1)S(1)} %dynamic-slice_bitcast_fusion), channel_id=1, source_target_pairs={{0,16},{16,0},{32,48},{48,32},{64,80},{80,64},{96,112},{112,96},{1... | collective-permute-start | bytes 786440 | tf_op jit(solution)/shard_map/ppermute | solution.py:132
  104.5 0.9 collective-permute-done
  105.4 1.0 select_bitcast_fusion.1
  106.5 18.1 %all-gather.2.cloned.1.call-done = bf16[2048,2048]{1,0:T(8,128)(2,1)} async-done(((bf16[128,2048]{1,0:T(8,128)(2,1)}), bf16[2048,2048]{1,0:T(8,128)(2,1)}) %all-gather.2.cloned.1.call-update) | async-done | bytes 8388624 | tf_op jit(solution)/shard_map/all_gather | solution.py:128
  124.7 4.7 %fusion.16 = (f32[128]{0:T(128)S(1)}, f32[128,2048]{1,0:T(8,128)S(1)}) fusion(bf16[2048,128]{1,0:T(8,128)(2,1)S(1)} %bitcast.61, bf16[2048,2048]{1,0:T(8,128)(2,1)} %all-gather.2.cloned.1.call-done), kind=kOutput, calls=%fused_computation.51 | convolution fusion | flops 1074003840 | bytes 9961984 | tf_op jit(solution)/shard_map/dot_general | solution.py:140
  130.9 7.5 %all-to-all-start.2 = ((f32[32,8,128]{2,1,0:T(8,128)}), f32[32,8,128]{2,1,0:T(8,128)S(1)}, u32[]{:S(2)}, u32[]{:S(2)}) async-start(f32[32,8,128]{2,1,0:T(8,128)} %broadcast_in_dim.14), calls=%async_computation.2 | async-start | bytes 262144 | tf_op jit(solution)/shard_map/all_to_all | solution.py:34
  138.7 5.7 %copy.40 = bf16[16,64,16,128]{3,2,1,0:T(8,128)(2,1)S(1)} copy(bf16[16,64,16,128]{3,1,2,0:T(8,128)(2,1)} %bitcast.23) | data formatting | bytes 8388608 | tf_op jit(solution)/shard_map/transpose | solution.py:136
  144.4 4.1 %copy.51 = bf16[128,8,16,128]{3,1,2,0:T(8,128)(2,1)} copy(bf16[128,8,16,128]{3,2,1,0:T(8,128)(2,1)S(1)} %bitcast.60) | data formatting | bytes 8388608
  148.5 2.1 collective-permute-start.1
  153.2 0.9 bitcast_bitcast_fusion
  154.2 9.2 %all-to-all-start.3 = ((bf16[16,128,128]{2,1,0:T(8,128)(2,1)}), bf16[16,128,128]{2,1,0:T(8,128)(2,1)S(1)}, u32[]{:S(2)}, u32[]{:S(2)}) async-start(bf16[16,128,128]{2,1,0:T(8,128)(2,1)} %bitcast_bitcast_fusion), calls=%async_computation.3 | async-start | bytes 1048576 | tf_op jit(solution)/shard_map/all_to_all | solution.py:188
  163.3 6.3 %convolution_convert_fusion = bf16[128,2048]{1,0:T(8,128)(2,1)S(1)} fusion(bf16[128,2048]{1,0:T(8,128)(2,1)S(1)} %fusion.4, bf16[2048,2048]{1,0:T(8,128)(2,1)} %all-gather.2.cloned.1.call-done), kind=kOutput, calls=%fused_computation.1 | convolution fusion | flops 1074003968 | bytes 9437184 | tf_op jit(solution)/shard_map/dot_general | solution.py:189
  169.6 1.0 copy.42
  170.6 15.4 %all-to-all-done.3 = bf16[16,128,128]{2,1,0:T(8,128)(2,1)S(1)} async-done(((bf16[16,128,128]{2,1,0:T(8,128)(2,1)}), bf16[16,128,128]{2,1,0:T(8,128)(2,1)S(1)}, u32[]{:S(2)}, u32[]{:S(2)}) %all-to-all-start.3) | async-done | bytes 524320 | tf_op jit(solution)/shard_map/all_to_all | solution.py:188
  186.0 14.3 %all-to-all-start.4 = ((bf16[32,128,64]{1,2,0:T(8,128)(2,1)}), bf16[32,128,64]{1,2,0:T(8,128)(2,1)S(1)}, u32[]{:S(2)}, u32[]{:S(2)}) async-start(bf16[32,128,64]{1,2,0:T(8,128)(2,1)} %bitcast.26), calls=%async_computation.4 | async-start | bytes 1048576 | tf_op jit(solution)/shard_map/all_to_all | solution.py:201
  201.5 5.4 %shard_map.85 = bf16[16,144,128]{2,1,0:T(8,128)(2,1)S(1)} custom-call(s32[1]{0:T(128)} %bitcast.core_ref, f32[1]{0:T(128)} %bitcast.22.objective_ref, bf16[1024,2048]{1,0:T(8,128)(2,1)} %bitcast.58.own_ref, bf16[1024,2048]{1,0:T(8,128)(2,1)} %collective-permute-done.1.other_ref, bf16[2048,128]{1,0:T(8,128)(2,1)S(1)} %bitcast.59), custom_call_target="tpu_custom_call" | custom-call | flops 1073741824 | bytes 9437184 | tf_op jit(solution)/shard_map/pallas_call | solution.py:74
  206.9 5.0 %all-to-all-done.4 = bf16[32,128,64]{1,2,0:T(8,128)(2,1)S(1)} async-done(((bf16[32,128,64]{1,2,0:T(8,128)(2,1)}), bf16[32,128,64]{1,2,0:T(8,128)(2,1)S(1)}, u32[]{:S(2)}, u32[]{:S(2)}) %all-to-all-start.4) | async-done | bytes 524320 | tf_op jit(solution)/shard_map/all_to_all | solution.py:201
  212.6 40.2 %all_to_all.31.parts_ref = bf16[16,144,128]{2,1,0:T(8,128)(2,1)S(1)} all-to-all(bf16[16,144,128]{2,1,0:T(8,128)(2,1)S(1)} %shard_map.85), channel_id=1, replica_groups=mesh['vocab'=32,'dp'=16] {'dp'}, dimensions={0} | all-to-all | bytes 1179648 | tf_op jit(solution)/shard_map/all_to_all | solution.py:204
  252.8 1.1 shard_map.86
  (38 shorter events, 6.7 us)
Async XLA Ops:
  7.2 97.2 %copy-start = (bf16[128,2048]{1,0:T(8,128)(2,1)S(1)}, bf16[128,2048]{1,0:T(8,128)(2,1)}, u32[]{:S(2)}) copy-start(bf16[128,2048]{1,0:T(8,128)(2,1)} %param.8) | copy-start | bytes 1572868
  7.2 117.5 %all-gather.2.cloned.1.call-start = ((), (), s32[]{:S(2)}) async-start(), calls=%async_computation.6 | async-start | bytes 8912896 | tf_op jit(solution)/shard_map/all_gather | solution.py:128
  40.4 51.5 %all-to-all-start.1 = ((bf16[16,16,64,128]{3,2,1,0:T(8,128)(2,1)}), bf16[16,16,64,128]{3,2,1,0:T(8,128)(2,1)}, u32[]{:S(2)}, u32[]{:S(2)}) async-start(bf16[16,16,64,128]{3,2,1,0:T(8,128)(2,1)} %broadcast_in_dim.11), calls=%async_computation.1 | async-start | bytes 8388608 | tf_op jit(solution)/shard_map/all_to_all | solution.py:34
  92.9 12.6 %collective-permute-start = (bf16[16,64,128]{2,1,0:T(8,128)(2,1)S(1)}, bf16[16,64,128]{2,1,0:T(8,128)(2,1)S(1)}, u32[]{:S(2)}, u32[]{:S(2)}) collective-permute-start(bf16[16,64,128]{2,1,0:T(8,128)(2,1)S(1)} %dynamic-slice_bitcast_fusion), channel_id=1, source_target_pairs={{0,16},{16,0},{32,48},{48,32},{64,80},{80,64},{96,112},{112,96},{1... | collective-permute-start | bytes 786440 | tf_op jit(solution)/shard_map/ppermute | solution.py:132
  106.5 22.9 %copy-start.1 = (s32[128]{0:T(128)S(1)}, s32[128]{0:T(128)}, u32[]{:S(2)}) copy-start(s32[128]{0:T(128)} %param.9) | copy-start | bytes 1540
  124.7 13.8 %copy-start.2 = (s32[1,16]{1,0:T(1,128)S(1)}, s32[1,16]{1,0:T(1,128)}, u32[]{:S(2)}) copy-start(s32[1,16]{1,0:T(1,128)} %param.11) | copy-start | bytes 196
  130.9 19.7 %all-to-all-start.2 = ((f32[32,8,128]{2,1,0:T(8,128)}), f32[32,8,128]{2,1,0:T(8,128)S(1)}, u32[]{:S(2)}, u32[]{:S(2)}) async-start(f32[32,8,128]{2,1,0:T(8,128)} %broadcast_in_dim.14), calls=%async_computation.2 | async-start | bytes 262144 | tf_op jit(solution)/shard_map/all_to_all | solution.py:34
  138.7 12.8 %copy-start.3 = (s32[1,128]{1,0:T(1,128)S(1)}, s32[1,128]{1,0:T(1,128)}, u32[]{:S(2)}) copy-start(s32[1,128]{1,0:T(1,128)} %param.10) | copy-start | bytes 1540
  148.5 53.0 %collective-permute-start.1 = (bf16[1024,2048]{1,0:T(8,128)(2,1)}, bf16[1024,2048]{1,0:T(8,128)(2,1)}, u32[]{:S(2)}, u32[]{:S(2)}) collective-permute-start(bf16[1024,2048]{1,0:T(8,128)(2,1)} %bitcast.58.own_ref), channel_id=1, source_target_pairs={{0,16},{16,0},{32,48},{48,32},{64,80},{80,64},{96,112},{112,96},{1... | collective-permute-start | bytes 12582920 | tf_op jit(solution)/shard_map/ppermute | solution.py:137
  154.2 31.8 %all-to-all-start.3 = ((bf16[16,128,128]{2,1,0:T(8,128)(2,1)}), bf16[16,128,128]{2,1,0:T(8,128)(2,1)S(1)}, u32[]{:S(2)}, u32[]{:S(2)}) async-start(bf16[16,128,128]{2,1,0:T(8,128)(2,1)} %bitcast_bitcast_fusion), calls=%async_computation.3 | async-start | bytes 1048576 | tf_op jit(solution)/shard_map/all_to_all | solution.py:188
  186.0 25.9 %all-to-all-start.4 = ((bf16[32,128,64]{1,2,0:T(8,128)(2,1)}), bf16[32,128,64]{1,2,0:T(8,128)(2,1)S(1)}, u32[]{:S(2)}, u32[]{:S(2)}) async-start(bf16[32,128,64]{1,2,0:T(8,128)(2,1)} %bitcast.26), calls=%async_computation.4 | async-start | bytes 1048576 | tf_op jit(solution)/shard_map/all_to_all | solution.py:201
Sparse Core Ops, SparseCore 0:
  10.1 114.5 all-gather.1

commit v3 on v2

v3 whole, which is shorter than its diff:
```python
import jax
import jax.numpy as jnp
from jax import lax
from jax.experimental import pallas as pl
from jax.experimental.pallas import tpu as pltpu
from jax.sharding import PartitionSpec as P

dpo_beta = 0.1
dpo_gamma = 4.0


def pair_signs(segments, ordering):
    count = ordering.shape[0]
    labels = lax.broadcasted_iota(jnp.int32, (count, 1), 0)
    seq_hot = (segments[None, :] == labels).astype(jnp.float32)
    chosen = (labels == ordering[None, 0::2]).astype(jnp.float32)
    rejected = (labels == ordering[None, 1::2]).astype(jnp.float32)
    side = chosen - rejected
    pair = chosen + rejected
    margin_sign = jnp.sum(pair[:, None, :] * side[None, :, :], axis=2)
    into_margin = jnp.sum(margin_sign[:, :, None] * seq_hot[None, :, :], axis=1)
    into_weight = jnp.sum(side, axis=1)[:, None] * seq_hot
    return into_margin, into_weight


def to_all(block, axis, groups=None):
    count = lax.axis_size(axis) if groups is None else len(groups[0])
    copies = jnp.broadcast_to(block[None], (count,) + block.shape)
    return lax.all_to_all(copies, axis, 0, 0, axis_index_groups=groups, tiled=True)


def relayout_kernel(in_ref, out_ref):
    groups, _, rows = in_ref.shape[1:]
    for j in range(groups):
        out_ref[:, j * rows : (j + 1) * rows] = in_ref[0, j]


def relayout(by_pair):
    pairs, groups, feats, rows = by_pair.shape
    return pl.pallas_call(
        relayout_kernel,
        out_shape=jax.ShapeDtypeStruct((pairs * feats, groups * rows), by_pair.dtype),
        grid=(pairs,),
        in_specs=[pl.BlockSpec((1, groups, feats, rows), lambda i: (i, 0, 0, 0))],
        out_specs=pl.BlockSpec((feats, groups * rows), lambda i: (i, 0)),
        compiler_params=pltpu.CompilerParams(vmem_limit_bytes=16 * 1024 * 1024),
        cost_estimate=pl.CostEstimate(flops=0, bytes_accessed=4 * by_pair.size, transcendentals=0),
    )(by_pair)


def grad_kernel(
    every_ref, student_ref, teacher_ref, target_ref, margin_ref, weight_ref,
    grad_ref, gathered_ref, chunks_ref, objective_ref,
):
    f32, bf16 = jnp.float32, jnp.bfloat16
    maxes_s, maxes_t = every_ref[:, 0, :], every_ref[:, 1, :]
    max_s = jnp.max(maxes_s, axis=0, keepdims=True)
    max_t = jnp.max(maxes_t, axis=0, keepdims=True)
    scale_s = jnp.exp(maxes_s - max_s)
    scale_t = jnp.exp(maxes_t - max_t)
    sum_s = jnp.sum(every_ref[:, 2, :] * scale_s, axis=0, keepdims=True)
    sum_t = jnp.sum(every_ref[:, 3, :] * scale_t, axis=0, keepdims=True)
    cross = jnp.sum(every_ref[:, 4, :] * scale_t, axis=0, keepdims=True)
    target_s = jnp.sum(every_ref[:, 5, :], axis=0, keepdims=True)
    target_t = jnp.sum(every_ref[:, 6, :], axis=0, keepdims=True)
    lse_s = max_s + jnp.log(sum_s)
    lse_t = max_t + jnp.log(sum_t)
    kl = cross / sum_t - lse_t + lse_s
    log_ratio = target_s - lse_s - (target_t - lse_t)
    margin = dpo_beta * jnp.sum(margin_ref[...] * log_ratio, axis=1, keepdims=True)
    strength = dpo_gamma * dpo_beta / (1.0 + jnp.exp(margin))
    weight = -jnp.sum(weight_ref[...] * strength, axis=0, keepdims=True)
    dpo = jnp.maximum(-margin, 0.0) + jnp.log(1.0 + jnp.exp(-jnp.abs(margin)))
    objective_ref[0] = jnp.sum(kl) + 0.5 * dpo_gamma * jnp.sum(dpo)
    lines = jnp.concatenate(
        [max_s, 1.0 / sum_s, max_t, 1.0 / sum_t, weight, weight, weight, weight], axis=0
    )
    columns = jnp.transpose(lines)
    max_s, inv_s = columns[:, 0:1], columns[:, 1:2]
    max_t, inv_t, weight = columns[:, 2:3], columns[:, 3:4], columns[:, 4:5]
    target = target_ref[...]
    rows, width = student_ref.shape
    split = gathered_ref.shape[1]
    step = 256
    for low in range(0, width, step):
        prob_s = jnp.exp(student_ref[:, low : low + step] - max_s) * inv_s
        prob_t = jnp.exp(teacher_ref[:, low : low + step].astype(f32) - max_t) * inv_t
        column = lax.broadcasted_iota(jnp.int32, (rows, step), 1) + low
        hot = jnp.where(column == target, 1.0, 0.0)
        grad = prob_s - prob_t + weight * (hot - prob_s)
        rounded = grad.astype(bf16)
        grad_ref[:, low : low + step] = rounded
        if low < split:
            gathered_ref[:, low : low + step] = rounded
        else:
            chunks_ref[low - split : low - split + step, :] = jnp.transpose(grad).astype(bf16)


def make_grad(every, student, teacher, target, into_margin, into_weight, split):
    rows, width = student.shape
    f32, bf16 = jnp.float32, jnp.bfloat16
    vmem = pl.BlockSpec(memory_space=pltpu.VMEM)
    return pl.pallas_call(
        grad_kernel,
        out_shape=(
            jax.ShapeDtypeStruct((rows, width), bf16),
            jax.ShapeDtypeStruct((rows, split), bf16),
            jax.ShapeDtypeStruct((width - split, rows), bf16),
            jax.ShapeDtypeStruct((1,), f32),
        ),
        out_specs=(vmem, vmem, vmem, pl.BlockSpec(memory_space=pltpu.SMEM)),
        compiler_params=pltpu.CompilerParams(vmem_limit_bytes=32 * 1024 * 1024),
    )(every, student, teacher, target, into_margin, into_weight)


def head_kernel(core_ref, objective_ref, own_ref, other_ref, grad_ref, out_ref, wide_ref):
    f32, bf16 = jnp.float32, jnp.bfloat16
    groups, chunk, rows = grad_ref.shape

    @pl.when(pl.program_id(0) == 0)
    def _():
        for z in range(groups):
            wide_ref[:, z * rows : (z + 1) * rows] = grad_ref[z]

    nt = (((1,), (1,)), ((), ()))
    wide = wide_ref[...]
    own = lax.dot_general(wide, own_ref[...], nt, preferred_element_type=f32)
    other = lax.dot_general(wide, other_ref[...], nt, preferred_element_type=f32)
    is_first = core_ref[0] == 0
    first = jnp.where(is_first, own, other)
    second = jnp.where(is_first, other, own)
    blocks, tall, lanes = out_ref.shape
    half = lanes // 2
    value = jnp.full((tall - chunk, lanes), objective_ref[0], f32)
    high = value.astype(bf16).astype(f32)
    middle = (value - high).astype(bf16).astype(f32)
    low = value - high - middle
    line = lax.broadcasted_iota(jnp.int32, value.shape, 0)
    pieces = jnp.where(line == 0, high, jnp.where(line == 1, middle, jnp.where(line == 2, low, 0.0)))
    pieces = pieces.astype(bf16)
    left = lax.broadcasted_iota(jnp.int32, (chunk, lanes), 1) < half
    for j in range(0, blocks, 2):
        front = first[:, j * half : j * half + lanes]
        back = second[:, j * half : j * half + lanes]
        out_ref[j, :chunk] = jnp.where(left, front, pltpu.roll(back, half, 1)).astype(bf16)
        out_ref[j + 1, :chunk] = jnp.where(left, pltpu.roll(front, half, 1), back).astype(bf16)
        out_ref[j, chunk:] = pieces
        out_ref[j + 1, chunk:] = pieces


def head_partial(core, objective, own, other, grad, blocks, extra):
    tall, all_rows = own.shape
    groups, chunk, rows = grad.shape
    steps = 4
    per = blocks // steps
    lanes = 2 * tall // blocks
    return pl.pallas_call(
        head_kernel,
        out_shape=jax.ShapeDtypeStruct((blocks, chunk + extra, lanes), jnp.bfloat16),
        grid=(steps,),
        in_specs=[
            pl.BlockSpec(memory_space=pltpu.SMEM),
            pl.BlockSpec(memory_space=pltpu.SMEM),
            pl.BlockSpec((tall // steps, all_rows), lambda i: (i, 0)),
            pl.BlockSpec((tall // steps, all_rows), lambda i: (i, 0)),
            pl.BlockSpec((groups, chunk, rows), lambda i: (0, 0, 0)),
        ],
        out_specs=pl.BlockSpec((per, chunk + extra, lanes), lambda i: (i, 0, 0)),
        scratch_shapes=[pltpu.VMEM((chunk, all_rows), jnp.bfloat16)],
        compiler_params=pltpu.CompilerParams(vmem_limit_bytes=32 * 1024 * 1024),
        cost_estimate=pl.CostEstimate(
            flops=4 * tall * all_rows * chunk,
            bytes_accessed=4 * tall * all_rows + 2 * all_rows * chunk + 4 * tall * chunk,
            transcendentals=0,
        ),
    )(core, objective, own, other, grad)


def finish_kernel(hidden_ref, gathered_ref, parts_ref, grad_ref, total_ref, stack_ref):
    f32 = jnp.float32
    count, tall, feats = parts_ref.shape
    step = gathered_ref.shape[1]
    i = pl.program_id(0)
    low = pl.multiple_of(i * step, step)
    grad_ref[:, pl.ds(low, step)] = jnp.dot(
        hidden_ref[...], gathered_ref[...], preferred_element_type=f32
    )

    @pl.when(i == 0)
    def _():
        chunk = stack_ref.shape[0] // count
        split = grad_ref.shape[1] - stack_ref.shape[0]
        for j in range(count):
            stack_ref[j * chunk : (j + 1) * chunk] = parts_ref[j, :chunk].astype(f32)
        for j in range(0, count * chunk, feats):
            grad_ref[:, split + j : split + j + feats] = jnp.transpose(stack_ref[j : j + feats])
        lines = jnp.sum(parts_ref[:, chunk:].astype(f32), axis=0)
        total_ref[0] = jnp.sum(lines[:3, :1])


def finish(hidden_slab, gathered, parts, extra):
    feats, all_rows = hidden_slab.shape
    split = gathered.shape[1]
    count, tall, _ = parts.shape
    chunk = tall - extra
    step = 256
    width = split + count * chunk
    return pl.pallas_call(
        finish_kernel,
        out_shape=(
            jax.ShapeDtypeStruct((feats, width), jnp.float32),
            jax.ShapeDtypeStruct((1,), jnp.float32),
        ),
        grid=(split // step,),
        in_specs=[
            pl.BlockSpec((feats, all_rows), lambda i: (0, 0)),
            pl.BlockSpec((all_rows, step), lambda i: (0, i)),
            pl.BlockSpec((count, tall, feats), lambda i: (0, 0, 0)),
        ],
        out_specs=(
            pl.BlockSpec((feats, width), lambda i: (0, 0)),
            pl.BlockSpec(memory_space=pltpu.SMEM),
        ),
        scratch_shapes=[pltpu.VMEM((count * chunk, feats), jnp.float32)],
        compiler_params=pltpu.CompilerParams(vmem_limit_bytes=32 * 1024 * 1024),
    )(hidden_slab, gathered, parts)


def on_device(hidden, head_weight, teacher_logits, target_ids, segment_ids, pair_order):
    f32, bf16 = jnp.float32, jnp.bfloat16
    n_vocab = lax.axis_size("vocab")
    n_dp = lax.axis_size("dp")
    rows, feats = hidden.shape
    width = head_weight.shape[1]
    pairs = n_vocab // 2
    core = lax.axis_index("vocab") % 2
    same_core = [[2 * j + c for j in range(pairs)] for c in range(2)]
    swap = [(i, i ^ 1) for i in range(n_vocab)]
    weight_full = lax.all_gather(head_weight, "dp", axis=0, tiled=True)
    by_group = to_all(hidden.T, "dp").reshape(n_dp, feats, rows)
    by_pair = to_all(by_group, "vocab", same_core).reshape(pairs, n_dp, feats, rows)
    own_t = relayout(by_pair)
    other_t = lax.ppermute(own_t, "vocab", swap)
    place = lax.axis_index("dp")

    def by_core(own, other, axis):
        return jnp.stack([jnp.where(core == 0, own, other), jnp.where(core == 0, other, own)], axis=axis)

    mine = lax.dynamic_slice_in_dim(own_t, place * rows, rows, 1).reshape(pairs, feats, rows)
    theirs = lax.dynamic_slice_in_dim(other_t, place * rows, rows, 1).reshape(pairs, feats, rows)
    rows_t = by_core(mine, theirs, 1).reshape(n_vocab * feats, rows)
    slab = by_core(
        lax.dynamic_slice_in_dim(own_t, place * feats, feats, 0),
        lax.dynamic_slice_in_dim(other_t, place * feats, feats, 0),
        0,
    ).reshape(2 * feats, n_dp * rows)
    into_margin, into_weight = pair_signs(segment_ids[0], pair_order[0])
    tn = (((0,), (0,)), ((), ()))
    nt = (((1,), (1,)), ((), ()))
    student = lax.dot_general(rows_t, weight_full, tn, preferred_element_type=f32)
    teacher = teacher_logits.astype(f32)
    offset = lax.axis_index("vocab") * width
    column = lax.broadcasted_iota(jnp.int32, student.shape, 1) + offset
    is_target = column == target_ids[:, None]
    own_max = jnp.max(student, axis=1)
    own_tmax = jnp.max(teacher, axis=1)
    own_exp = jnp.exp(student - own_max[:, None])
    own_texp = jnp.exp(teacher - own_tmax[:, None])
    stats = jnp.stack(
        [
            own_max,
            own_tmax,
            jnp.sum(own_exp, axis=1),
            jnp.sum(own_texp, axis=1),
            jnp.sum(own_texp * (teacher - student), axis=1),
            jnp.sum(jnp.where(is_target, student, 0.0), axis=1),
            jnp.sum(jnp.where(is_target, teacher, 0.0), axis=1),
            jnp.zeros((rows,), f32),
        ]
    )
    every = to_all(stats, "vocab").reshape(n_vocab, 8, rows)
    split = 3 * width // 8
    extra = 16
    logit_grad, gathered, chunks, objective = make_grad(
        every, student, teacher_logits, (target_ids - offset)[:, None], into_margin, into_weight, split
    )
    gathered = lax.all_gather(gathered, "dp", axis=0, tiled=True)
    chunks = chunks.reshape(n_dp, (width - split) // n_dp, rows)
    chunks = lax.all_to_all(chunks, "dp", 0, 0, tiled=True)
    hidden_term = lax.dot_general(logit_grad, weight_full, nt, preferred_element_type=f32)
    terms = hidden_term.astype(bf16).reshape(rows, n_vocab, feats).swapaxes(0, 1)
    chunks, terms = lax.optimization_barrier((chunks, terms))
    partial = head_partial(
        core.astype(jnp.int32).reshape(1), objective, own_t, other_t, chunks, pairs, extra
    )
    terms = lax.all_to_all(terms, "vocab", 0, 0, tiled=True)
    hidden_grad = jnp.sum(terms.astype(f32), axis=0).astype(bf16)
    partial, hidden_grad = lax.optimization_barrier((partial, hidden_grad))
    parts = lax.all_to_all(partial, "dp", 0, 0, tiled=True)
    head_grad, total = finish(slab, gathered, parts, extra)
    loss_value = total[0] / (rows * n_dp)
    return (hidden_grad, head_grad, loss_value)


def solution(mesh):
    return jax.shard_map(
        on_device,
        mesh=mesh,
        in_specs=(
            P("dp", "vocab"),
            P("dp", "vocab"),
            P("dp", "vocab"),
            P("dp"),
            P("dp", None),
            P("dp", None),
        ),
        out_specs=(P("dp", "vocab"), P("dp", "vocab"), P()),
        check_vma=False,
    )
```

time: 263 us -> 256 us (0.973)
  the two profiles are of different devices: /device:TPU:1 before, /device:TPU:2 now
where the time goes in v3:
time: 256 us; the launch traced here: 255 us
  waiting for transfers between devices  86.5 us (34%)
  blocking collectives  83.7 us (33%)
  starting transfers between devices  29.8 us (12%)
  Pallas kernels  17.5 us (7%)
  between operations  16 us (6%)
  matrix products  11 us (4%)
  local copies, waits for them, and re-layouts  5.79 us (2%)
  other arithmetic  4.45 us (2%)
    all_to_all x2, blocking collectives, to_all(): lax.all_to_all(copies, axis, 0, 0, axis_index_groups=groups, tiled=True)  83.7 us
    all_to_all x1, waiting for transfers between devices, on_device(): parts = lax.all_to_all(partial, 'dp', 0, 0, tiled=True)  25.8 us
    all_to_all x1, waiting for transfers between devices, on_device(): chunks = lax.all_to_all(chunks, 'dp', 0, 0, tiled=True)  17.6 us
    all_gather x1, waiting for transfers between devices, on_device(): gathered = lax.all_gather(gathered, 'dp', axis=0, tiled=True)  13.5 us
    all_gather x1, waiting for transfers between devices, on_device(): weight_full = lax.all_gather(head_weight, 'dp', axis=0, tiled=True)  13.3 us
    all_to_all x1, starting transfers between devices, on_device(): chunks = lax.all_to_all(chunks, 'dp', 0, 0, tiled=True)  9.46 us
    all_to_all x1, starting transfers between devices, to_all(): lax.all_to_all(copies, axis, 0, 0, axis_index_groups=groups, tiled=True)  7.62 us
    pallas_call x1, Pallas kernels, head_partial(): pl.pallas_call(head_kernel, out_shape=jax.ShapeDtypeStruct((blocks, chunk...  7.21 us
  transfers between devices with their start and end apart: 7, of which 7 were waited for; matrix products, arithmetic and copies ran while one was open for 5% of the time, Pallas kernels for 5%

profile of v3, /device:TPU:2, one launch (start us, length us, event | category | flops | bytes accessed | tf_op | source)
XLA Modules:
  0.0 254.8 jit_solution(16168719123714711503)
XLA Ops:
  8.7 34.1 %all_to_all.30 = bf16[16,64,128]{2,1,0:T(8,128)(2,1)S(1)} all-to-all(bf16[16,64,128]{2,1,0:T(8,128)(2,1)S(1)} %broadcast_in_dim.12), channel_id=1, replica_groups=mesh['vocab'=32,'dp'=16] {'dp'}, dimensions={0} | all-to-all | bytes 524288 | tf_op jit(solution)/shard_map/all_to_all | solution.py:29
  42.7 1.1 broadcast_in_dim.13
  43.8 49.7 %all_to_all.31.in_ref = bf16[16,16,64,128]{3,2,1,0:T(8,128)(2,1)S(1)} all-to-all(bf16[16,16,64,128]{3,2,1,0:T(8,128)(2,1)S(1)} %broadcast_in_dim.13), channel_id=1, replica_groups={{0,32,64,96,128,160,192,224,256,288,320,352,384,416,448,480},{16,48,80,..., dimensions={0} | all-to-all | bytes 8388608 | tf_op jit(solution)/shard_map/all_to_all | solution.py:29
  93.5 6.2 %shard_map.88.own_ref = bf16[1024,2048]{1,0:T(8,128)(2,1)} custom-call(bf16[16,16,64,128]{3,2,1,0:T(8,128)(2,1)S(1)} %all_to_all.31.in_ref), custom_call_target="tpu_custom_call" | custom-call | bytes 8388608 | tf_op jit(solution)/shard_map/pallas_call | solution.py:40
  99.7 1.9 collective-permute-start
  102.3 6.8 %collective-permute-done.other_ref = bf16[1024,2048]{1,0:T(8,128)(2,1)} collective-permute-done((bf16[1024,2048]{1,0:T(8,128)(2,1)}, bf16[1024,2048]{1,0:T(8,128)(2,1)}, u32[]{:S(2)}, u32[]{:S(2)}) %collective-permute-start) | collective-permute-done | bytes 4194336 | tf_op jit(solution)/shard_map/ppermute | solution.py:243
  109.1 1.2 broadcast_select_fusion.1
  110.3 13.3 %all-gather.3.cloned.1.call-done = bf16[2048,2048]{1,0:T(8,128)(2,1)} async-done(((bf16[128,2048]{1,0:T(8,128)(2,1)}), bf16[2048,2048]{1,0:T(8,128)(2,1)}) %all-gather.3.cloned.1.call-update) | async-done | bytes 8388624 | tf_op jit(solution)/shard_map/all_gather | solution.py:239
  123.6 4.7 %fusion.10 = (f32[128]{0:T(128)S(1)}, f32[128,2048]{1,0:T(8,128)S(1)}) fusion(bf16[2048,128]{1,0:T(8,128)(2,1)S(1)} %bitcast.36, bf16[2048,2048]{1,0:T(8,128)(2,1)} %all-gather.3.cloned.1.call-done), kind=kOutput, calls=%fused_computation.32 | convolution fusion | flops 1074003840 | bytes 9961984 | tf_op jit(solution)/shard_map/dot_general | solution.py:260
  129.9 7.6 %all-to-all-start.2 = ((f32[32,8,128]{2,1,0:T(8,128)}), f32[32,8,128]{2,1,0:T(8,128)S(1)}, u32[]{:S(2)}, u32[]{:S(2)}) async-start(f32[32,8,128]{2,1,0:T(8,128)} %broadcast_in_dim.15), calls=%async_computation.2 | async-start | bytes 262144 | tf_op jit(solution)/shard_map/all_to_all | solution.py:29
  137.9 6.3 %all-to-all-done.2.every_ref = f32[32,8,128]{2,1,0:T(8,128)S(1)} async-done(((f32[32,8,128]{2,1,0:T(8,128)}), f32[32,8,128]{2,1,0:T(8,128)S(1)}, u32[]{:S(2)}, u32[]{:S(2)}) %all-to-all-start.2) | async-done | bytes 131104 | tf_op jit(solution)/shard_map/all_to_all | solution.py:29
  144.2 1.7 shard_map.89
  145.9 9.5 %all-to-all-start.3 = ((bf16[16,80,128]{2,1,0:T(8,128)(2,1)}), bf16[16,80,128]{2,1,0:T(8,128)(2,1)S(1)}, u32[]{:S(2)}, u32[]{:S(2)}) async-start(bf16[16,80,128]{2,1,0:T(8,128)(2,1)} %bitcast.17), calls=%async_computation.3 | async-start | bytes 655360 | tf_op jit(solution)/shard_map/all_to_all | solution.py:289
  155.3 6.3 %convolution_convert_fusion = bf16[128,2048]{1,0:T(8,128)(2,1)S(1)} fusion(bf16[128,2048]{1,0:T(8,128)(2,1)S(1)} %get-tuple-element.15, bf16[2048,2048]{1,0:T(8,128)(2,1)} %all-gather.3.cloned.1.call-done), kind=kOutput, calls=%fused_computation | convolution fusion | flops 1074003968 | bytes 9437184 | tf_op jit(solution)/shard_map/dot_general | solution.py:290
  162.6 17.6 %all-to-all-done.3.grad_ref = bf16[16,80,128]{2,1,0:T(8,128)(2,1)S(1)} async-done(((bf16[16,80,128]{2,1,0:T(8,128)(2,1)}), bf16[16,80,128]{2,1,0:T(8,128)(2,1)S(1)}, u32[]{:S(2)}, u32[]{:S(2)}) %all-to-all-start.3) | async-done | bytes 327712 | tf_op jit(solution)/shard_map/all_to_all | solution.py:289
  180.2 5.1 %all-to-all-start.4 = ((bf16[32,128,64]{1,2,0:T(8,128)(2,1)}), bf16[32,128,64]{1,2,0:T(8,128)(2,1)S(1)}, u32[]{:S(2)}, u32[]{:S(2)}) async-start(bf16[32,128,64]{1,2,0:T(8,128)(2,1)} %bitcast.19), calls=%async_computation.4 | async-start | bytes 1048576 | tf_op jit(solution)/shard_map/all_to_all | solution.py:296
  185.4 7.2 %shard_map.90 = bf16[16,96,128]{2,1,0:T(8,128)(2,1)} custom-call(s32[1]{0:T(128)} %bitcast.core_ref, f32[1]{0:T(128)} %get-tuple-element.13.objective_ref, bf16[1024,2048]{1,0:T(8,128)(2,1)} %shard_map.88.own_ref, bf16[1024,2048]{1,0:T(8,128)(2,1)} %collective-permute-done.other_ref, bf16[16,80,128]{2,1,0:T(8,128)(2,1)S(1)} %all-to-all-done.3.grad_ref), custom_call_target="tpu_custom_call" | custom-call | flops 671088640 | bytes 9043968 | tf_op jit(solution)/shard_map/pallas_call | solution.py:157
  192.6 2.5 all-to-all-done.4
  195.8 5.6 %all-to-all-start.5 = ((bf16[16,96,128]{2,1,0:T(8,128)(2,1)}), bf16[16,96,128]{2,1,0:T(8,128)(2,1)S(1)}, u32[]{:S(2)}, u32[]{:S(2)}) async-start(bf16[16,96,128]{2,1,0:T(8,128)(2,1)} %shard_map.90), calls=%async_computation.5 | async-start | bytes 786432 | tf_op jit(solution)/shard_map/all_to_all | solution.py:299
  201.4 1.1 select_bitcast_fusion.1
  202.6 25.8 %all-to-all-done.5.parts_ref = bf16[16,96,128]{2,1,0:T(8,128)(2,1)S(1)} async-done(((bf16[16,96,128]{2,1,0:T(8,128)(2,1)}), bf16[16,96,128]{2,1,0:T(8,128)(2,1)S(1)}, u32[]{:S(2)}, u32[]{:S(2)}) %all-to-all-start.5) | async-done | bytes 393248 | tf_op jit(solution)/shard_map/all_to_all | solution.py:299
  228.4 13.5 %all-gather.5.cloned.1.call-done.gathered_ref = bf16[2048,768]{1,0:T(8,128)(2,1)} async-done(((bf16[128,768]{1,0:T(8,128)(2,1)}), bf16[2048,768]{1,0:T(8,128)(2,1)}) %all-gather.5.cloned.1.call-update) | async-done | bytes 3145744 | tf_op jit(solution)/shard_map/all_gather | solution.py:287
  241.9 1.9 copy-done.1
  243.8 2.4 shard_map.91
  (35 shorter events, 5.8 us)
Async XLA Ops:
  7.2 116.4 %all-gather.3.cloned.1.call-start = ((), (), s32[]{:S(2)}) async-start(), calls=%async_computation.6 | async-start | bytes 8912896 | tf_op jit(solution)/shard_map/all_gather | solution.py:239
  93.5 8.2 %copy-start.4 = (s32[1,16]{1,0:T(1,128)S(1)}, s32[1,16]{1,0:T(1,128)}, u32[]{:S(2)}) copy-start(s32[1,16]{1,0:T(1,128)} %param.11) | copy-start | bytes 196
  93.5 8.5 %copy-start = (bf16[128,2048]{1,0:T(8,128)(2,1)S(1)}, bf16[128,2048]{1,0:T(8,128)(2,1)}, u32[]{:S(2)}) copy-start(bf16[128,2048]{1,0:T(8,128)(2,1)} %teacher_ref.1) | copy-start | bytes 1572868
  93.5 8.7 %copy-start.3 = (s32[128]{0:T(128)S(1)}, s32[128]{0:T(128)}, u32[]{:S(2)}) copy-start(s32[128]{0:T(128)} %param.9) | copy-start | bytes 1540
  93.5 8.7 %copy-start.2 = (s32[1,128]{1,0:T(1,128)S(1)}, s32[1,128]{1,0:T(1,128)}, u32[]{:S(2)}) copy-start(s32[1,128]{1,0:T(1,128)} %param.10) | copy-start | bytes 1540
  99.7 9.4 %collective-permute-start = (bf16[1024,2048]{1,0:T(8,128)(2,1)}, bf16[1024,2048]{1,0:T(8,128)(2,1)}, u32[]{:S(2)}, u32[]{:S(2)}) collective-permute-start(bf16[1024,2048]{1,0:T(8,128)(2,1)} %shard_map.88.own_ref), channel_id=1, source_target_pairs={{0,16},{16,0},{32,48},{48,32},{64,80},{80,64},{96,112},{112,96},{1... | collective-permute-start | bytes 12582920 | tf_op jit(solution)/shard_map/ppermute | solution.py:243
  129.9 14.3 %all-to-all-start.2 = ((f32[32,8,128]{2,1,0:T(8,128)}), f32[32,8,128]{2,1,0:T(8,128)S(1)}, u32[]{:S(2)}, u32[]{:S(2)}) async-start(f32[32,8,128]{2,1,0:T(8,128)} %broadcast_in_dim.15), calls=%async_computation.2 | async-start | bytes 262144 | tf_op jit(solution)/shard_map/all_to_all | solution.py:29
  137.5 104.4 %all-gather.5.cloned.1.call-start = ((), (), s32[]{:S(2)}) async-start(), calls=%async_computation.7 | async-start | bytes 3342336 | tf_op jit(solution)/shard_map/all_gather | solution.py:287
  145.9 34.4 %all-to-all-start.3 = ((bf16[16,80,128]{2,1,0:T(8,128)(2,1)}), bf16[16,80,128]{2,1,0:T(8,128)(2,1)S(1)}, u32[]{:S(2)}, u32[]{:S(2)}) async-start(bf16[16,80,128]{2,1,0:T(8,128)(2,1)} %bitcast.17), calls=%async_computation.3 | async-start | bytes 655360 | tf_op jit(solution)/shard_map/all_to_all | solution.py:289
  180.2 14.9 %all-to-all-start.4 = ((bf16[32,128,64]{1,2,0:T(8,128)(2,1)}), bf16[32,128,64]{1,2,0:T(8,128)(2,1)S(1)}, u32[]{:S(2)}, u32[]{:S(2)}) async-start(bf16[32,128,64]{1,2,0:T(8,128)(2,1)} %bitcast.19), calls=%async_computation.4 | async-start | bytes 1048576 | tf_op jit(solution)/shard_map/all_to_all | solution.py:296
  195.8 32.6 %all-to-all-start.5 = ((bf16[16,96,128]{2,1,0:T(8,128)(2,1)}), bf16[16,96,128]{2,1,0:T(8,128)(2,1)S(1)}, u32[]{:S(2)}, u32[]{:S(2)}) async-start(bf16[16,96,128]{2,1,0:T(8,128)(2,1)} %shard_map.90), calls=%async_computation.5 | async-start | bytes 786432 | tf_op jit(solution)/shard_map/all_to_all | solution.py:299
  241.9 1.9 copy-start.1
Sparse Core Ops, SparseCore 0:
  10.1 113.4 all-gather.2
  146.0 95.9 all-gather.4

commit v4 on v3

--- a/solution.py
+++ b/solution.py
@@ -113,19 +113,18 @@
     )(every, student, teacher, target, into_margin, into_weight)
 
 
-def head_kernel(core_ref, objective_ref, own_ref, other_ref, grad_ref, out_ref, wide_ref):
+def head_kernel(core_ref, objective_ref, own_ref, other_ref, grad_ref, out_ref, tall_ref):
     f32, bf16 = jnp.float32, jnp.bfloat16
     groups, chunk, rows = grad_ref.shape
 
     @pl.when(pl.program_id(0) == 0)
     def _():
         for z in range(groups):
-            wide_ref[:, z * rows : (z + 1) * rows] = grad_ref[z]
-
-    nt = (((1,), (1,)), ((), ()))
-    wide = wide_ref[...]
-    own = lax.dot_general(wide, own_ref[...], nt, preferred_element_type=f32)
-    other = lax.dot_general(wide, other_ref[...], nt, preferred_element_type=f32)
+            tall_ref[z * rows : (z + 1) * rows] = jnp.transpose(grad_ref[z].astype(f32)).astype(bf16)
+
+    grad = tall_ref[...]
+    own = jnp.transpose(jnp.dot(own_ref[...], grad, preferred_element_type=f32))
+    other = jnp.transpose(jnp.dot(other_ref[...], grad, preferred_element_type=f32))
     is_first = core_ref[0] == 0
     first = jnp.where(is_first, own, other)
     second = jnp.where(is_first, other, own)
@@ -166,7 +165,7 @@
             pl.BlockSpec((groups, chunk, rows), lambda i: (0, 0, 0)),
         ],
         out_specs=pl.BlockSpec((per, chunk + extra, lanes), lambda i: (i, 0, 0)),
-        scratch_shapes=[pltpu.VMEM((chunk, all_rows), jnp.bfloat16)],
+        scratch_shapes=[pltpu.VMEM((all_rows, chunk), jnp.bfloat16)],
         compiler_params=pltpu.CompilerParams(vmem_limit_bytes=32 * 1024 * 1024),
         cost_estimate=pl.CostEstimate(
             flops=4 * tall * all_rows * chunk,
@@ -222,7 +221,7 @@
             pl.BlockSpec(memory_space=pltpu.SMEM),
         ),
         scratch_shapes=[pltpu.VMEM((count * chunk, feats), jnp.float32)],
-        compiler_params=pltpu.CompilerParams(vmem_limit_bytes=32 * 1024 * 1024),
+        compiler_params=pltpu.CompilerParams(vmem_limit_bytes=56 * 1024 * 1024),
     )(hidden_slab, gathered, parts)
 
 
@@ -279,7 +278,7 @@
         ]
     )
     every = to_all(stats, "vocab").reshape(n_vocab, 8, rows)
-    split = 3 * width // 8
+    split = width // 4
     extra = 16
     logit_grad, gathered, chunks, objective = make_grad(
         every, student, teacher_logits, (target_ids - offset)[:, None], into_margin, into_weight, split

time: 256 us -> 252 us (0.984)
  the two profiles are of different devices: /device:TPU:2 before, /device:TPU:32 now
where the time goes in v4:
time: 252 us; the launch traced here: 251 us
  blocking collectives  89.9 us (36%)
  waiting for transfers between devices  74.8 us (30%)
  starting transfers between devices  31.7 us (13%)
  Pallas kernels  18.7 us (7%)
  between operations  16 us (6%)
  matrix products  11.1 us (4%)
  other arithmetic  5.23 us (2%)
  local copies, waits for them, and re-layouts  3.9 us (2%)
    all_to_all x2, blocking collectives, to_all(): lax.all_to_all(copies, axis, 0, 0, axis_index_groups=groups, tiled=True)  89.9 us
    all_to_all x1, waiting for transfers between devices, on_device(): parts = lax.all_to_all(partial, 'dp', 0, 0, tiled=True)  26.7 us
    all_to_all x1, waiting for transfers between devices, on_device(): chunks = lax.all_to_all(chunks, 'dp', 0, 0, tiled=True)  19.4 us
    all_to_all x1, starting transfers between devices, on_device(): chunks = lax.all_to_all(chunks, 'dp', 0, 0, tiled=True)  11.1 us
    all_to_all x1, waiting for transfers between devices, to_all(): lax.all_to_all(copies, axis, 0, 0, axis_index_groups=groups, tiled=True)  7.48 us
    all_to_all x1, starting transfers between devices, on_device(): parts = lax.all_to_all(partial, 'dp', 0, 0, tiled=True)  7.4 us
    pallas_call x1, Pallas kernels, head_partial(): pl.pallas_call(head_kernel, out_shape=jax.ShapeDtypeStruct((blocks, chunk...  7.39 us
    all_to_all x1, starting transfers between devices, to_all(): lax.all_to_all(copies, axis, 0, 0, axis_index_groups=groups, tiled=True)  7.33 us
  transfers between devices with their start and end apart: 7, of which 7 were waited for; matrix products, arithmetic and copies ran while one was open for 6% of the time, Pallas kernels for 5%

profile of v4, /device:TPU:32, one launch (start us, length us, event | category | flops | bytes accessed | tf_op | source)
XLA Modules:
  0.0 251.2 jit_solution(11328837110331798595)
XLA Ops:
  8.7 33.4 %all_to_all.30 = bf16[16,64,128]{2,1,0:T(8,128)(2,1)S(1)} all-to-all(bf16[16,64,128]{2,1,0:T(8,128)(2,1)S(1)} %broadcast_in_dim.12), channel_id=1, replica_groups=mesh['vocab'=32,'dp'=16] {'dp'}, dimensions={0} | all-to-all | bytes 524288 | tf_op jit(solution)/shard_map/all_to_all | solution.py:29
  42.1 1.1 broadcast_in_dim.13
  43.2 56.4 %all_to_all.31.in_ref = bf16[16,16,64,128]{3,2,1,0:T(8,128)(2,1)S(1)} all-to-all(bf16[16,16,64,128]{3,2,1,0:T(8,128)(2,1)S(1)} %broadcast_in_dim.13), channel_id=1, replica_groups={{0,32,64,96,128,160,192,224,256,288,320,352,384,416,448,480},{16,48,80,..., dimensions={0} | all-to-all | bytes 8388608 | tf_op jit(solution)/shard_map/all_to_all | solution.py:29
  99.6 6.2 %shard_map.88.own_ref = bf16[1024,2048]{1,0:T(8,128)(2,1)} custom-call(bf16[16,16,64,128]{3,2,1,0:T(8,128)(2,1)S(1)} %all_to_all.31.in_ref), custom_call_target="tpu_custom_call" | custom-call | bytes 8388608 | tf_op jit(solution)/shard_map/pallas_call | solution.py:40
  105.8 1.9 collective-permute-start
  108.4 6.8 %collective-permute-done.other_ref = bf16[1024,2048]{1,0:T(8,128)(2,1)} collective-permute-done((bf16[1024,2048]{1,0:T(8,128)(2,1)}, bf16[1024,2048]{1,0:T(8,128)(2,1)}, u32[]{:S(2)}, u32[]{:S(2)}) %collective-permute-start) | collective-permute-done | bytes 4194336 | tf_op jit(solution)/shard_map/ppermute | solution.py:242
  115.2 1.1 broadcast_select_fusion.1
  116.4 5.6 %all-gather.3.cloned.1.call-done = bf16[2048,2048]{1,0:T(8,128)(2,1)} async-done(((bf16[128,2048]{1,0:T(8,128)(2,1)}), bf16[2048,2048]{1,0:T(8,128)(2,1)}) %all-gather.3.cloned.1.call-update) | async-done | bytes 8388624 | tf_op jit(solution)/shard_map/all_gather | solution.py:238
  122.0 4.8 %fusion.10 = (f32[128]{0:T(128)S(1)}, f32[128,2048]{1,0:T(8,128)S(1)}) fusion(bf16[2048,128]{1,0:T(8,128)(2,1)S(1)} %bitcast.35, bf16[2048,2048]{1,0:T(8,128)(2,1)} %all-gather.3.cloned.1.call-done), kind=kOutput, calls=%fused_computation.32 | convolution fusion | flops 1074003840 | bytes 9961984 | tf_op jit(solution)/shard_map/dot_general | solution.py:259
  128.3 7.3 %all-to-all-start.2 = ((f32[32,8,128]{2,1,0:T(8,128)}), f32[32,8,128]{2,1,0:T(8,128)S(1)}, u32[]{:S(2)}, u32[]{:S(2)}) async-start(f32[32,8,128]{2,1,0:T(8,128)} %broadcast_in_dim.15), calls=%async_computation.2 | async-start | bytes 262144 | tf_op jit(solution)/shard_map/all_to_all | solution.py:29
  136.0 7.5 %all-to-all-done.2.every_ref = f32[32,8,128]{2,1,0:T(8,128)S(1)} async-done(((f32[32,8,128]{2,1,0:T(8,128)}), f32[32,8,128]{2,1,0:T(8,128)S(1)}, u32[]{:S(2)}, u32[]{:S(2)}) %all-to-all-start.2) | async-done | bytes 131104 | tf_op jit(solution)/shard_map/all_to_all | solution.py:29
  143.5 1.7 shard_map.89
  145.2 11.1 %all-to-all-start.3 = ((bf16[16,96,128]{2,1,0:T(8,128)(2,1)}), bf16[16,96,128]{2,1,0:T(8,128)(2,1)S(1)}, u32[]{:S(2)}, u32[]{:S(2)}) async-start(bf16[16,96,128]{2,1,0:T(8,128)(2,1)} %bitcast.17), calls=%async_computation.3 | async-start | bytes 786432 | tf_op jit(solution)/shard_map/all_to_all | solution.py:288
  156.3 6.3 %convolution_convert_fusion = bf16[128,2048]{1,0:T(8,128)(2,1)S(1)} fusion(bf16[128,2048]{1,0:T(8,128)(2,1)S(1)} %get-tuple-element.15, bf16[2048,2048]{1,0:T(8,128)(2,1)} %all-gather.3.cloned.1.call-done), kind=kOutput, calls=%fused_computation | convolution fusion | flops 1074003968 | bytes 9437184 | tf_op jit(solution)/shard_map/dot_general | solution.py:289
  162.6 1.0 copy.18
  163.6 19.4 %all-to-all-done.3.grad_ref = bf16[16,96,128]{2,1,0:T(8,128)(2,1)S(1)} async-done(((bf16[16,96,128]{2,1,0:T(8,128)(2,1)}), bf16[16,96,128]{2,1,0:T(8,128)(2,1)S(1)}, u32[]{:S(2)}, u32[]{:S(2)}) %all-to-all-start.3) | async-done | bytes 393248 | tf_op jit(solution)/shard_map/all_to_all | solution.py:288
  183.0 3.9 %all-to-all-start.4 = ((bf16[32,128,64]{1,2,0:T(8,128)(2,1)}), bf16[32,128,64]{1,2,0:T(8,128)(2,1)S(1)}, u32[]{:S(2)}, u32[]{:S(2)}) async-start(bf16[32,128,64]{1,2,0:T(8,128)(2,1)} %bitcast.19), calls=%async_computation.4 | async-start | bytes 1048576 | tf_op jit(solution)/shard_map/all_to_all | solution.py:295
  186.9 7.4 %shard_map.90 = bf16[16,112,128]{2,1,0:T(8,128)(2,1)} custom-call(s32[1]{0:T(128)} %bitcast.core_ref, f32[1]{0:T(128)} %get-tuple-element.13.objective_ref, bf16[1024,2048]{1,0:T(8,128)(2,1)} %shard_map.88.own_ref, bf16[1024,2048]{1,0:T(8,128)(2,1)} %collective-permute-done.other_ref, bf16[16,96,128]{2,1,0:T(8,128)(2,1)S(1)} %all-to-all-done.3.grad_ref), custom_call_target="tpu_custom_call" | custom-call | flops 805306368 | bytes 9175040 | tf_op jit(solution)/shard_map/pallas_call | solution.py:156
  194.3 3.8 %all-to-all-done.4 = bf16[32,128,64]{1,2,0:T(8,128)(2,1)S(1)} async-done(((bf16[32,128,64]{1,2,0:T(8,128)(2,1)}), bf16[32,128,64]{1,2,0:T(8,128)(2,1)S(1)}, u32[]{:S(2)}, u32[]{:S(2)}) %all-to-all-start.4) | async-done | bytes 524320 | tf_op jit(solution)/shard_map/all_to_all | solution.py:295
  198.8 7.4 %all-to-all-start.5 = ((bf16[16,112,128]{2,1,0:T(8,128)(2,1)}), bf16[16,112,128]{2,1,0:T(8,128)(2,1)S(1)}, u32[]{:S(2)}, u32[]{:S(2)}) async-start(bf16[16,112,128]{2,1,0:T(8,128)(2,1)} %shard_map.90), calls=%async_computation.5 | async-start | bytes 917504 | tf_op jit(solution)/shard_map/all_to_all | solution.py:298
  206.2 1.1 select_bitcast_fusion.1
  208.2 26.7 %all-to-all-done.5.parts_ref = bf16[16,112,128]{2,1,0:T(8,128)(2,1)S(1)} async-done(((bf16[16,112,128]{2,1,0:T(8,128)(2,1)}), bf16[16,112,128]{2,1,0:T(8,128)(2,1)S(1)}, u32[]{:S(2)}, u32[]{:S(2)}) %all-to-all-start.5) | async-done | bytes 458784 | tf_op jit(solution)/shard_map/all_to_all | solution.py:298
  234.9 4.3 %all-gather.5.cloned.1.call-done.gathered_ref = bf16[2048,512]{1,0:T(8,128)(2,1)} async-done(((bf16[128,512]{1,0:T(8,128)(2,1)}), bf16[2048,512]{1,0:T(8,128)(2,1)}) %all-gather.5.cloned.1.call-update) | async-done | bytes 2097168 | tf_op jit(solution)/shard_map/all_gather | solution.py:286
  239.2 3.3 %shard_map.91 = (f32[128,2048]{1,0:T(8,128)}, f32[1]{0:T(128)}) custom-call(bf16[128,2048]{1,0:T(8,128)(2,1)} %bitcast.36, bf16[2048,512]{1,0:T(8,128)(2,1)} %all-gather.5.cloned.1.call-done.gathered_ref, bf16[16,112,128]{2,1,0:T(8,128)(2,1)} %copy-done.1), custom_call_target="tpu_custom_call" | custom-call | tf_op jit(solution)/shard_map/pallas_call | solution.py:207
  (35 shorter events, 5.6 us)
Async XLA Ops:
  7.2 114.8 %all-gather.3.cloned.1.call-start = ((), (), s32[]{:S(2)}) async-start(), calls=%async_computation.6 | async-start | bytes 8912896 | tf_op jit(solution)/shard_map/all_gather | solution.py:238
  99.6 8.2 %copy-start.4 = (s32[1,16]{1,0:T(1,128)S(1)}, s32[1,16]{1,0:T(1,128)}, u32[]{:S(2)}) copy-start(s32[1,16]{1,0:T(1,128)} %param.11) | copy-start | bytes 196
  99.6 8.5 %copy-start = (bf16[128,2048]{1,0:T(8,128)(2,1)S(1)}, bf16[128,2048]{1,0:T(8,128)(2,1)}, u32[]{:S(2)}) copy-start(bf16[128,2048]{1,0:T(8,128)(2,1)} %teacher_ref.1) | copy-start | bytes 1572868
  99.6 8.7 %copy-start.3 = (s32[128]{0:T(128)S(1)}, s32[128]{0:T(128)}, u32[]{:S(2)}) copy-start(s32[128]{0:T(128)} %param.9) | copy-start | bytes 1540
  99.6 8.7 %copy-start.2 = (s32[1,128]{1,0:T(1,128)S(1)}, s32[1,128]{1,0:T(1,128)}, u32[]{:S(2)}) copy-start(s32[1,128]{1,0:T(1,128)} %param.10) | copy-start | bytes 1540
  105.8 9.4 %collective-permute-start = (bf16[1024,2048]{1,0:T(8,128)(2,1)}, bf16[1024,2048]{1,0:T(8,128)(2,1)}, u32[]{:S(2)}, u32[]{:S(2)}) collective-permute-start(bf16[1024,2048]{1,0:T(8,128)(2,1)} %shard_map.88.own_ref), channel_id=1, source_target_pairs={{0,16},{16,0},{32,48},{48,32},{64,80},{80,64},{96,112},{112,96},{1... | collective-permute-start | bytes 12582920 | tf_op jit(solution)/shard_map/ppermute | solution.py:242
  128.3 15.2 %all-to-all-start.2 = ((f32[32,8,128]{2,1,0:T(8,128)}), f32[32,8,128]{2,1,0:T(8,128)S(1)}, u32[]{:S(2)}, u32[]{:S(2)}) async-start(f32[32,8,128]{2,1,0:T(8,128)} %broadcast_in_dim.15), calls=%async_computation.2 | async-start | bytes 262144 | tf_op jit(solution)/shard_map/all_to_all | solution.py:29
  135.6 103.6 %all-gather.5.cloned.1.call-start = ((), (), s32[]{:S(2)}) async-start(), calls=%async_computation.7 | async-start | bytes 2228224 | tf_op jit(solution)/shard_map/all_gather | solution.py:286
  145.2 37.8 %all-to-all-start.3 = ((bf16[16,96,128]{2,1,0:T(8,128)(2,1)}), bf16[16,96,128]{2,1,0:T(8,128)(2,1)S(1)}, u32[]{:S(2)}, u32[]{:S(2)}) async-start(bf16[16,96,128]{2,1,0:T(8,128)(2,1)} %bitcast.17), calls=%async_computation.3 | async-start | bytes 786432 | tf_op jit(solution)/shard_map/all_to_all | solution.py:288
  183.0 15.1 %all-to-all-start.4 = ((bf16[32,128,64]{1,2,0:T(8,128)(2,1)}), bf16[32,128,64]{1,2,0:T(8,128)(2,1)S(1)}, u32[]{:S(2)}, u32[]{:S(2)}) async-start(bf16[32,128,64]{1,2,0:T(8,128)(2,1)} %bitcast.19), calls=%async_computation.4 | async-start | bytes 1048576 | tf_op jit(solution)/shard_map/all_to_all | solution.py:295
  198.8 36.1 %all-to-all-start.5 = ((bf16[16,112,128]{2,1,0:T(8,128)(2,1)}), bf16[16,112,128]{2,1,0:T(8,128)(2,1)S(1)}, u32[]{:S(2)}, u32[]{:S(2)}) async-start(bf16[16,112,128]{2,1,0:T(8,128)(2,1)} %shard_map.90), calls=%async_computation.5 | async-start | bytes 917504 | tf_op jit(solution)/shard_map/all_to_all | solution.py:298
  234.9 4.3 %copy-start.1 = (bf16[16,112,128]{2,1,0:T(8,128)(2,1)}, bf16[16,112,128]{2,1,0:T(8,128)(2,1)S(1)}, u32[]{:S(2)}) copy-start(bf16[16,112,128]{2,1,0:T(8,128)(2,1)S(1)} %all-to-all-done.5.parts_ref) | copy-start | bytes 1376260
Sparse Core Ops, SparseCore 0:
  10.1 111.8 all-gather.2
  145.3 93.8 all-gather.4

commit v5 on v2

--- a/solution.py
+++ b/solution.py
@@ -1,3 +1,5 @@
+import math
+
 import jax
 import jax.numpy as jnp
 from jax import lax
@@ -9,29 +11,114 @@
 dpo_gamma = 4.0
 
 
-def pair_weights(log_ratio, segments, ordering):
-    seq_count = ordering.shape[0]
-    labels = lax.broadcasted_iota(jnp.int32, (1, seq_count), 1)
-    seq_hot = (segments[:, None] == labels).astype(jnp.float32)
-    seq_ratio = jnp.sum(seq_hot * log_ratio[:, None], axis=0)
-    chosen = ordering[0::2]
-    rejected = ordering[1::2]
-    chosen_hot = (chosen[:, None] == labels).astype(jnp.float32)
-    rejected_hot = (rejected[:, None] == labels).astype(jnp.float32)
-    margin = dpo_beta * (
-        jnp.sum(chosen_hot * seq_ratio[None, :], axis=1)
-        - jnp.sum(rejected_hot * seq_ratio[None, :], axis=1)
-    )
-    strength = dpo_gamma * dpo_beta * jax.nn.sigmoid(-margin)
-    coeffs = jnp.sum((rejected_hot - chosen_hot) * strength[:, None], axis=0)
-    row_weight = jnp.sum(seq_hot * coeffs[None, :], axis=1)
-    return (row_weight, jnp.sum(jax.nn.softplus(-margin)))
+def pair_signs(segments, ordering):
+    count = ordering.shape[0]
+    labels = lax.broadcasted_iota(jnp.int32, (count, 1), 0)
+    seq_hot = (segments[None, :] == labels).astype(jnp.float32)
+    chosen = (labels == ordering[None, 0::2]).astype(jnp.float32)
+    rejected = (labels == ordering[None, 1::2]).astype(jnp.float32)
+    side = chosen - rejected
+    pair = chosen + rejected
+    margin_sign = jnp.sum(pair[:, None, :] * side[None, :, :], axis=2)
+    into_margin = jnp.sum(margin_sign[:, :, None] * seq_hot[None, :, :], axis=1)
+    into_weight = jnp.sum(side, axis=1)[:, None] * seq_hot
+    return into_margin, into_weight
 
 
 def to_all(block, axis, groups=None):
     count = lax.axis_size(axis) if groups is None else len(groups[0])
     copies = jnp.broadcast_to(block[None], (count,) + block.shape)
     return lax.all_to_all(copies, axis, 0, 0, axis_index_groups=groups, tiled=True)
+
+
+def ring_sum(terms, place, around):
+    count = terms.shape[0]
+    turned = lax.dynamic_slice_in_dim(jnp.concatenate([terms, terms]), place, count, 0)
+    rounded = turned.astype(jnp.bfloat16)
+    arrived = [lax.ppermute(rounded[d], "vocab", around[d]) for d in range(1, count)]
+    return turned[0] + sum(term.astype(jnp.float32) for term in arrived)
+
+
+def relayout_kernel(in_ref, out_ref):
+    groups, _, rows = in_ref.shape[1:]
+    for j in range(groups):
+        out_ref[:, j * rows : (j + 1) * rows] = in_ref[0, j]
+
+
+def relayout(by_pair):
+    pairs, groups, feats, rows = by_pair.shape
+    return pl.pallas_call(
+        relayout_kernel,
+        out_shape=jax.ShapeDtypeStruct((pairs * feats, groups * rows), by_pair.dtype),
+        grid=(pairs,),
+        in_specs=[pl.BlockSpec((1, groups, feats, rows), lambda i: (i, 0, 0, 0))],
+        out_specs=pl.BlockSpec((feats, groups * rows), lambda i: (i, 0)),
+        compiler_params=pltpu.CompilerParams(vmem_limit_bytes=16 * 1024 * 1024),
+        cost_estimate=pl.CostEstimate(flops=0, bytes_accessed=4 * by_pair.size, transcendentals=0),
+    )(by_pair)
+
+
+def grad_kernel(
+    every_ref, student_ref, teacher_ref, target_ref, margin_ref, weight_ref,
+    grad_ref, chunks_ref, objective_ref,
+):
+    f32, bf16 = jnp.float32, jnp.bfloat16
+    maxes_s, maxes_t = every_ref[:, 0, :], every_ref[:, 1, :]
+    max_s = jnp.max(maxes_s, axis=0, keepdims=True)
+    max_t = jnp.max(maxes_t, axis=0, keepdims=True)
+    scale_s = jnp.exp(maxes_s - max_s)
+    scale_t = jnp.exp(maxes_t - max_t)
+    sum_s = jnp.sum(every_ref[:, 2, :] * scale_s, axis=0, keepdims=True)
+    sum_t = jnp.sum(every_ref[:, 3, :] * scale_t, axis=0, keepdims=True)
+    cross = jnp.sum(every_ref[:, 4, :] * scale_t, axis=0, keepdims=True)
+    target_s = jnp.sum(every_ref[:, 5, :], axis=0, keepdims=True)
+    target_t = jnp.sum(every_ref[:, 6, :], axis=0, keepdims=True)
+    lse_s = max_s + jnp.log(sum_s)
+    lse_t = max_t + jnp.log(sum_t)
+    kl = cross / sum_t - lse_t + lse_s
+    log_ratio = target_s - lse_s - (target_t - lse_t)
+    margin = dpo_beta * jnp.sum(margin_ref[...] * log_ratio, axis=1, keepdims=True)
+    strength = dpo_gamma * dpo_beta / (1.0 + jnp.exp(margin))
+    weight = -jnp.sum(weight_ref[...] * strength, axis=0, keepdims=True)
+    dpo = jnp.maximum(-margin, 0.0) + jnp.log(1.0 + jnp.exp(-jnp.abs(margin)))
+    objective = jnp.sum(kl) + 0.5 * dpo_gamma * jnp.sum(dpo)
+    objective_ref[0] = objective
+    lines = jnp.concatenate(
+        [max_s, 1.0 / sum_s, max_t, 1.0 / sum_t, weight, weight, weight, weight], axis=0
+    )
+    columns = jnp.transpose(lines)
+    max_s, inv_s = columns[:, 0:1], columns[:, 1:2]
+    max_t, inv_t, weight = columns[:, 2:3], columns[:, 3:4], columns[:, 4:5]
+    target = target_ref[...]
+    rows, width = student_ref.shape
+    chunk = chunks_ref.shape[2]
+    step = 256
+    for low in range(0, width, step):
+        prob_s = jnp.exp(student_ref[:, low : low + step] - max_s) * inv_s
+        prob_t = jnp.exp(teacher_ref[:, low : low + step].astype(f32) - max_t) * inv_t
+        column = lax.broadcasted_iota(jnp.int32, (rows, step), 1) + low
+        hot = jnp.where(column == target, 1.0, 0.0)
+        grad = prob_s - prob_t + weight * (hot - prob_s)
+        rounded = grad.astype(bf16)
+        grad_ref[:, low : low + step] = rounded
+        for j in range(0, step, chunk):
+            chunks_ref[(low + j) // chunk] = rounded[:, j : j + chunk]
+
+
+def make_grad(every, student, teacher, target, into_margin, into_weight, chunks):
+    rows, width = student.shape
+    f32, bf16 = jnp.float32, jnp.bfloat16
+    vmem = pl.BlockSpec(memory_space=pltpu.VMEM)
+    return pl.pallas_call(
+        grad_kernel,
+        out_shape=(
+            jax.ShapeDtypeStruct((rows, width), bf16),
+            jax.ShapeDtypeStruct((chunks, rows, width // chunks), bf16),
+            jax.ShapeDtypeStruct((1,), f32),
+        ),
+        out_specs=(vmem, vmem, pl.BlockSpec(memory_space=pltpu.SMEM)),
+        compiler_params=pltpu.CompilerParams(vmem_limit_bytes=32 * 1024 * 1024),
+    )(every, student, teacher, target, into_margin, into_weight)
 
 
 def head_kernel(core_ref, objective_ref, own_ref, other_ref, grad_ref, out_ref):
@@ -125,16 +212,31 @@
     core = lax.axis_index("vocab") % 2
     same_core = [[2 * j + c for j in range(pairs)] for c in range(2)]
     swap = [(i, i ^ 1) for i in range(n_vocab)]
+    side = math.isqrt(pairs)
+    index = lax.axis_index("vocab")
+    place_x, place_y = index // (2 * side), index // 2 % side
+
+    def around(i, along_x, distance):
+        x, y, c = i // (2 * side), i // 2 % side, i % 2
+        x, y = ((x + distance) % side, y) if along_x else (x, (y + distance) % side)
+        return (x * side + y) * 2 + c
+
+    around_x = [[(i, around(i, True, d)) for i in range(n_vocab)] for d in range(side)]
+    around_y = [[(i, around(i, False, d)) for i in range(n_vocab)] for d in range(side)]
     weight_full = lax.all_gather(head_weight, "dp", axis=0, tiled=True)
     by_group = to_all(hidden.T, "dp").reshape(n_dp, feats, rows)
     by_pair = to_all(by_group, "vocab", same_core).reshape(pairs, n_dp, feats, rows)
-    mine = lax.dynamic_index_in_dim(by_pair, lax.axis_index("dp"), 1, keepdims=False)
-    theirs = lax.ppermute(mine, "vocab", swap)
-    rows_t = jnp.stack(
-        [jnp.where(core == 0, mine, theirs), jnp.where(core == 0, theirs, mine)], axis=1
-    ).reshape(n_vocab * feats, rows)
-    own_t = by_pair.swapaxes(1, 2).reshape(pairs * feats, n_dp * rows)
+    own_t = relayout(by_pair)
     other_t = lax.ppermute(own_t, "vocab", swap)
+    place = lax.axis_index("dp")
+
+    def by_core(own, other, axis):
+        return jnp.stack([jnp.where(core == 0, own, other), jnp.where(core == 0, other, own)], axis=axis)
+
+    mine = lax.dynamic_slice_in_dim(own_t, place * rows, rows, 1).reshape(pairs, feats, rows)
+    theirs = lax.dynamic_slice_in_dim(other_t, place * rows, rows, 1).reshape(pairs, feats, rows)
+    rows_t = by_core(mine, theirs, 1).reshape(n_vocab * feats, rows)
+    into_margin, into_weight = pair_signs(segment_ids[0], pair_order[0])
     tn = (((0,), (0,)), ((), ()))
     nt = (((1,), (1,)), ((), ()))
     student = lax.dot_general(rows_t, weight_full, tn, preferred_element_type=f32)
@@ -159,49 +261,29 @@
         ]
     )
     every = to_all(stats, "vocab").reshape(n_vocab, 8, rows)
-    max_student = jnp.max(every[:, 0], axis=0)
-    max_teacher = jnp.max(every[:, 1], axis=0)
-    scale_s = jnp.exp(every[:, 0] - max_student[None])
-    scale_t = jnp.exp(every[:, 1] - max_teacher[None])
-    sum_student = jnp.sum(every[:, 2] * scale_s, axis=0)
-    sum_teacher = jnp.sum(every[:, 3] * scale_t, axis=0)
-    cross = jnp.sum(every[:, 4] * scale_t, axis=0)
-    target_student = jnp.sum(every[:, 5], axis=0)
-    target_teacher = jnp.sum(every[:, 6], axis=0)
-    lse_student = max_student + jnp.log(sum_student)
-    lse_teacher = max_teacher + jnp.log(sum_teacher)
-    kl_rows = cross / sum_teacher - lse_teacher + lse_student
-    log_ratio = target_student - lse_student - (target_teacher - lse_teacher)
-    row_weight, dpo_sum = pair_weights(log_ratio, segment_ids[0], pair_order[0])
-    group_objective = jnp.sum(kl_rows) + dpo_gamma * dpo_sum
-    exp_student = jnp.exp(student - max_student[:, None])
-    exp_teacher = jnp.exp(teacher - max_teacher[:, None])
-    prob_student = exp_student / sum_student[:, None]
-    prob_teacher = exp_teacher / sum_teacher[:, None]
-    logit_grad = (
-        prob_student
-        - prob_teacher
-        + row_weight[:, None] * (is_target.astype(f32) - prob_student)
-    ).astype(bf16)
-    chunk = width // n_dp
-    chunks = logit_grad.reshape(rows, n_dp, chunk).swapaxes(0, 1)
+    logit_grad, chunks, objective = make_grad(
+        every, student, teacher_logits, (target_ids - offset)[:, None], into_margin, into_weight, n_dp
+    )
     chunks = lax.all_to_all(chunks, "dp", 0, 0, tiled=True)
-    hidden_term = lax.dot_general(logit_grad, weight_full, nt, preferred_element_type=f32)
-    terms = hidden_term.astype(bf16).reshape(rows, n_vocab, feats).swapaxes(0, 1)
-    chunks, terms = lax.optimization_barrier((chunks, terms))
+    term = lax.dot_general(weight_full, logit_grad, nt, preferred_element_type=f32).astype(bf16)
+    term = term.reshape(side * side, 2, feats, rows)
+    kept = lax.dynamic_index_in_dim(term, core, 1, keepdims=False)
+    sent = lax.dynamic_index_in_dim(term, 1 - core, 1, keepdims=False)
+    term = kept.astype(f32) + lax.ppermute(sent, "vocab", swap).astype(f32)
+    term = ring_sum(term.reshape(side, side, feats, rows), place_x, around_x)
+    chunks, term = lax.optimization_barrier((chunks, term))
     partial = head_partial(
         core.astype(jnp.int32).reshape(1),
-        group_objective.reshape(1),
+        objective,
         own_t,
         other_t,
-        chunks.reshape(n_dp * rows, chunk),
+        chunks.reshape(n_dp * rows, width // n_dp),
         pairs,
         16,
     )
-    terms = lax.all_to_all(terms, "vocab", 0, 0, tiled=True)
-    hidden_grad = jnp.sum(terms.astype(f32), axis=0).astype(bf16)
-    partial, hidden_grad = lax.optimization_barrier((partial, hidden_grad))
+    partial, term = lax.optimization_barrier((partial, term))
     parts = lax.all_to_all(partial, "dp", 0, 0, tiled=True)
+    hidden_grad = ring_sum(term, place_y, around_y).astype(bf16).T
     head_grad, total = unpack(parts, 2 * feats)
     loss_value = total[0] / (rows * n_dp)
     return (hidden_grad, head_grad, loss_value)

time: 263 us -> 241 us (0.916)
  the two profiles are of different devices: /device:TPU:1 before, /device:TPU:32 now
where the time goes in v5:
time: 241 us; the launch traced here: 240 us
  blocking collectives  90 us (37%)
  waiting for transfers between devices  52.3 us (22%)
  starting transfers between devices  48.3 us (20%)
  between operations  16.2 us (7%)
  Pallas kernels  15.7 us (7%)
  matrix products  11 us (5%)
  other arithmetic  3.45 us (1%)
  local copies, waits for them, and re-layouts  3.23 us (1%)
    all_to_all x2, blocking collectives, to_all(): lax.all_to_all(copies, axis, 0, 0, axis_index_groups=groups, tiled=True)  90 us
    ppermute x6, starting transfers between devices, ring_sum(): lax.ppermute(rounded[d], 'vocab', around[d])  18 us
    all_to_all x1, waiting for transfers between devices, on_device(): parts = lax.all_to_all(partial, 'dp', 0, 0, tiled=True)  15.4 us
    all_to_all x1, starting transfers between devices, on_device(): chunks = lax.all_to_all(chunks, 'dp', 0, 0, tiled=True)  11.1 us
    ppermute x6, waiting for transfers between devices, ring_sum(): lax.ppermute(rounded[d], 'vocab', around[d])  10.9 us
    all_to_all x1, starting transfers between devices, on_device(): parts = lax.all_to_all(partial, 'dp', 0, 0, tiled=True)  8.02 us
    all_to_all x1, waiting for transfers between devices, to_all(): lax.all_to_all(copies, axis, 0, 0, axis_index_groups=groups, tiled=True)  7.53 us
    all_to_all x1, starting transfers between devices, to_all(): lax.all_to_all(copies, axis, 0, 0, axis_index_groups=groups, tiled=True)  7.32 us
  transfers between devices with their start and end apart: 12, of which 8 were waited for; matrix products, arithmetic and copies ran while one was open for 5% of the time, Pallas kernels for 3%

profile of v5, /device:TPU:32, one launch (start us, length us, event | category | flops | bytes accessed | tf_op | source)
XLA Modules:
  0.0 240.1 jit_solution(8998868790009018438)
XLA Ops:
  8.7 33.4 %all_to_all.25 = bf16[16,64,128]{2,1,0:T(8,128)(2,1)S(1)} all-to-all(bf16[16,64,128]{2,1,0:T(8,128)(2,1)S(1)} %broadcast_in_dim.12), channel_id=1, replica_groups=mesh['vocab'=32,'dp'=16] {'dp'}, dimensions={0} | all-to-all | bytes 524288 | tf_op jit(solution)/shard_map/all_to_all | solution.py:31
  43.2 56.5 %all_to_all.26.in_ref = bf16[16,16,64,128]{3,2,1,0:T(8,128)(2,1)S(1)} all-to-all(bf16[16,16,64,128]{3,2,1,0:T(8,128)(2,1)S(1)} %broadcast_in_dim.13), channel_id=1, replica_groups={{0,32,64,96,128,160,192,224,256,288,320,352,384,416,448,480},{16,48,80,..., dimensions={0} | all-to-all | bytes 8388608 | tf_op jit(solution)/shard_map/all_to_all | solution.py:31
  99.8 6.2 %shard_map.88.own_ref = bf16[1024,2048]{1,0:T(8,128)(2,1)} custom-call(bf16[16,16,64,128]{3,2,1,0:T(8,128)(2,1)S(1)} %all_to_all.26.in_ref), custom_call_target="tpu_custom_call" | custom-call | bytes 8388608 | tf_op jit(solution)/shard_map/pallas_call | solution.py:50
  105.9 1.9 collective-permute-start
  108.5 6.8 %collective-permute-done.other_ref = bf16[1024,2048]{1,0:T(8,128)(2,1)} collective-permute-done((bf16[1024,2048]{1,0:T(8,128)(2,1)}, bf16[1024,2048]{1,0:T(8,128)(2,1)}, u32[]{:S(2)}, u32[]{:S(2)}) %collective-permute-start) | collective-permute-done | bytes 4194336 | tf_op jit(solution)/shard_map/ppermute | solution.py:230
  116.5 5.5 %all-gather.2.cloned.1.call-done = bf16[2048,2048]{1,0:T(8,128)(2,1)} async-done(((bf16[128,2048]{1,0:T(8,128)(2,1)}), bf16[2048,2048]{1,0:T(8,128)(2,1)}) %all-gather.2.cloned.1.call-update) | async-done | bytes 8388624 | tf_op jit(solution)/shard_map/all_gather | solution.py:226
  122.0 4.8 %fusion.21 = (f32[128]{0:T(128)S(1)}, f32[128,2048]{1,0:T(8,128)S(1)}) fusion(bf16[2048,128]{1,0:T(8,128)(2,1)S(1)} %bitcast.63, bf16[2048,2048]{1,0:T(8,128)(2,1)} %all-gather.2.cloned.1.call-done), kind=kOutput, calls=%fused_computation.52 | convolution fusion | flops 1074003840 | bytes 9961984 | tf_op jit(solution)/shard_map/dot_general | solution.py:242
  128.3 7.3 %all-to-all-start.2 = ((f32[32,8,128]{2,1,0:T(8,128)}), f32[32,8,128]{2,1,0:T(8,128)S(1)}, u32[]{:S(2)}, u32[]{:S(2)}) async-start(f32[32,8,128]{2,1,0:T(8,128)} %broadcast_in_dim.15), calls=%async_computation.2 | async-start | bytes 262144 | tf_op jit(solution)/shard_map/all_to_all | solution.py:31
  135.9 7.5 %all-to-all-done.2.every_ref = f32[32,8,128]{2,1,0:T(8,128)S(1)} async-done(((f32[32,8,128]{2,1,0:T(8,128)}), f32[32,8,128]{2,1,0:T(8,128)S(1)}, u32[]{:S(2)}, u32[]{:S(2)}) %all-to-all-start.2) | async-done | bytes 131104 | tf_op jit(solution)/shard_map/all_to_all | solution.py:31
  145.2 11.1 %all-to-all-start.3 = ((bf16[16,128,128]{2,1,0:T(8,128)(2,1)}), bf16[16,128,128]{2,1,0:T(8,128)(2,1)S(1)}, u32[]{:S(2)}, u32[]{:S(2)}) async-start(bf16[16,128,128]{2,1,0:T(8,128)(2,1)} %get-tuple-element.13), calls=%async_computation.3 | async-start | bytes 1048576 | tf_op jit(solution)/shard_map/all_to_all | solution.py:267
  156.3 6.3 %fusion = bf16[2048,128]{0,1:T(8,128)(2,1)S(1)} fusion(bf16[128,2048]{1,0:T(8,128)(2,1)S(1)} %get-tuple-element.14, bf16[2048,2048]{1,0:T(8,128)(2,1)} %all-gather.2.cloned.1.call-done), kind=kOutput, calls=%fused_computation.1 | convolution fusion | flops 1074003968 | bytes 9437184 | tf_op jit(solution)/shard_map/dot_general | solution.py:268
  162.8 1.9 collective-permute-start.1
  166.5 2.5 %collective-permute-start.2 = (bf16[4,64,128]{2,1,0:T(8,128)(2,1)S(1)}, bf16[4,64,128]{2,1,0:T(8,128)(2,1)S(1)}, u32[]{:S(2)}, u32[]{:S(2)}) collective-permute-start(bf16[4,64,128]{2,1,0:T(8,128)(2,1)S(1)} %get-tuple-element.32), channel_id=1, source_target_pairs={{0,128},{16,144},{32,160},{48,176},{64,192},{80,208},{96,224},{112... | collective-permute-start | bytes 196616 | tf_op jit(solution)/shard_map/ppermute | solution.py:38
  169.0 4.6 %collective-permute-start.4 = (bf16[4,64,128]{2,1,0:T(8,128)(2,1)S(1)}, bf16[4,64,128]{2,1,0:T(8,128)(2,1)S(1)}, u32[]{:S(2)}, u32[]{:S(2)}) collective-permute-start(bf16[4,64,128]{2,1,0:T(8,128)(2,1)S(1)} %get-tuple-element.33), channel_id=1, source_target_pairs={{0,384},{16,400},{32,416},{48,432},{64,448},{80,464},{96,480},{112... | collective-permute-start | bytes 196616 | tf_op jit(solution)/shard_map/ppermute | solution.py:38
  173.5 2.0 collective-permute-start.3
  175.5 5.7 %collective-permute-done.3 = bf16[4,64,128]{2,1,0:T(8,128)(2,1)S(1)} collective-permute-done((bf16[4,64,128]{2,1,0:T(8,128)(2,1)S(1)}, bf16[4,64,128]{2,1,0:T(8,128)(2,1)S(1)}, u32[]{:S(2)}, u32[]{:S(2)}) %collective-permute-start.3) | collective-permute-done | bytes 65568 | tf_op jit(solution)/shard_map/ppermute | solution.py:38
  181.2 4.0 %all-to-all-done.3 = bf16[16,128,128]{2,1,0:T(8,128)(2,1)S(1)} async-done(((bf16[16,128,128]{2,1,0:T(8,128)(2,1)}), bf16[16,128,128]{2,1,0:T(8,128)(2,1)S(1)}, u32[]{:S(2)}, u32[]{:S(2)}) %all-to-all-start.3) | async-done | bytes 524320 | tf_op jit(solution)/shard_map/all_to_all | solution.py:267
  185.3 6.8 %shard_map.90 = bf16[16,144,128]{2,1,0:T(8,128)(2,1)} custom-call(s32[1]{0:T(128)} %bitcast.core_ref, f32[1]{0:T(128)} %get-tuple-element.12.objective_ref, bf16[1024,2048]{1,0:T(8,128)(2,1)} %shard_map.88.own_ref, bf16[1024,2048]{1,0:T(8,128)(2,1)} %collective-permute-done.other_ref, bf16[2048,128]{1,0:T(8,128)(2,1)S(1)} %bitcast.62), custom_call_target="tpu_custom_call" | custom-call | flops 1073741824 | bytes 9437184 | tf_op jit(solution)/shard_map/pallas_call | solution.py:161
  192.1 8.0 %all-to-all-start.4 = ((bf16[16,144,128]{2,1,0:T(8,128)(2,1)}), bf16[16,144,128]{2,1,0:T(8,128)(2,1)S(1)}, u32[]{:S(2)}, u32[]{:S(2)}) async-start(bf16[16,144,128]{2,1,0:T(8,128)(2,1)} %shard_map.90), calls=%async_computation.4 | async-start | bytes 1179648 | tf_op jit(solution)/shard_map/all_to_all | solution.py:285
  200.1 2.4 %collective-permute-start.5 = (bf16[64,128]{1,0:T(8,128)(2,1)S(1)}, bf16[64,128]{1,0:T(8,128)(2,1)S(1)}, u32[]{:S(2)}, u32[]{:S(2)}) collective-permute-start(bf16[64,128]{1,0:T(8,128)(2,1)S(1)} %get-tuple-element.35), channel_id=1, source_target_pairs={{0,32},{16,48},{32,64},{48,80},{64,96},{80,112},{96,0},{112,16},{1... | collective-permute-start | bytes 49160 | tf_op jit(solution)/shard_map/ppermute | solution.py:38
  202.6 4.6 %collective-permute-start.7 = (bf16[64,128]{1,0:T(8,128)(2,1)S(1)}, bf16[64,128]{1,0:T(8,128)(2,1)S(1)}, u32[]{:S(2)}, u32[]{:S(2)}) collective-permute-start(bf16[64,128]{1,0:T(8,128)(2,1)S(1)} %get-tuple-element.36), channel_id=1, source_target_pairs={{0,96},{16,112},{32,0},{48,16},{64,32},{80,48},{96,64},{112,80},{1... | collective-permute-start | bytes 49160 | tf_op jit(solution)/shard_map/ppermute | solution.py:38
  207.2 1.9 collective-permute-start.6
  209.1 5.2 %collective-permute-done.6 = bf16[64,128]{1,0:T(8,128)(2,1)S(1)} collective-permute-done((bf16[64,128]{1,0:T(8,128)(2,1)S(1)}, bf16[64,128]{1,0:T(8,128)(2,1)S(1)}, u32[]{:S(2)}, u32[]{:S(2)}) %collective-permute-start.6) | collective-permute-done | bytes 16416 | tf_op jit(solution)/shard_map/ppermute | solution.py:38
  214.9 15.4 %all-to-all-done.4.parts_ref = bf16[16,144,128]{2,1,0:T(8,128)(2,1)S(1)} async-done(((bf16[16,144,128]{2,1,0:T(8,128)(2,1)}), bf16[16,144,128]{2,1,0:T(8,128)(2,1)S(1)}, u32[]{:S(2)}, u32[]{:S(2)}) %all-to-all-start.4) | async-done | bytes 589856 | tf_op jit(solution)/shard_map/all_to_all | solution.py:285
  (47 shorter events, 11.7 us)
Async XLA Ops:
  7.2 114.8 %all-gather.2.cloned.1.call-start = ((), (), s32[]{:S(2)}) async-start(), calls=%async_computation.5 | async-start | bytes 8912896 | tf_op jit(solution)/shard_map/all_gather | solution.py:226
  43.2 64.7 %copy-start.3 = (s32[1,16]{1,0:T(1,128)S(1)}, s32[1,16]{1,0:T(1,128)}, u32[]{:S(2)}) copy-start(s32[1,16]{1,0:T(1,128)} %param.11) | copy-start | bytes 196
  43.2 65.0 %copy-start = (bf16[128,2048]{1,0:T(8,128)(2,1)S(1)}, bf16[128,2048]{1,0:T(8,128)(2,1)}, u32[]{:S(2)}) copy-start(bf16[128,2048]{1,0:T(8,128)(2,1)} %teacher_ref.1) | copy-start | bytes 1572868
  43.2 65.2 %copy-start.2 = (s32[128]{0:T(128)S(1)}, s32[128]{0:T(128)}, u32[]{:S(2)}) copy-start(s32[128]{0:T(128)} %param.9) | copy-start | bytes 1540
  43.2 65.2 %copy-start.1 = (s32[1,128]{1,0:T(1,128)S(1)}, s32[1,128]{1,0:T(1,128)}, u32[]{:S(2)}) copy-start(s32[1,128]{1,0:T(1,128)} %param.10) | copy-start | bytes 1540
  105.9 9.4 %collective-permute-start = (bf16[1024,2048]{1,0:T(8,128)(2,1)}, bf16[1024,2048]{1,0:T(8,128)(2,1)}, u32[]{:S(2)}, u32[]{:S(2)}) collective-permute-start(bf16[1024,2048]{1,0:T(8,128)(2,1)} %shard_map.88.own_ref), channel_id=1, source_target_pairs={{0,16},{16,0},{32,48},{48,32},{64,80},{80,64},{96,112},{112,96},{1... | collective-permute-start | bytes 12582920 | tf_op jit(solution)/shard_map/ppermute | solution.py:230
  128.3 15.2 %all-to-all-start.2 = ((f32[32,8,128]{2,1,0:T(8,128)}), f32[32,8,128]{2,1,0:T(8,128)S(1)}, u32[]{:S(2)}, u32[]{:S(2)}) async-start(f32[32,8,128]{2,1,0:T(8,128)} %broadcast_in_dim.15), calls=%async_computation.2 | async-start | bytes 262144 | tf_op jit(solution)/shard_map/all_to_all | solution.py:31
  145.2 40.1 %all-to-all-start.3 = ((bf16[16,128,128]{2,1,0:T(8,128)(2,1)}), bf16[16,128,128]{2,1,0:T(8,128)(2,1)S(1)}, u32[]{:S(2)}, u32[]{:S(2)}) async-start(bf16[16,128,128]{2,1,0:T(8,128)(2,1)} %get-tuple-element.13), calls=%async_computation.3 | async-start | bytes 1048576 | tf_op jit(solution)/shard_map/all_to_all | solution.py:267
  162.8 3.4 %collective-permute-start.1 = (bf16[16,64,128]{2,1,0:T(8,128)(2,1)S(1)}, bf16[16,64,128]{2,1,0:T(8,128)(2,1)S(1)}, u32[]{:S(2)}, u32[]{:S(2)}) collective-permute-start(bf16[16,64,128]{2,1,0:T(8,128)(2,1)S(1)} %dynamic-slice_bitcast_fusion), channel_id=1, source_target_pairs={{0,16},{16,0},{32,48},{48,32},{64,80},{80,64},{96,112},{112,96},{1... | collective-permute-start | bytes 786440 | tf_op jit(solution)/shard_map/ppermute | solution.py:272
  166.5 9.0 %collective-permute-start.2 = (bf16[4,64,128]{2,1,0:T(8,128)(2,1)S(1)}, bf16[4,64,128]{2,1,0:T(8,128)(2,1)S(1)}, u32[]{:S(2)}, u32[]{:S(2)}) collective-permute-start(bf16[4,64,128]{2,1,0:T(8,128)(2,1)S(1)} %get-tuple-element.32), channel_id=1, source_target_pairs={{0,128},{16,144},{32,160},{48,176},{64,192},{80,208},{96,224},{112... | collective-permute-start | bytes 196616 | tf_op jit(solution)/shard_map/ppermute | solution.py:38
  169.0 6.6 %collective-permute-start.4 = (bf16[4,64,128]{2,1,0:T(8,128)(2,1)S(1)}, bf16[4,64,128]{2,1,0:T(8,128)(2,1)S(1)}, u32[]{:S(2)}, u32[]{:S(2)}) collective-permute-start(bf16[4,64,128]{2,1,0:T(8,128)(2,1)S(1)} %get-tuple-element.33), channel_id=1, source_target_pairs={{0,384},{16,400},{32,416},{48,432},{64,448},{80,464},{96,480},{112... | collective-permute-start | bytes 196616 | tf_op jit(solution)/shard_map/ppermute | solution.py:38
  173.5 7.7 %collective-permute-start.3 = (bf16[4,64,128]{2,1,0:T(8,128)(2,1)S(1)}, bf16[4,64,128]{2,1,0:T(8,128)(2,1)S(1)}, u32[]{:S(2)}, u32[]{:S(2)}) collective-permute-start(bf16[4,64,128]{2,1,0:T(8,128)(2,1)S(1)} %get-tuple-element.34), channel_id=1, source_target_pairs={{0,256},{16,272},{32,288},{48,304},{64,320},{80,336},{96,352},{112... | collective-permute-start | bytes 196616 | tf_op jit(solution)/shard_map/ppermute | solution.py:38
  192.1 38.3 %all-to-all-start.4 = ((bf16[16,144,128]{2,1,0:T(8,128)(2,1)}), bf16[16,144,128]{2,1,0:T(8,128)(2,1)S(1)}, u32[]{:S(2)}, u32[]{:S(2)}) async-start(bf16[16,144,128]{2,1,0:T(8,128)(2,1)} %shard_map.90), calls=%async_computation.4 | async-start | bytes 1179648 | tf_op jit(solution)/shard_map/all_to_all | solution.py:285
  200.1 9.0 %collective-permute-start.5 = (bf16[64,128]{1,0:T(8,128)(2,1)S(1)}, bf16[64,128]{1,0:T(8,128)(2,1)S(1)}, u32[]{:S(2)}, u32[]{:S(2)}) collective-permute-start(bf16[64,128]{1,0:T(8,128)(2,1)S(1)} %get-tuple-element.35), channel_id=1, source_target_pairs={{0,32},{16,48},{32,64},{48,80},{64,96},{80,112},{96,0},{112,16},{1... | collective-permute-start | bytes 49160 | tf_op jit(solution)/shard_map/ppermute | solution.py:38
  202.6 6.6 %collective-permute-start.7 = (bf16[64,128]{1,0:T(8,128)(2,1)S(1)}, bf16[64,128]{1,0:T(8,128)(2,1)S(1)}, u32[]{:S(2)}, u32[]{:S(2)}) collective-permute-start(bf16[64,128]{1,0:T(8,128)(2,1)S(1)} %get-tuple-element.36), channel_id=1, source_target_pairs={{0,96},{16,112},{32,0},{48,16},{64,32},{80,48},{96,64},{112,80},{1... | collective-permute-start | bytes 49160 | tf_op jit(solution)/shard_map/ppermute | solution.py:38
  207.2 7.1 %collective-permute-start.6 = (bf16[64,128]{1,0:T(8,128)(2,1)S(1)}, bf16[64,128]{1,0:T(8,128)(2,1)S(1)}, u32[]{:S(2)}, u32[]{:S(2)}) collective-permute-start(bf16[64,128]{1,0:T(8,128)(2,1)S(1)} %get-tuple-element.37), channel_id=1, source_target_pairs={{0,64},{16,80},{32,96},{48,112},{64,0},{80,16},{96,32},{112,48},{1... | collective-permute-start | bytes 49160 | tf_op jit(solution)/shard_map/ppermute | solution.py:38
Sparse Core Ops, SparseCore 0:
  10.1 111.8 all-gather.1

commit v6 on v5

--- a/solution.py
+++ b/solution.py
@@ -53,7 +53,7 @@
         grid=(pairs,),
         in_specs=[pl.BlockSpec((1, groups, feats, rows), lambda i: (i, 0, 0, 0))],
         out_specs=pl.BlockSpec((feats, groups * rows), lambda i: (i, 0)),
-        compiler_params=pltpu.CompilerParams(vmem_limit_bytes=16 * 1024 * 1024),
+        compiler_params=pltpu.CompilerParams(vmem_limit_bytes=8 * 1024 * 1024),
         cost_estimate=pl.CostEstimate(flops=0, bytes_accessed=4 * by_pair.size, transcendentals=0),
     )(by_pair)
 
@@ -117,7 +117,7 @@
             jax.ShapeDtypeStruct((1,), f32),
         ),
         out_specs=(vmem, vmem, pl.BlockSpec(memory_space=pltpu.SMEM)),
-        compiler_params=pltpu.CompilerParams(vmem_limit_bytes=32 * 1024 * 1024),
+        compiler_params=pltpu.CompilerParams(vmem_limit_bytes=12 * 1024 * 1024),
     )(every, student, teacher, target, into_margin, into_weight)
 
 
@@ -155,7 +155,7 @@
 def head_partial(core, objective, own, other, grad, blocks, extra):
     tall, rows = own.shape
     cols = grad.shape[1]
-    steps = 4
+    steps = 8
     per = blocks // steps
     feats = tall // blocks
     return pl.pallas_call(
@@ -170,7 +170,7 @@
             pl.BlockSpec((rows, cols), lambda i: (0, 0)),
         ],
         out_specs=pl.BlockSpec((per, 2 * feats + extra, cols), lambda i: (i, 0, 0)),
-        compiler_params=pltpu.CompilerParams(vmem_limit_bytes=32 * 1024 * 1024),
+        compiler_params=pltpu.CompilerParams(vmem_limit_bytes=8 * 1024 * 1024),
         cost_estimate=pl.CostEstimate(
             flops=4 * tall * rows * cols,
             bytes_accessed=4 * tall * rows + 2 * rows * cols + 4 * tall * cols,
@@ -198,7 +198,7 @@
             jax.ShapeDtypeStruct((1,), jnp.float32),
         ),
         out_specs=(pl.BlockSpec(memory_space=pltpu.VMEM), pl.BlockSpec(memory_space=pltpu.SMEM)),
-        compiler_params=pltpu.CompilerParams(vmem_limit_bytes=16 * 1024 * 1024),
+        compiler_params=pltpu.CompilerParams(vmem_limit_bytes=8 * 1024 * 1024),
     )(parts)
 
 
@@ -224,7 +224,7 @@
     around_x = [[(i, around(i, True, d)) for i in range(n_vocab)] for d in range(side)]
     around_y = [[(i, around(i, False, d)) for i in range(n_vocab)] for d in range(side)]
     weight_full = lax.all_gather(head_weight, "dp", axis=0, tiled=True)
-    by_group = to_all(hidden.T, "dp").reshape(n_dp, feats, rows)
+    by_group = lax.all_gather(hidden.T, "dp")
     by_pair = to_all(by_group, "vocab", same_core).reshape(pairs, n_dp, feats, rows)
     own_t = relayout(by_pair)
     other_t = lax.ppermute(own_t, "vocab", swap)

time: 241 us -> 240 us (level)
  blocking collectives: 90 us -> 86.1 us
    all_to_all x2 -> x1, blocking collectives: 90 us -> 50.8 us  [to_all(): lax.all_to_all(copies, axis, 0, 0, axis_index_groups=groups, tiled=True)]
    all_gather x0 -> x1, blocking collectives: none -> 35.4 us  [on_device(): by_group = lax.all_gather(hidden.T, 'dp')]
  transfers between devices with their start and end apart: 12 -> 12, of which waited for: 8 -> 8; matrix products, arithmetic and copies ran while one was open for 5% -> 4% of each run, Pallas kernels for 3% -> 3%
where the time goes in v6:
time: 240 us; the launch traced here: 239 us
  blocking collectives  86.1 us (36%)
  waiting for transfers between devices  53.4 us (22%)
  starting transfers between devices  48.5 us (20%)
  Pallas kernels  17.7 us (7%)
  between operations  16.1 us (7%)
  matrix products  11 us (5%)
  other arithmetic  3.45 us (1%)
  local copies, waits for them, and re-layouts  2.47 us (1%)
    all_to_all x1, blocking collectives, to_all(): lax.all_to_all(copies, axis, 0, 0, axis_index_groups=groups, tiled=True)  50.8 us
    all_gather x1, blocking collectives, on_device(): by_group = lax.all_gather(hidden.T, 'dp')  35.4 us
    ppermute x6, starting transfers between devices, ring_sum(): lax.ppermute(rounded[d], 'vocab', around[d])  18 us
    all_to_all x1, waiting for transfers between devices, on_device(): parts = lax.all_to_all(partial, 'dp', 0, 0, tiled=True)  15.4 us
    all_to_all x1, starting transfers between devices, on_device(): chunks = lax.all_to_all(chunks, 'dp', 0, 0, tiled=True)  11.5 us
    ppermute x6, waiting for transfers between devices, ring_sum(): lax.ppermute(rounded[d], 'vocab', around[d])  10.9 us
    pallas_call x1, Pallas kernels, head_partial(): pl.pallas_call(head_kernel, out_shape=jax.ShapeDtypeStruct((blocks, 2 * f...  8.75 us
    all_to_all x1, starting transfers between devices, on_device(): parts = lax.all_to_all(partial, 'dp', 0, 0, tiled=True)  8.02 us
  transfers between devices with their start and end apart: 12, of which 8 were waited for; matrix products, arithmetic and copies ran while one was open for 4% of the time, Pallas kernels for 3%

profile of v6, /device:TPU:32, one launch (start us, length us, event | category | flops | bytes accessed | tf_op | source)
XLA Modules:
  0.0 238.8 jit_solution(12318443190912947813)
XLA Ops:
  7.9 35.4 %all-gather = bf16[1024,128]{1,0:T(8,128)(2,1)S(1)} all-gather(bf16[64,128]{1,0:T(8,128)(2,1)} %bitcast.71), channel_id=2, replica_groups=mesh['vocab'=32,'dp'=16] {'dp'}, dimensions={0}, use_global_device_ids=true | all-gather | bytes 278528 | tf_op jit(solution)/shard_map/all_gather | solution.py:227
  44.4 50.8 %all_to_all.20.in_ref = bf16[16,16,64,128]{3,2,1,0:T(8,128)(2,1)S(1)} all-to-all(bf16[16,16,64,128]{3,2,1,0:T(8,128)(2,1)S(1)} %broadcast_in_dim.10), channel_id=1, replica_groups={{0,32,64,96,128,160,192,224,256,288,320,352,384,416,448,480},{16,48,80,..., dimensions={0} | all-to-all | bytes 8388608 | tf_op jit(solution)/shard_map/all_to_all | solution.py:31
  95.2 6.2 %shard_map.88.own_ref = bf16[1024,2048]{1,0:T(8,128)(2,1)} custom-call(bf16[16,16,64,128]{3,2,1,0:T(8,128)(2,1)S(1)} %all_to_all.20.in_ref), custom_call_target="tpu_custom_call" | custom-call | bytes 8388608 | tf_op jit(solution)/shard_map/pallas_call | solution.py:50
  101.3 1.9 collective-permute-start
  103.9 6.8 %collective-permute-done.other_ref = bf16[1024,2048]{1,0:T(8,128)(2,1)} collective-permute-done((bf16[1024,2048]{1,0:T(8,128)(2,1)}, bf16[1024,2048]{1,0:T(8,128)(2,1)}, u32[]{:S(2)}, u32[]{:S(2)}) %collective-permute-start) | collective-permute-done | bytes 4194336 | tf_op jit(solution)/shard_map/ppermute | solution.py:230
  111.9 6.6 %all-gather.3.cloned.1.call-done = bf16[2048,2048]{1,0:T(8,128)(2,1)} async-done(((bf16[128,2048]{1,0:T(8,128)(2,1)}), bf16[2048,2048]{1,0:T(8,128)(2,1)}) %all-gather.3.cloned.1.call-update) | async-done | bytes 8388624 | tf_op jit(solution)/shard_map/all_gather | solution.py:226
  118.5 4.8 %fusion.21 = (f32[128]{0:T(128)S(1)}, f32[128,2048]{1,0:T(8,128)S(1)}) fusion(bf16[2048,128]{1,0:T(8,128)(2,1)S(1)} %bitcast.64, bf16[2048,2048]{1,0:T(8,128)(2,1)} %all-gather.3.cloned.1.call-done), kind=kOutput, calls=%fused_computation.52 | convolution fusion | flops 1074003840 | bytes 9961984 | tf_op jit(solution)/shard_map/dot_general | solution.py:242
  124.8 7.1 %all-to-all-start.1 = ((f32[32,8,128]{2,1,0:T(8,128)}), f32[32,8,128]{2,1,0:T(8,128)S(1)}, u32[]{:S(2)}, u32[]{:S(2)}) async-start(f32[32,8,128]{2,1,0:T(8,128)} %broadcast_in_dim.12), calls=%async_computation.1 | async-start | bytes 262144 | tf_op jit(solution)/shard_map/all_to_all | solution.py:31
  132.3 7.5 %all-to-all-done.1.every_ref = f32[32,8,128]{2,1,0:T(8,128)S(1)} async-done(((f32[32,8,128]{2,1,0:T(8,128)}), f32[32,8,128]{2,1,0:T(8,128)S(1)}, u32[]{:S(2)}, u32[]{:S(2)}) %all-to-all-start.1) | async-done | bytes 131104 | tf_op jit(solution)/shard_map/all_to_all | solution.py:31
  141.5 11.5 %all-to-all-start.2 = ((bf16[16,128,128]{2,1,0:T(8,128)(2,1)}), bf16[16,128,128]{2,1,0:T(8,128)(2,1)S(1)}, u32[]{:S(2)}, u32[]{:S(2)}) async-start(bf16[16,128,128]{2,1,0:T(8,128)(2,1)} %get-tuple-element.13), calls=%async_computation.2 | async-start | bytes 1048576 | tf_op jit(solution)/shard_map/all_to_all | solution.py:267
  153.0 6.3 %fusion = bf16[2048,128]{0,1:T(8,128)(2,1)S(1)} fusion(bf16[128,2048]{1,0:T(8,128)(2,1)S(1)} %get-tuple-element.14, bf16[2048,2048]{1,0:T(8,128)(2,1)} %all-gather.3.cloned.1.call-done), kind=kOutput, calls=%fused_computation.1 | convolution fusion | flops 1074003968 | bytes 9437184 | tf_op jit(solution)/shard_map/dot_general | solution.py:268
  159.6 1.9 collective-permute-start.1
  163.3 2.5 %collective-permute-start.2 = (bf16[4,64,128]{2,1,0:T(8,128)(2,1)S(1)}, bf16[4,64,128]{2,1,0:T(8,128)(2,1)S(1)}, u32[]{:S(2)}, u32[]{:S(2)}) collective-permute-start(bf16[4,64,128]{2,1,0:T(8,128)(2,1)S(1)} %get-tuple-element.32), channel_id=1, source_target_pairs={{0,128},{16,144},{32,160},{48,176},{64,192},{80,208},{96,224},{112... | collective-permute-start | bytes 196616 | tf_op jit(solution)/shard_map/ppermute | solution.py:38
  165.7 4.6 %collective-permute-start.4 = (bf16[4,64,128]{2,1,0:T(8,128)(2,1)S(1)}, bf16[4,64,128]{2,1,0:T(8,128)(2,1)S(1)}, u32[]{:S(2)}, u32[]{:S(2)}) collective-permute-start(bf16[4,64,128]{2,1,0:T(8,128)(2,1)S(1)} %get-tuple-element.33), channel_id=1, source_target_pairs={{0,384},{16,400},{32,416},{48,432},{64,448},{80,464},{96,480},{112... | collective-permute-start | bytes 196616 | tf_op jit(solution)/shard_map/ppermute | solution.py:38
  170.3 2.0 collective-permute-start.3
  172.3 5.7 %collective-permute-done.3 = bf16[4,64,128]{2,1,0:T(8,128)(2,1)S(1)} collective-permute-done((bf16[4,64,128]{2,1,0:T(8,128)(2,1)S(1)}, bf16[4,64,128]{2,1,0:T(8,128)(2,1)S(1)}, u32[]{:S(2)}, u32[]{:S(2)}) %collective-permute-start.3) | collective-permute-done | bytes 65568 | tf_op jit(solution)/shard_map/ppermute | solution.py:38
  178.0 4.0 %all-to-all-done.2 = bf16[16,128,128]{2,1,0:T(8,128)(2,1)S(1)} async-done(((bf16[16,128,128]{2,1,0:T(8,128)(2,1)}), bf16[16,128,128]{2,1,0:T(8,128)(2,1)S(1)}, u32[]{:S(2)}, u32[]{:S(2)}) %all-to-all-start.2) | async-done | bytes 524320 | tf_op jit(solution)/shard_map/all_to_all | solution.py:267
  182.1 8.8 %shard_map.90 = bf16[16,144,128]{2,1,0:T(8,128)(2,1)} custom-call(s32[1]{0:T(128)} %bitcast.core_ref, f32[1]{0:T(128)} %get-tuple-element.12.objective_ref, bf16[1024,2048]{1,0:T(8,128)(2,1)} %shard_map.88.own_ref, bf16[1024,2048]{1,0:T(8,128)(2,1)} %collective-permute-done.other_ref, bf16[2048,128]{1,0:T(8,128)(2,1)S(1)} %bitcast.63), custom_call_target="tpu_custom_call" | custom-call | flops 1073741824 | bytes 9437184 | tf_op jit(solution)/shard_map/pallas_call | solution.py:161
  190.8 8.0 %all-to-all-start.3 = ((bf16[16,144,128]{2,1,0:T(8,128)(2,1)}), bf16[16,144,128]{2,1,0:T(8,128)(2,1)S(1)}, u32[]{:S(2)}, u32[]{:S(2)}) async-start(bf16[16,144,128]{2,1,0:T(8,128)(2,1)} %shard_map.90), calls=%async_computation.3 | async-start | bytes 1179648 | tf_op jit(solution)/shard_map/all_to_all | solution.py:285
  198.9 2.4 %collective-permute-start.5 = (bf16[64,128]{1,0:T(8,128)(2,1)S(1)}, bf16[64,128]{1,0:T(8,128)(2,1)S(1)}, u32[]{:S(2)}, u32[]{:S(2)}) collective-permute-start(bf16[64,128]{1,0:T(8,128)(2,1)S(1)} %get-tuple-element.35), channel_id=1, source_target_pairs={{0,32},{16,48},{32,64},{48,80},{64,96},{80,112},{96,0},{112,16},{1... | collective-permute-start | bytes 49160 | tf_op jit(solution)/shard_map/ppermute | solution.py:38
  201.3 4.6 %collective-permute-start.7 = (bf16[64,128]{1,0:T(8,128)(2,1)S(1)}, bf16[64,128]{1,0:T(8,128)(2,1)S(1)}, u32[]{:S(2)}, u32[]{:S(2)}) collective-permute-start(bf16[64,128]{1,0:T(8,128)(2,1)S(1)} %get-tuple-element.36), channel_id=1, source_target_pairs={{0,96},{16,112},{32,0},{48,16},{64,32},{80,48},{96,64},{112,80},{1... | collective-permute-start | bytes 49160 | tf_op jit(solution)/shard_map/ppermute | solution.py:38
  206.0 1.9 collective-permute-start.6
  207.9 5.2 %collective-permute-done.6 = bf16[64,128]{1,0:T(8,128)(2,1)S(1)} collective-permute-done((bf16[64,128]{1,0:T(8,128)(2,1)S(1)}, bf16[64,128]{1,0:T(8,128)(2,1)S(1)}, u32[]{:S(2)}, u32[]{:S(2)}) %collective-permute-start.6) | collective-permute-done | bytes 16416 | tf_op jit(solution)/shard_map/ppermute | solution.py:38
  213.7 15.4 %all-to-all-done.3.parts_ref = bf16[16,144,128]{2,1,0:T(8,128)(2,1)S(1)} async-done(((bf16[16,144,128]{2,1,0:T(8,128)(2,1)}), bf16[16,144,128]{2,1,0:T(8,128)(2,1)S(1)}, u32[]{:S(2)}, u32[]{:S(2)}) %all-to-all-start.3) | async-done | bytes 589856 | tf_op jit(solution)/shard_map/all_to_all | solution.py:285
  (46 shorter events, 10.9 us)
Async XLA Ops:
  7.2 111.4 %all-gather.3.cloned.1.call-start = ((), (), s32[]{:S(2)}) async-start(), calls=%async_computation.4 | async-start | bytes 8912896 | tf_op jit(solution)/shard_map/all_gather | solution.py:226
  44.3 58.9 %copy-start.3 = (s32[1,16]{1,0:T(1,128)S(1)}, s32[1,16]{1,0:T(1,128)}, u32[]{:S(2)}) copy-start(s32[1,16]{1,0:T(1,128)} %param.11) | copy-start | bytes 196
  44.3 59.3 %copy-start = (bf16[128,2048]{1,0:T(8,128)(2,1)S(1)}, bf16[128,2048]{1,0:T(8,128)(2,1)}, u32[]{:S(2)}) copy-start(bf16[128,2048]{1,0:T(8,128)(2,1)} %teacher_ref.1) | copy-start | bytes 1572868
  44.4 59.4 %copy-start.2 = (s32[128]{0:T(128)S(1)}, s32[128]{0:T(128)}, u32[]{:S(2)}) copy-start(s32[128]{0:T(128)} %param.9) | copy-start | bytes 1540
  44.4 59.4 %copy-start.1 = (s32[1,128]{1,0:T(1,128)S(1)}, s32[1,128]{1,0:T(1,128)}, u32[]{:S(2)}) copy-start(s32[1,128]{1,0:T(1,128)} %param.10) | copy-start | bytes 1540
  101.3 9.4 %collective-permute-start = (bf16[1024,2048]{1,0:T(8,128)(2,1)}, bf16[1024,2048]{1,0:T(8,128)(2,1)}, u32[]{:S(2)}, u32[]{:S(2)}) collective-permute-start(bf16[1024,2048]{1,0:T(8,128)(2,1)} %shard_map.88.own_ref), channel_id=1, source_target_pairs={{0,16},{16,0},{32,48},{48,32},{64,80},{80,64},{96,112},{112,96},{1... | collective-permute-start | bytes 12582920 | tf_op jit(solution)/shard_map/ppermute | solution.py:230
  124.8 15.0 %all-to-all-start.1 = ((f32[32,8,128]{2,1,0:T(8,128)}), f32[32,8,128]{2,1,0:T(8,128)S(1)}, u32[]{:S(2)}, u32[]{:S(2)}) async-start(f32[32,8,128]{2,1,0:T(8,128)} %broadcast_in_dim.12), calls=%async_computation.1 | async-start | bytes 262144 | tf_op jit(solution)/shard_map/all_to_all | solution.py:31
  141.5 40.5 %all-to-all-start.2 = ((bf16[16,128,128]{2,1,0:T(8,128)(2,1)}), bf16[16,128,128]{2,1,0:T(8,128)(2,1)S(1)}, u32[]{:S(2)}, u32[]{:S(2)}) async-start(bf16[16,128,128]{2,1,0:T(8,128)(2,1)} %get-tuple-element.13), calls=%async_computation.2 | async-start | bytes 1048576 | tf_op jit(solution)/shard_map/all_to_all | solution.py:267
  159.6 3.4 %collective-permute-start.1 = (bf16[16,64,128]{2,1,0:T(8,128)(2,1)S(1)}, bf16[16,64,128]{2,1,0:T(8,128)(2,1)S(1)}, u32[]{:S(2)}, u32[]{:S(2)}) collective-permute-start(bf16[16,64,128]{2,1,0:T(8,128)(2,1)S(1)} %dynamic-slice_bitcast_fusion), channel_id=1, source_target_pairs={{0,16},{16,0},{32,48},{48,32},{64,80},{80,64},{96,112},{112,96},{1... | collective-permute-start | bytes 786440 | tf_op jit(solution)/shard_map/ppermute | solution.py:272
  163.3 9.0 %collective-permute-start.2 = (bf16[4,64,128]{2,1,0:T(8,128)(2,1)S(1)}, bf16[4,64,128]{2,1,0:T(8,128)(2,1)S(1)}, u32[]{:S(2)}, u32[]{:S(2)}) collective-permute-start(bf16[4,64,128]{2,1,0:T(8,128)(2,1)S(1)} %get-tuple-element.32), channel_id=1, source_target_pairs={{0,128},{16,144},{32,160},{48,176},{64,192},{80,208},{96,224},{112... | collective-permute-start | bytes 196616 | tf_op jit(solution)/shard_map/ppermute | solution.py:38
  165.7 6.6 %collective-permute-start.4 = (bf16[4,64,128]{2,1,0:T(8,128)(2,1)S(1)}, bf16[4,64,128]{2,1,0:T(8,128)(2,1)S(1)}, u32[]{:S(2)}, u32[]{:S(2)}) collective-permute-start(bf16[4,64,128]{2,1,0:T(8,128)(2,1)S(1)} %get-tuple-element.33), channel_id=1, source_target_pairs={{0,384},{16,400},{32,416},{48,432},{64,448},{80,464},{96,480},{112... | collective-permute-start | bytes 196616 | tf_op jit(solution)/shard_map/ppermute | solution.py:38
  170.3 7.7 %collective-permute-start.3 = (bf16[4,64,128]{2,1,0:T(8,128)(2,1)S(1)}, bf16[4,64,128]{2,1,0:T(8,128)(2,1)S(1)}, u32[]{:S(2)}, u32[]{:S(2)}) collective-permute-start(bf16[4,64,128]{2,1,0:T(8,128)(2,1)S(1)} %get-tuple-element.34), channel_id=1, source_target_pairs={{0,256},{16,272},{32,288},{48,304},{64,320},{80,336},{96,352},{112... | collective-permute-start | bytes 196616 | tf_op jit(solution)/shard_map/ppermute | solution.py:38
  190.8 38.3 %all-to-all-start.3 = ((bf16[16,144,128]{2,1,0:T(8,128)(2,1)}), bf16[16,144,128]{2,1,0:T(8,128)(2,1)S(1)}, u32[]{:S(2)}, u32[]{:S(2)}) async-start(bf16[16,144,128]{2,1,0:T(8,128)(2,1)} %shard_map.90), calls=%async_computation.3 | async-start | bytes 1179648 | tf_op jit(solution)/shard_map/all_to_all | solution.py:285
  198.9 9.0 %collective-permute-start.5 = (bf16[64,128]{1,0:T(8,128)(2,1)S(1)}, bf16[64,128]{1,0:T(8,128)(2,1)S(1)}, u32[]{:S(2)}, u32[]{:S(2)}) collective-permute-start(bf16[64,128]{1,0:T(8,128)(2,1)S(1)} %get-tuple-element.35), channel_id=1, source_target_pairs={{0,32},{16,48},{32,64},{48,80},{64,96},{80,112},{96,0},{112,16},{1... | collective-permute-start | bytes 49160 | tf_op jit(solution)/shard_map/ppermute | solution.py:38
  201.3 6.6 %collective-permute-start.7 = (bf16[64,128]{1,0:T(8,128)(2,1)S(1)}, bf16[64,128]{1,0:T(8,128)(2,1)S(1)}, u32[]{:S(2)}, u32[]{:S(2)}) collective-permute-start(bf16[64,128]{1,0:T(8,128)(2,1)S(1)} %get-tuple-element.36), channel_id=1, source_target_pairs={{0,96},{16,112},{32,0},{48,16},{64,32},{80,48},{96,64},{112,80},{1... | collective-permute-start | bytes 49160 | tf_op jit(solution)/shard_map/ppermute | solution.py:38
  206.0 7.1 %collective-permute-start.6 = (bf16[64,128]{1,0:T(8,128)(2,1)S(1)}, bf16[64,128]{1,0:T(8,128)(2,1)S(1)}, u32[]{:S(2)}, u32[]{:S(2)}) collective-permute-start(bf16[64,128]{1,0:T(8,128)(2,1)S(1)} %get-tuple-element.37), channel_id=1, source_target_pairs={{0,64},{16,80},{32,96},{48,112},{64,0},{80,16},{96,32},{112,48},{1... | collective-permute-start | bytes 49160 | tf_op jit(solution)/shard_map/ppermute | solution.py:38
Sparse Core Ops, SparseCore 0:
  10.1 108.4 all-gather.2

commit v7 on v6

--- a/solution.py
+++ b/solution.py
@@ -121,56 +121,78 @@
     )(every, student, teacher, target, into_margin, into_weight)
 
 
-def head_kernel(core_ref, objective_ref, own_ref, other_ref, grad_ref, out_ref):
+head_steps = 4
+
+
+def head_kernel(
+    core_ref, objective_ref, own_hbm, other_hbm, grad_ref, out_ref,
+    own_ref, other_ref, own_sem, other_sem,
+):
     f32, bf16 = jnp.float32, jnp.bfloat16
-    grad = grad_ref[...]
-    own = jnp.dot(own_ref[...], grad, preferred_element_type=f32).astype(bf16)
-    other = jnp.dot(other_ref[...], grad, preferred_element_type=f32).astype(bf16)
-    blocks, tall, _ = out_ref.shape
-    feats = own.shape[0] // blocks
-    extra = tall - 2 * feats
-    value = jnp.full((extra, own.shape[1]), objective_ref[0], f32)
+    total, tall, cols = out_ref.shape
+    blocks = total // head_steps
+    step = own_ref.shape[0] // head_steps
+    feats = step // blocks
+
+    def copies(i):
+        part = pl.ds(i * step, step)
+        return (
+            pltpu.make_async_copy(own_hbm.at[part], own_ref.at[part], own_sem.at[i]),
+            pltpu.make_async_copy(other_hbm.at[part], other_ref.at[part], other_sem.at[i]),
+        )
+
+    for i in range(head_steps):
+        for copy in copies(i):
+            copy.start()
+    value = jnp.full((tall - 2 * feats, cols), objective_ref[0], f32)
     high = value.astype(bf16).astype(f32)
     middle = (value - high).astype(bf16).astype(f32)
     low = value - high - middle
     line = lax.broadcasted_iota(jnp.int32, value.shape, 0)
     pieces = jnp.where(line == 0, high, jnp.where(line == 1, middle, jnp.where(line == 2, low, 0.0)))
     pieces = pieces.astype(bf16)
-
-    def store(first, second):
-        for j in range(blocks):
-            out_ref[j, :feats] = first[j * feats : (j + 1) * feats]
-            out_ref[j, feats : 2 * feats] = second[j * feats : (j + 1) * feats]
-            out_ref[j, 2 * feats :] = pieces
-
-    @pl.when(core_ref[0] == 0)
-    def _():
-        store(own, other)
-
-    @pl.when(core_ref[0] != 0)
-    def _():
-        store(other, own)
+    for j in range(total):
+        out_ref[j, 2 * feats :] = pieces
+    for i in range(head_steps):
+        for copy in copies(i):
+            copy.wait()
+        part = slice(i * step, (i + 1) * step)
+        own = jnp.dot(own_ref[part], grad_ref[...], preferred_element_type=f32).astype(bf16)
+        other = jnp.dot(other_ref[part], grad_ref[...], preferred_element_type=f32).astype(bf16)
+
+        def store(first, second):
+            for j in range(blocks):
+                out_ref[i * blocks + j, :feats] = first[j * feats : (j + 1) * feats]
+                out_ref[i * blocks + j, feats : 2 * feats] = second[j * feats : (j + 1) * feats]
+
+        @pl.when(core_ref[0] == 0)
+        def _():
+            store(own, other)
+
+        @pl.when(core_ref[0] != 0)
+        def _():
+            store(other, own)
 
 
 def head_partial(core, objective, own, other, grad, blocks, extra):
     tall, rows = own.shape
     cols = grad.shape[1]
-    steps = 8
-    per = blocks // steps
     feats = tall // blocks
+    smem = pl.BlockSpec(memory_space=pltpu.SMEM)
+    vmem = pl.BlockSpec(memory_space=pltpu.VMEM)
+    hbm = pl.BlockSpec(memory_space=pl.ANY)
     return pl.pallas_call(
         head_kernel,
         out_shape=jax.ShapeDtypeStruct((blocks, 2 * feats + extra, cols), jnp.bfloat16),
-        grid=(steps,),
-        in_specs=[
-            pl.BlockSpec(memory_space=pltpu.SMEM),
-            pl.BlockSpec(memory_space=pltpu.SMEM),
-            pl.BlockSpec((tall // steps, rows), lambda i: (i, 0)),
-            pl.BlockSpec((tall // steps, rows), lambda i: (i, 0)),
-            pl.BlockSpec((rows, cols), lambda i: (0, 0)),
+        in_specs=[smem, smem, hbm, hbm, vmem],
+        out_specs=vmem,
+        scratch_shapes=[
+            pltpu.VMEM((tall, rows), own.dtype),
+            pltpu.VMEM((tall, rows), own.dtype),
+            pltpu.SemaphoreType.DMA((head_steps,)),
+            pltpu.SemaphoreType.DMA((head_steps,)),
         ],
-        out_specs=pl.BlockSpec((per, 2 * feats + extra, cols), lambda i: (i, 0, 0)),
-        compiler_params=pltpu.CompilerParams(vmem_limit_bytes=8 * 1024 * 1024),
+        compiler_params=pltpu.CompilerParams(vmem_limit_bytes=32 * 1024 * 1024),
         cost_estimate=pl.CostEstimate(
             flops=4 * tall * rows * cols,
             bytes_accessed=4 * tall * rows + 2 * rows * cols + 4 * tall * cols,

time: 240 us -> 237 us (0.988)
  Pallas kernels: 17.7 us -> 14.8 us
    pallas_call x1, Pallas kernels: 8.75 us -> 5.89 us  [head_partial(): pl.pallas_call(head_kernel, out_shape=jax.ShapeDtypeStruct((blocks, 2 * f...]
  transfers between devices with their start and end apart: 12 -> 12, of which waited for: 8 -> 8; matrix products, arithmetic and copies ran while one was open for 4% -> 5% of each run, Pallas kernels for 3% -> 3%
where the time goes in v7:
time: 237 us; the launch traced here: 236 us
  blocking collectives  86.1 us (36%)
  waiting for transfers between devices  53.4 us (23%)
  starting transfers between devices  48.5 us (20%)
  between operations  16.2 us (7%)
  Pallas kernels  14.8 us (6%)
  matrix products  11 us (5%)
  other arithmetic  3.45 us (1%)
  local copies, waits for them, and re-layouts  2.47 us (1%)
    all_to_all x1, blocking collectives, to_all(): lax.all_to_all(copies, axis, 0, 0, axis_index_groups=groups, tiled=True)  50.8 us
    all_gather x1, blocking collectives, on_device(): by_group = lax.all_gather(hidden.T, 'dp')  35.4 us
    ppermute x6, starting transfers between devices, ring_sum(): lax.ppermute(rounded[d], 'vocab', around[d])  18 us
    all_to_all x1, waiting for transfers between devices, on_device(): parts = lax.all_to_all(partial, 'dp', 0, 0, tiled=True)  15.4 us
    all_to_all x1, starting transfers between devices, on_device(): chunks = lax.all_to_all(chunks, 'dp', 0, 0, tiled=True)  11.5 us
    ppermute x6, waiting for transfers between devices, ring_sum(): lax.ppermute(rounded[d], 'vocab', around[d])  10.9 us
    all_to_all x1, starting transfers between devices, on_device(): parts = lax.all_to_all(partial, 'dp', 0, 0, tiled=True)  8.04 us
    all_to_all x1, waiting for transfers between devices, to_all(): lax.all_to_all(copies, axis, 0, 0, axis_index_groups=groups, tiled=True)  7.53 us
  transfers between devices with their start and end apart: 12, of which 8 were waited for; matrix products, arithmetic and copies ran while one was open for 5% of the time, Pallas kernels for 3%

profile of v7, /device:TPU:32, one launch (start us, length us, event | category | flops | bytes accessed | tf_op | source)
XLA Modules:
  0.0 236.0 jit_solution(5534408049413298350)
XLA Ops:
  7.9 35.4 %all-gather = bf16[1024,128]{1,0:T(8,128)(2,1)S(1)} all-gather(bf16[64,128]{1,0:T(8,128)(2,1)} %bitcast.71), channel_id=2, replica_groups=mesh['vocab'=32,'dp'=16] {'dp'}, dimensions={0}, use_global_device_ids=true | all-gather | bytes 278528 | tf_op jit(solution)/shard_map/all_gather | solution.py:249
  44.4 50.8 %all_to_all.20.in_ref = bf16[16,16,64,128]{3,2,1,0:T(8,128)(2,1)S(1)} all-to-all(bf16[16,16,64,128]{3,2,1,0:T(8,128)(2,1)S(1)} %broadcast_in_dim.10), channel_id=1, replica_groups={{0,32,64,96,128,160,192,224,256,288,320,352,384,416,448,480},{16,48,80,..., dimensions={0} | all-to-all | bytes 8388608 | tf_op jit(solution)/shard_map/all_to_all | solution.py:31
  95.2 6.2 %shard_map.88.own_hbm = bf16[1024,2048]{1,0:T(8,128)(2,1)} custom-call(bf16[16,16,64,128]{3,2,1,0:T(8,128)(2,1)S(1)} %all_to_all.20.in_ref), custom_call_target="tpu_custom_call" | custom-call | bytes 8388608 | tf_op jit(solution)/shard_map/pallas_call | solution.py:50
  101.3 1.9 collective-permute-start
  103.9 6.8 %collective-permute-done.other_hbm = bf16[1024,2048]{1,0:T(8,128)(2,1)} collective-permute-done((bf16[1024,2048]{1,0:T(8,128)(2,1)}, bf16[1024,2048]{1,0:T(8,128)(2,1)}, u32[]{:S(2)}, u32[]{:S(2)}) %collective-permute-start) | collective-permute-done | bytes 4194336 | tf_op jit(solution)/shard_map/ppermute | solution.py:252
  111.9 6.6 %all-gather.3.cloned.1.call-done = bf16[2048,2048]{1,0:T(8,128)(2,1)} async-done(((bf16[128,2048]{1,0:T(8,128)(2,1)}), bf16[2048,2048]{1,0:T(8,128)(2,1)}) %all-gather.3.cloned.1.call-update) | async-done | bytes 8388624 | tf_op jit(solution)/shard_map/all_gather | solution.py:248
  118.5 4.8 %fusion.21 = (f32[128]{0:T(128)S(1)}, f32[128,2048]{1,0:T(8,128)S(1)}) fusion(bf16[2048,128]{1,0:T(8,128)(2,1)S(1)} %bitcast.64, bf16[2048,2048]{1,0:T(8,128)(2,1)} %all-gather.3.cloned.1.call-done), kind=kOutput, calls=%fused_computation.52 | convolution fusion | flops 1074003840 | bytes 9961984 | tf_op jit(solution)/shard_map/dot_general | solution.py:264
  124.8 7.1 %all-to-all-start.1 = ((f32[32,8,128]{2,1,0:T(8,128)}), f32[32,8,128]{2,1,0:T(8,128)S(1)}, u32[]{:S(2)}, u32[]{:S(2)}) async-start(f32[32,8,128]{2,1,0:T(8,128)} %broadcast_in_dim.12), calls=%async_computation.1 | async-start | bytes 262144 | tf_op jit(solution)/shard_map/all_to_all | solution.py:31
  132.3 7.5 %all-to-all-done.1.every_ref = f32[32,8,128]{2,1,0:T(8,128)S(1)} async-done(((f32[32,8,128]{2,1,0:T(8,128)}), f32[32,8,128]{2,1,0:T(8,128)S(1)}, u32[]{:S(2)}, u32[]{:S(2)}) %all-to-all-start.1) | async-done | bytes 131104 | tf_op jit(solution)/shard_map/all_to_all | solution.py:31
  141.5 11.5 %all-to-all-start.2 = ((bf16[16,128,128]{2,1,0:T(8,128)(2,1)}), bf16[16,128,128]{2,1,0:T(8,128)(2,1)S(1)}, u32[]{:S(2)}, u32[]{:S(2)}) async-start(bf16[16,128,128]{2,1,0:T(8,128)(2,1)} %get-tuple-element.13), calls=%async_computation.2 | async-start | bytes 1048576 | tf_op jit(solution)/shard_map/all_to_all | solution.py:289
  153.0 6.3 %fusion = bf16[2048,128]{0,1:T(8,128)(2,1)S(1)} fusion(bf16[128,2048]{1,0:T(8,128)(2,1)S(1)} %get-tuple-element.14, bf16[2048,2048]{1,0:T(8,128)(2,1)} %all-gather.3.cloned.1.call-done), kind=kOutput, calls=%fused_computation.1 | convolution fusion | flops 1074003968 | bytes 9437184 | tf_op jit(solution)/shard_map/dot_general | solution.py:290
  159.6 1.9 collective-permute-start.1
  163.3 2.5 %collective-permute-start.2 = (bf16[4,64,128]{2,1,0:T(8,128)(2,1)S(1)}, bf16[4,64,128]{2,1,0:T(8,128)(2,1)S(1)}, u32[]{:S(2)}, u32[]{:S(2)}) collective-permute-start(bf16[4,64,128]{2,1,0:T(8,128)(2,1)S(1)} %get-tuple-element.32), channel_id=1, source_target_pairs={{0,128},{16,144},{32,160},{48,176},{64,192},{80,208},{96,224},{112... | collective-permute-start | bytes 196616 | tf_op jit(solution)/shard_map/ppermute | solution.py:38
  165.7 4.6 %collective-permute-start.4 = (bf16[4,64,128]{2,1,0:T(8,128)(2,1)S(1)}, bf16[4,64,128]{2,1,0:T(8,128)(2,1)S(1)}, u32[]{:S(2)}, u32[]{:S(2)}) collective-permute-start(bf16[4,64,128]{2,1,0:T(8,128)(2,1)S(1)} %get-tuple-element.33), channel_id=1, source_target_pairs={{0,384},{16,400},{32,416},{48,432},{64,448},{80,464},{96,480},{112... | collective-permute-start | bytes 196616 | tf_op jit(solution)/shard_map/ppermute | solution.py:38
  170.3 2.0 collective-permute-start.3
  172.3 5.7 %collective-permute-done.3 = bf16[4,64,128]{2,1,0:T(8,128)(2,1)S(1)} collective-permute-done((bf16[4,64,128]{2,1,0:T(8,128)(2,1)S(1)}, bf16[4,64,128]{2,1,0:T(8,128)(2,1)S(1)}, u32[]{:S(2)}, u32[]{:S(2)}) %collective-permute-start.3) | collective-permute-done | bytes 65568 | tf_op jit(solution)/shard_map/ppermute | solution.py:38
  178.0 4.0 %all-to-all-done.2 = bf16[16,128,128]{2,1,0:T(8,128)(2,1)S(1)} async-done(((bf16[16,128,128]{2,1,0:T(8,128)(2,1)}), bf16[16,128,128]{2,1,0:T(8,128)(2,1)S(1)}, u32[]{:S(2)}, u32[]{:S(2)}) %all-to-all-start.2) | async-done | bytes 524320 | tf_op jit(solution)/shard_map/all_to_all | solution.py:289
  182.1 5.9 %shard_map.90 = bf16[16,144,128]{2,1,0:T(8,128)(2,1)} custom-call(s32[1]{0:T(128)} %bitcast.core_ref, f32[1]{0:T(128)} %get-tuple-element.12.objective_ref, bf16[1024,2048]{1,0:T(8,128)(2,1)} %shard_map.88.own_hbm, bf16[1024,2048]{1,0:T(8,128)(2,1)} %collective-permute-done.other_hbm, bf16[2048,128]{1,0:T(8,128)(2,1)S(1)} %bitcast.63), custom_call_target="tpu_custom_call" | custom-call | flops 1073741824 | bytes 9437184 | tf_op jit(solution)/shard_map/pallas_call | solution.py:184
  188.0 8.0 %all-to-all-start.3 = ((bf16[16,144,128]{2,1,0:T(8,128)(2,1)}), bf16[16,144,128]{2,1,0:T(8,128)(2,1)S(1)}, u32[]{:S(2)}, u32[]{:S(2)}) async-start(bf16[16,144,128]{2,1,0:T(8,128)(2,1)} %shard_map.90), calls=%async_computation.3 | async-start | bytes 1179648 | tf_op jit(solution)/shard_map/all_to_all | solution.py:307
  196.0 2.4 %collective-permute-start.5 = (bf16[64,128]{1,0:T(8,128)(2,1)S(1)}, bf16[64,128]{1,0:T(8,128)(2,1)S(1)}, u32[]{:S(2)}, u32[]{:S(2)}) collective-permute-start(bf16[64,128]{1,0:T(8,128)(2,1)S(1)} %get-tuple-element.35), channel_id=1, source_target_pairs={{0,32},{16,48},{32,64},{48,80},{64,96},{80,112},{96,0},{112,16},{1... | collective-permute-start | bytes 49160 | tf_op jit(solution)/shard_map/ppermute | solution.py:38
  198.5 4.6 %collective-permute-start.7 = (bf16[64,128]{1,0:T(8,128)(2,1)S(1)}, bf16[64,128]{1,0:T(8,128)(2,1)S(1)}, u32[]{:S(2)}, u32[]{:S(2)}) collective-permute-start(bf16[64,128]{1,0:T(8,128)(2,1)S(1)} %get-tuple-element.36), channel_id=1, source_target_pairs={{0,96},{16,112},{32,0},{48,16},{64,32},{80,48},{96,64},{112,80},{1... | collective-permute-start | bytes 49160 | tf_op jit(solution)/shard_map/ppermute | solution.py:38
  203.1 1.9 collective-permute-start.6
  205.1 5.2 %collective-permute-done.6 = bf16[64,128]{1,0:T(8,128)(2,1)S(1)} collective-permute-done((bf16[64,128]{1,0:T(8,128)(2,1)S(1)}, bf16[64,128]{1,0:T(8,128)(2,1)S(1)}, u32[]{:S(2)}, u32[]{:S(2)}) %collective-permute-start.6) | collective-permute-done | bytes 16416 | tf_op jit(solution)/shard_map/ppermute | solution.py:38
  210.9 15.4 %all-to-all-done.3.parts_ref = bf16[16,144,128]{2,1,0:T(8,128)(2,1)S(1)} async-done(((bf16[16,144,128]{2,1,0:T(8,128)(2,1)}), bf16[16,144,128]{2,1,0:T(8,128)(2,1)S(1)}, u32[]{:S(2)}, u32[]{:S(2)}) %all-to-all-start.3) | async-done | bytes 589856 | tf_op jit(solution)/shard_map/all_to_all | solution.py:307
  (46 shorter events, 10.9 us)
Async XLA Ops:
  7.2 111.4 %all-gather.3.cloned.1.call-start = ((), (), s32[]{:S(2)}) async-start(), calls=%async_computation.4 | async-start | bytes 8912896 | tf_op jit(solution)/shard_map/all_gather | solution.py:248
  44.3 58.9 %copy-start.3 = (s32[1,16]{1,0:T(1,128)S(1)}, s32[1,16]{1,0:T(1,128)}, u32[]{:S(2)}) copy-start(s32[1,16]{1,0:T(1,128)} %param.11) | copy-start | bytes 196
  44.3 59.3 %copy-start = (bf16[128,2048]{1,0:T(8,128)(2,1)S(1)}, bf16[128,2048]{1,0:T(8,128)(2,1)}, u32[]{:S(2)}) copy-start(bf16[128,2048]{1,0:T(8,128)(2,1)} %teacher_ref.1) | copy-start | bytes 1572868
  44.4 59.4 %copy-start.2 = (s32[128]{0:T(128)S(1)}, s32[128]{0:T(128)}, u32[]{:S(2)}) copy-start(s32[128]{0:T(128)} %param.9) | copy-start | bytes 1540
  44.4 59.4 %copy-start.1 = (s32[1,128]{1,0:T(1,128)S(1)}, s32[1,128]{1,0:T(1,128)}, u32[]{:S(2)}) copy-start(s32[1,128]{1,0:T(1,128)} %param.10) | copy-start | bytes 1540
  101.3 9.4 %collective-permute-start = (bf16[1024,2048]{1,0:T(8,128)(2,1)}, bf16[1024,2048]{1,0:T(8,128)(2,1)}, u32[]{:S(2)}, u32[]{:S(2)}) collective-permute-start(bf16[1024,2048]{1,0:T(8,128)(2,1)} %shard_map.88.own_hbm), channel_id=1, source_target_pairs={{0,16},{16,0},{32,48},{48,32},{64,80},{80,64},{96,112},{112,96},{1... | collective-permute-start | bytes 12582920 | tf_op jit(solution)/shard_map/ppermute | solution.py:252
  124.8 15.0 %all-to-all-start.1 = ((f32[32,8,128]{2,1,0:T(8,128)}), f32[32,8,128]{2,1,0:T(8,128)S(1)}, u32[]{:S(2)}, u32[]{:S(2)}) async-start(f32[32,8,128]{2,1,0:T(8,128)} %broadcast_in_dim.12), calls=%async_computation.1 | async-start | bytes 262144 | tf_op jit(solution)/shard_map/all_to_all | solution.py:31
  141.5 40.5 %all-to-all-start.2 = ((bf16[16,128,128]{2,1,0:T(8,128)(2,1)}), bf16[16,128,128]{2,1,0:T(8,128)(2,1)S(1)}, u32[]{:S(2)}, u32[]{:S(2)}) async-start(bf16[16,128,128]{2,1,0:T(8,128)(2,1)} %get-tuple-element.13), calls=%async_computation.2 | async-start | bytes 1048576 | tf_op jit(solution)/shard_map/all_to_all | solution.py:289
  159.6 3.4 %collective-permute-start.1 = (bf16[16,64,128]{2,1,0:T(8,128)(2,1)S(1)}, bf16[16,64,128]{2,1,0:T(8,128)(2,1)S(1)}, u32[]{:S(2)}, u32[]{:S(2)}) collective-permute-start(bf16[16,64,128]{2,1,0:T(8,128)(2,1)S(1)} %dynamic-slice_bitcast_fusion), channel_id=1, source_target_pairs={{0,16},{16,0},{32,48},{48,32},{64,80},{80,64},{96,112},{112,96},{1... | collective-permute-start | bytes 786440 | tf_op jit(solution)/shard_map/ppermute | solution.py:294
  163.3 9.0 %collective-permute-start.2 = (bf16[4,64,128]{2,1,0:T(8,128)(2,1)S(1)}, bf16[4,64,128]{2,1,0:T(8,128)(2,1)S(1)}, u32[]{:S(2)}, u32[]{:S(2)}) collective-permute-start(bf16[4,64,128]{2,1,0:T(8,128)(2,1)S(1)} %get-tuple-element.32), channel_id=1, source_target_pairs={{0,128},{16,144},{32,160},{48,176},{64,192},{80,208},{96,224},{112... | collective-permute-start | bytes 196616 | tf_op jit(solution)/shard_map/ppermute | solution.py:38
  165.7 6.6 %collective-permute-start.4 = (bf16[4,64,128]{2,1,0:T(8,128)(2,1)S(1)}, bf16[4,64,128]{2,1,0:T(8,128)(2,1)S(1)}, u32[]{:S(2)}, u32[]{:S(2)}) collective-permute-start(bf16[4,64,128]{2,1,0:T(8,128)(2,1)S(1)} %get-tuple-element.33), channel_id=1, source_target_pairs={{0,384},{16,400},{32,416},{48,432},{64,448},{80,464},{96,480},{112... | collective-permute-start | bytes 196616 | tf_op jit(solution)/shard_map/ppermute | solution.py:38
  170.3 7.7 %collective-permute-start.3 = (bf16[4,64,128]{2,1,0:T(8,128)(2,1)S(1)}, bf16[4,64,128]{2,1,0:T(8,128)(2,1)S(1)}, u32[]{:S(2)}, u32[]{:S(2)}) collective-permute-start(bf16[4,64,128]{2,1,0:T(8,128)(2,1)S(1)} %get-tuple-element.34), channel_id=1, source_target_pairs={{0,256},{16,272},{32,288},{48,304},{64,320},{80,336},{96,352},{112... | collective-permute-start | bytes 196616 | tf_op jit(solution)/shard_map/ppermute | solution.py:38
  188.0 38.3 %all-to-all-start.3 = ((bf16[16,144,128]{2,1,0:T(8,128)(2,1)}), bf16[16,144,128]{2,1,0:T(8,128)(2,1)S(1)}, u32[]{:S(2)}, u32[]{:S(2)}) async-start(bf16[16,144,128]{2,1,0:T(8,128)(2,1)} %shard_map.90), calls=%async_computation.3 | async-start | bytes 1179648 | tf_op jit(solution)/shard_map/all_to_all | solution.py:307
  196.0 9.0 %collective-permute-start.5 = (bf16[64,128]{1,0:T(8,128)(2,1)S(1)}, bf16[64,128]{1,0:T(8,128)(2,1)S(1)}, u32[]{:S(2)}, u32[]{:S(2)}) collective-permute-start(bf16[64,128]{1,0:T(8,128)(2,1)S(1)} %get-tuple-element.35), channel_id=1, source_target_pairs={{0,32},{16,48},{32,64},{48,80},{64,96},{80,112},{96,0},{112,16},{1... | collective-permute-start | bytes 49160 | tf_op jit(solution)/shard_map/ppermute | solution.py:38
  198.5 6.6 %collective-permute-start.7 = (bf16[64,128]{1,0:T(8,128)(2,1)S(1)}, bf16[64,128]{1,0:T(8,128)(2,1)S(1)}, u32[]{:S(2)}, u32[]{:S(2)}) collective-permute-start(bf16[64,128]{1,0:T(8,128)(2,1)S(1)} %get-tuple-element.36), channel_id=1, source_target_pairs={{0,96},{16,112},{32,0},{48,16},{64,32},{80,48},{96,64},{112,80},{1... | collective-permute-start | bytes 49160 | tf_op jit(solution)/shard_map/ppermute | solution.py:38
  203.1 7.1 %collective-permute-start.6 = (bf16[64,128]{1,0:T(8,128)(2,1)S(1)}, bf16[64,128]{1,0:T(8,128)(2,1)S(1)}, u32[]{:S(2)}, u32[]{:S(2)}) collective-permute-start(bf16[64,128]{1,0:T(8,128)(2,1)S(1)} %get-tuple-element.37), channel_id=1, source_target_pairs={{0,64},{16,80},{32,96},{48,112},{64,0},{80,16},{96,32},{112,48},{1... | collective-permute-start | bytes 49160 | tf_op jit(solution)/shard_map/ppermute | solution.py:38
Sparse Core Ops, SparseCore 0:
  10.1 108.4 all-gather.2

commit v8 on v7

--- a/solution.py
+++ b/solution.py
@@ -56,6 +56,45 @@
         compiler_params=pltpu.CompilerParams(vmem_limit_bytes=8 * 1024 * 1024),
         cost_estimate=pl.CostEstimate(flops=0, bytes_accessed=4 * by_pair.size, transcendentals=0),
     )(by_pair)
+
+
+def stats_kernel(student_ref, teacher_ref, target_ref, out_ref):
+    f32 = jnp.float32
+    rows, width = student_ref.shape
+    step = 256
+    lows = range(0, width, step)
+    max_s = student_ref[:, :step]
+    max_t = teacher_ref[:, :step].astype(f32)
+    for low in lows[1:]:
+        max_s = jnp.maximum(max_s, student_ref[:, low : low + step])
+        max_t = jnp.maximum(max_t, teacher_ref[:, low : low + step].astype(f32))
+    max_s = jnp.max(max_s, axis=1, keepdims=True)
+    max_t = jnp.max(max_t, axis=1, keepdims=True)
+    target = target_ref[...]
+    zero = jnp.zeros((rows, step), f32)
+    sum_s, sum_t, cross, target_s, target_t = zero, zero, zero, zero, zero
+    for low in lows:
+        student = student_ref[:, low : low + step]
+        teacher = teacher_ref[:, low : low + step].astype(f32)
+        weight = jnp.exp(teacher - max_t)
+        sum_s += jnp.exp(student - max_s)
+        sum_t += weight
+        cross += weight * (teacher - student)
+        hot = lax.broadcasted_iota(jnp.int32, (rows, step), 1) + low == target
+        target_s += jnp.where(hot, student, 0.0)
+        target_t += jnp.where(hot, teacher, 0.0)
+    sums = [jnp.sum(x, axis=1, keepdims=True) for x in (sum_s, sum_t, cross, target_s, target_t)]
+    lines = jnp.transpose(jnp.concatenate([max_s, max_t] + sums + [max_s], axis=1))
+    for i in range(out_ref.shape[0]):
+        out_ref[i] = lines
+
+
+def local_stats(student, teacher, target, copies):
+    return pl.pallas_call(
+        stats_kernel,
+        out_shape=jax.ShapeDtypeStruct((copies, 8, student.shape[0]), jnp.float32),
+        compiler_params=pltpu.CompilerParams(vmem_limit_bytes=12 * 1024 * 1024),
+    )(student, teacher, target)
 
 
 def grad_kernel(
@@ -262,29 +301,10 @@
     tn = (((0,), (0,)), ((), ()))
     nt = (((1,), (1,)), ((), ()))
     student = lax.dot_general(rows_t, weight_full, tn, preferred_element_type=f32)
-    teacher = teacher_logits.astype(f32)
-    offset = lax.axis_index("vocab") * width
-    column = lax.broadcasted_iota(jnp.int32, student.shape, 1) + offset
-    is_target = column == target_ids[:, None]
-    own_max = jnp.max(student, axis=1)
-    own_tmax = jnp.max(teacher, axis=1)
-    own_exp = jnp.exp(student - own_max[:, None])
-    own_texp = jnp.exp(teacher - own_tmax[:, None])
-    stats = jnp.stack(
-        [
-            own_max,
-            own_tmax,
-            jnp.sum(own_exp, axis=1),
-            jnp.sum(own_texp, axis=1),
-            jnp.sum(own_texp * (teacher - student), axis=1),
-            jnp.sum(jnp.where(is_target, student, 0.0), axis=1),
-            jnp.sum(jnp.where(is_target, teacher, 0.0), axis=1),
-            jnp.zeros((rows,), f32),
-        ]
-    )
-    every = to_all(stats, "vocab").reshape(n_vocab, 8, rows)
+    target = (target_ids - index * width)[:, None]
+    every = lax.all_to_all(local_stats(student, teacher_logits, target, n_vocab), "vocab", 0, 0, tiled=True)
     logit_grad, chunks, objective = make_grad(
-        every, student, teacher_logits, (target_ids - offset)[:, None], into_margin, into_weight, n_dp
+        every, student, teacher_logits, target, into_margin, into_weight, n_dp
     )
     chunks = lax.all_to_all(chunks, "dp", 0, 0, tiled=True)
     term = lax.dot_general(weight_full, logit_grad, nt, preferred_element_type=f32).astype(bf16)

time: 237 us -> 237 us (level)
  transfers between devices with their start and end apart: 12 -> 12, of which waited for: 8 -> 8; matrix products, arithmetic and copies ran while one was open for 5% -> 4% of each run, Pallas kernels for 3% -> 3%
where the time goes in v8:
time: 237 us; the launch traced here: 236 us
  blocking collectives  86.1 us (36%)
  waiting for transfers between devices  53.6 us (23%)
  starting transfers between devices  48.5 us (20%)
  Pallas kernels  16.4 us (7%)
  between operations  16.1 us (7%)
  matrix products  10.9 us (5%)
  other arithmetic  2.44 us (1%)
    all_to_all x1, blocking collectives, to_all(): lax.all_to_all(copies, axis, 0, 0, axis_index_groups=groups, tiled=True)  50.8 us
    all_gather x1, blocking collectives, on_device(): by_group = lax.all_gather(hidden.T, 'dp')  35.4 us
    ppermute x6, starting transfers between devices, ring_sum(): lax.ppermute(rounded[d], 'vocab', around[d])  18 us
    all_to_all x1, waiting for transfers between devices, on_device(): parts = lax.all_to_all(partial, 'dp', 0, 0, tiled=True)  15.4 us
    all_to_all x1, starting transfers between devices, on_device(): chunks = lax.all_to_all(chunks, 'dp', 0, 0, tiled=True)  11.5 us
    ppermute x6, waiting for transfers between devices, ring_sum(): lax.ppermute(rounded[d], 'vocab', around[d])  10.9 us
    all_to_all x1, starting transfers between devices, on_device(): parts = lax.all_to_all(partial, 'dp', 0, 0, tiled=True)  8.02 us
    all_to_all x1, waiting for transfers between devices, on_device(): lax.all_to_all(local_stats(student, teacher_logits, target, n_vocab), 'vo...  7.64 us
  transfers between devices with their start and end apart: 12, of which 8 were waited for; matrix products, arithmetic and copies ran while one was open for 4% of the time, Pallas kernels for 3%

profile of v8, /device:TPU:32, one launch (start us, length us, event | category | flops | bytes accessed | tf_op | source)
XLA Modules:
  0.0 236.0 jit_solution(9131004608011714191)
XLA Ops:
  7.9 35.4 %all-gather = bf16[1024,128]{1,0:T(8,128)(2,1)S(1)} all-gather(bf16[64,128]{1,0:T(8,128)(2,1)} %bitcast.63), channel_id=2, replica_groups=mesh['vocab'=32,'dp'=16] {'dp'}, dimensions={0}, use_global_device_ids=true | all-gather | bytes 278528 | tf_op jit(solution)/shard_map/all_gather | solution.py:288
  44.4 50.8 %all_to_all.20.in_ref = bf16[16,16,64,128]{3,2,1,0:T(8,128)(2,1)S(1)} all-to-all(bf16[16,16,64,128]{3,2,1,0:T(8,128)(2,1)S(1)} %broadcast_in_dim.4), channel_id=1, replica_groups={{0,32,64,96,128,160,192,224,256,288,320,352,384,416,448,480},{16,48,80,..., dimensions={0} | all-to-all | bytes 8388608 | tf_op jit(solution)/shard_map/all_to_all | solution.py:31
  95.1 6.2 %shard_map.88.own_hbm = bf16[1024,2048]{1,0:T(8,128)(2,1)} custom-call(bf16[16,16,64,128]{3,2,1,0:T(8,128)(2,1)S(1)} %all_to_all.20.in_ref), custom_call_target="tpu_custom_call" | custom-call | bytes 8388608 | tf_op jit(solution)/shard_map/pallas_call | solution.py:50
  101.3 1.9 collective-permute-start
  103.8 6.9 %collective-permute-done.other_hbm = bf16[1024,2048]{1,0:T(8,128)(2,1)} collective-permute-done((bf16[1024,2048]{1,0:T(8,128)(2,1)}, bf16[1024,2048]{1,0:T(8,128)(2,1)}, u32[]{:S(2)}, u32[]{:S(2)}) %collective-permute-start) | collective-permute-done | bytes 4194336 | tf_op jit(solution)/shard_map/ppermute | solution.py:291
  111.9 6.6 %all-gather.3.cloned.1.call-done = bf16[2048,2048]{1,0:T(8,128)(2,1)} async-done(((bf16[128,2048]{1,0:T(8,128)(2,1)}), bf16[2048,2048]{1,0:T(8,128)(2,1)}) %all-gather.3.cloned.1.call-update) | async-done | bytes 8388624 | tf_op jit(solution)/shard_map/all_gather | solution.py:287
  118.5 4.7 %fusion.14.student_ref = f32[128,2048]{1,0:T(8,128)S(1)} fusion(bf16[2048,128]{1,0:T(8,128)(2,1)S(1)} %bitcast.56, bf16[2048,2048]{1,0:T(8,128)(2,1)} %all-gather.3.cloned.1.call-done), kind=kOutput, calls=%fused_computation.38 | convolution fusion | flops 1073741824 | bytes 9961472 | tf_op jit(solution)/shard_map/dot_general | solution.py:303
  124.8 7.1 %all-to-all-start.1 = ((f32[32,8,128]{2,1,0:T(8,128)}), f32[32,8,128]{2,1,0:T(8,128)S(1)}, u32[]{:S(2)}, u32[]{:S(2)}) async-start(f32[32,8,128]{2,1,0:T(8,128)} %shard_map.89), calls=%async_computation.1 | async-start | bytes 262144 | tf_op jit(solution)/shard_map/all_to_all | solution.py:305
  132.1 7.6 %all-to-all-done.1.every_ref = f32[32,8,128]{2,1,0:T(8,128)S(1)} async-done(((f32[32,8,128]{2,1,0:T(8,128)}), f32[32,8,128]{2,1,0:T(8,128)S(1)}, u32[]{:S(2)}, u32[]{:S(2)}) %all-to-all-start.1) | async-done | bytes 131104 | tf_op jit(solution)/shard_map/all_to_all | solution.py:305
  141.5 11.5 %all-to-all-start.2 = ((bf16[16,128,128]{2,1,0:T(8,128)(2,1)}), bf16[16,128,128]{2,1,0:T(8,128)(2,1)S(1)}, u32[]{:S(2)}, u32[]{:S(2)}) async-start(bf16[16,128,128]{2,1,0:T(8,128)(2,1)} %get-tuple-element.13), calls=%async_computation.2 | async-start | bytes 1048576 | tf_op jit(solution)/shard_map/all_to_all | solution.py:309
  153.0 6.3 %fusion = bf16[2048,128]{0,1:T(8,128)(2,1)S(1)} fusion(bf16[128,2048]{1,0:T(8,128)(2,1)S(1)} %get-tuple-element.14, bf16[2048,2048]{1,0:T(8,128)(2,1)} %all-gather.3.cloned.1.call-done), kind=kOutput, calls=%fused_computation.1 | convolution fusion | flops 1074003968 | bytes 9437184 | tf_op jit(solution)/shard_map/dot_general | solution.py:310
  159.6 1.9 collective-permute-start.1
  163.2 2.5 %collective-permute-start.2 = (bf16[4,64,128]{2,1,0:T(8,128)(2,1)S(1)}, bf16[4,64,128]{2,1,0:T(8,128)(2,1)S(1)}, u32[]{:S(2)}, u32[]{:S(2)}) collective-permute-start(bf16[4,64,128]{2,1,0:T(8,128)(2,1)S(1)} %get-tuple-element.27), channel_id=1, source_target_pairs={{0,128},{16,144},{32,160},{48,176},{64,192},{80,208},{96,224},{112... | collective-permute-start | bytes 196616 | tf_op jit(solution)/shard_map/ppermute | solution.py:38
  165.7 4.6 %collective-permute-start.4 = (bf16[4,64,128]{2,1,0:T(8,128)(2,1)S(1)}, bf16[4,64,128]{2,1,0:T(8,128)(2,1)S(1)}, u32[]{:S(2)}, u32[]{:S(2)}) collective-permute-start(bf16[4,64,128]{2,1,0:T(8,128)(2,1)S(1)} %get-tuple-element.28), channel_id=1, source_target_pairs={{0,384},{16,400},{32,416},{48,432},{64,448},{80,464},{96,480},{112... | collective-permute-start | bytes 196616 | tf_op jit(solution)/shard_map/ppermute | solution.py:38
  170.3 2.0 collective-permute-start.3
  172.3 5.7 %collective-permute-done.3 = bf16[4,64,128]{2,1,0:T(8,128)(2,1)S(1)} collective-permute-done((bf16[4,64,128]{2,1,0:T(8,128)(2,1)S(1)}, bf16[4,64,128]{2,1,0:T(8,128)(2,1)S(1)}, u32[]{:S(2)}, u32[]{:S(2)}) %collective-permute-start.3) | collective-permute-done | bytes 65568 | tf_op jit(solution)/shard_map/ppermute | solution.py:38
  178.0 4.0 %all-to-all-done.2 = bf16[16,128,128]{2,1,0:T(8,128)(2,1)S(1)} async-done(((bf16[16,128,128]{2,1,0:T(8,128)(2,1)}), bf16[16,128,128]{2,1,0:T(8,128)(2,1)S(1)}, u32[]{:S(2)}, u32[]{:S(2)}) %all-to-all-start.2) | async-done | bytes 524320 | tf_op jit(solution)/shard_map/all_to_all | solution.py:309
  182.0 5.9 %shard_map.91 = bf16[16,144,128]{2,1,0:T(8,128)(2,1)} custom-call(s32[1]{0:T(128)} %bitcast.core_ref, f32[1]{0:T(128)} %get-tuple-element.12.objective_ref, bf16[1024,2048]{1,0:T(8,128)(2,1)} %shard_map.88.own_hbm, bf16[1024,2048]{1,0:T(8,128)(2,1)} %collective-permute-done.other_hbm, bf16[2048,128]{1,0:T(8,128)(2,1)S(1)} %bitcast.55), custom_call_target="tpu_custom_call" | custom-call | flops 1073741824 | bytes 9437184 | tf_op jit(solution)/shard_map/pallas_call | solution.py:223
  187.9 8.0 %all-to-all-start.3 = ((bf16[16,144,128]{2,1,0:T(8,128)(2,1)}), bf16[16,144,128]{2,1,0:T(8,128)(2,1)S(1)}, u32[]{:S(2)}, u32[]{:S(2)}) async-start(bf16[16,144,128]{2,1,0:T(8,128)(2,1)} %shard_map.91), calls=%async_computation.3 | async-start | bytes 1179648 | tf_op jit(solution)/shard_map/all_to_all | solution.py:327
  196.0 2.4 %collective-permute-start.5 = (bf16[64,128]{1,0:T(8,128)(2,1)S(1)}, bf16[64,128]{1,0:T(8,128)(2,1)S(1)}, u32[]{:S(2)}, u32[]{:S(2)}) collective-permute-start(bf16[64,128]{1,0:T(8,128)(2,1)S(1)} %get-tuple-element.30), channel_id=1, source_target_pairs={{0,32},{16,48},{32,64},{48,80},{64,96},{80,112},{96,0},{112,16},{1... | collective-permute-start | bytes 49160 | tf_op jit(solution)/shard_map/ppermute | solution.py:38
  198.5 4.6 %collective-permute-start.7 = (bf16[64,128]{1,0:T(8,128)(2,1)S(1)}, bf16[64,128]{1,0:T(8,128)(2,1)S(1)}, u32[]{:S(2)}, u32[]{:S(2)}) collective-permute-start(bf16[64,128]{1,0:T(8,128)(2,1)S(1)} %get-tuple-element.31), channel_id=1, source_target_pairs={{0,96},{16,112},{32,0},{48,16},{64,32},{80,48},{96,64},{112,80},{1... | collective-permute-start | bytes 49160 | tf_op jit(solution)/shard_map/ppermute | solution.py:38
  203.1 1.9 collective-permute-start.6
  205.0 5.2 %collective-permute-done.6 = bf16[64,128]{1,0:T(8,128)(2,1)S(1)} collective-permute-done((bf16[64,128]{1,0:T(8,128)(2,1)S(1)}, bf16[64,128]{1,0:T(8,128)(2,1)S(1)}, u32[]{:S(2)}, u32[]{:S(2)}) %collective-permute-start.6) | collective-permute-done | bytes 16416 | tf_op jit(solution)/shard_map/ppermute | solution.py:38
  210.8 15.4 %all-to-all-done.3.parts_ref = bf16[16,144,128]{2,1,0:T(8,128)(2,1)S(1)} async-done(((bf16[16,144,128]{2,1,0:T(8,128)(2,1)}), bf16[16,144,128]{2,1,0:T(8,128)(2,1)S(1)}, u32[]{:S(2)}, u32[]{:S(2)}) %all-to-all-start.3) | async-done | bytes 589856 | tf_op jit(solution)/shard_map/all_to_all | solution.py:327
  (40 shorter events, 10.8 us)
Async XLA Ops:
  7.2 111.4 %all-gather.3.cloned.1.call-start = ((), (), s32[]{:S(2)}) async-start(), calls=%async_computation.4 | async-start | bytes 8912896 | tf_op jit(solution)/shard_map/all_gather | solution.py:287
  44.3 58.9 %copy-start.2 = (s32[1,16]{1,0:T(1,128)S(1)}, s32[1,16]{1,0:T(1,128)}, u32[]{:S(2)}) copy-start(s32[1,16]{1,0:T(1,128)} %param.11) | copy-start | bytes 196
  44.3 59.3 %copy-start.3 = (s32[128]{0:T(128)S(1)}, s32[128]{0:T(128)}, u32[]{:S(2)}) copy-start(s32[128]{0:T(128)} %param.9) | copy-start | bytes 1540
  44.4 59.4 %copy-start.1 = (s32[1,128]{1,0:T(1,128)S(1)}, s32[1,128]{1,0:T(1,128)}, u32[]{:S(2)}) copy-start(s32[1,128]{1,0:T(1,128)} %param.10) | copy-start | bytes 1540
  101.3 9.4 %collective-permute-start = (bf16[1024,2048]{1,0:T(8,128)(2,1)}, bf16[1024,2048]{1,0:T(8,128)(2,1)}, u32[]{:S(2)}, u32[]{:S(2)}) collective-permute-start(bf16[1024,2048]{1,0:T(8,128)(2,1)} %shard_map.88.own_hbm), channel_id=1, source_target_pairs={{0,16},{16,0},{32,48},{48,32},{64,80},{80,64},{96,112},{112,96},{1... | collective-permute-start | bytes 12582920 | tf_op jit(solution)/shard_map/ppermute | solution.py:291
  111.8 11.4 %copy-start = (bf16[128,2048]{1,0:T(8,128)(2,1)S(1)}, bf16[128,2048]{1,0:T(8,128)(2,1)}, u32[]{:S(2)}) copy-start(bf16[128,2048]{1,0:T(8,128)(2,1)} %teacher_ref.3) | copy-start | bytes 1572868
  124.8 15.0 %all-to-all-start.1 = ((f32[32,8,128]{2,1,0:T(8,128)}), f32[32,8,128]{2,1,0:T(8,128)S(1)}, u32[]{:S(2)}, u32[]{:S(2)}) async-start(f32[32,8,128]{2,1,0:T(8,128)} %shard_map.89), calls=%async_computation.1 | async-start | bytes 262144 | tf_op jit(solution)/shard_map/all_to_all | solution.py:305
  141.5 40.6 %all-to-all-start.2 = ((bf16[16,128,128]{2,1,0:T(8,128)(2,1)}), bf16[16,128,128]{2,1,0:T(8,128)(2,1)S(1)}, u32[]{:S(2)}, u32[]{:S(2)}) async-start(bf16[16,128,128]{2,1,0:T(8,128)(2,1)} %get-tuple-element.13), calls=%async_computation.2 | async-start | bytes 1048576 | tf_op jit(solution)/shard_map/all_to_all | solution.py:309
  159.6 3.4 %collective-permute-start.1 = (bf16[16,64,128]{2,1,0:T(8,128)(2,1)S(1)}, bf16[16,64,128]{2,1,0:T(8,128)(2,1)S(1)}, u32[]{:S(2)}, u32[]{:S(2)}) collective-permute-start(bf16[16,64,128]{2,1,0:T(8,128)(2,1)S(1)} %dynamic-slice_bitcast_fusion), channel_id=1, source_target_pairs={{0,16},{16,0},{32,48},{48,32},{64,80},{80,64},{96,112},{112,96},{1... | collective-permute-start | bytes 786440 | tf_op jit(solution)/shard_map/ppermute | solution.py:314
  163.2 9.0 %collective-permute-start.2 = (bf16[4,64,128]{2,1,0:T(8,128)(2,1)S(1)}, bf16[4,64,128]{2,1,0:T(8,128)(2,1)S(1)}, u32[]{:S(2)}, u32[]{:S(2)}) collective-permute-start(bf16[4,64,128]{2,1,0:T(8,128)(2,1)S(1)} %get-tuple-element.27), channel_id=1, source_target_pairs={{0,128},{16,144},{32,160},{48,176},{64,192},{80,208},{96,224},{112... | collective-permute-start | bytes 196616 | tf_op jit(solution)/shard_map/ppermute | solution.py:38
  165.7 6.6 %collective-permute-start.4 = (bf16[4,64,128]{2,1,0:T(8,128)(2,1)S(1)}, bf16[4,64,128]{2,1,0:T(8,128)(2,1)S(1)}, u32[]{:S(2)}, u32[]{:S(2)}) collective-permute-start(bf16[4,64,128]{2,1,0:T(8,128)(2,1)S(1)} %get-tuple-element.28), channel_id=1, source_target_pairs={{0,384},{16,400},{32,416},{48,432},{64,448},{80,464},{96,480},{112... | collective-permute-start | bytes 196616 | tf_op jit(solution)/shard_map/ppermute | solution.py:38
  170.3 7.7 %collective-permute-start.3 = (bf16[4,64,128]{2,1,0:T(8,128)(2,1)S(1)}, bf16[4,64,128]{2,1,0:T(8,128)(2,1)S(1)}, u32[]{:S(2)}, u32[]{:S(2)}) collective-permute-start(bf16[4,64,128]{2,1,0:T(8,128)(2,1)S(1)} %get-tuple-element.29), channel_id=1, source_target_pairs={{0,256},{16,272},{32,288},{48,304},{64,320},{80,336},{96,352},{112... | collective-permute-start | bytes 196616 | tf_op jit(solution)/shard_map/ppermute | solution.py:38
  187.9 38.3 %all-to-all-start.3 = ((bf16[16,144,128]{2,1,0:T(8,128)(2,1)}), bf16[16,144,128]{2,1,0:T(8,128)(2,1)S(1)}, u32[]{:S(2)}, u32[]{:S(2)}) async-start(bf16[16,144,128]{2,1,0:T(8,128)(2,1)} %shard_map.91), calls=%async_computation.3 | async-start | bytes 1179648 | tf_op jit(solution)/shard_map/all_to_all | solution.py:327
  196.0 9.0 %collective-permute-start.5 = (bf16[64,128]{1,0:T(8,128)(2,1)S(1)}, bf16[64,128]{1,0:T(8,128)(2,1)S(1)}, u32[]{:S(2)}, u32[]{:S(2)}) collective-permute-start(bf16[64,128]{1,0:T(8,128)(2,1)S(1)} %get-tuple-element.30), channel_id=1, source_target_pairs={{0,32},{16,48},{32,64},{48,80},{64,96},{80,112},{96,0},{112,16},{1... | collective-permute-start | bytes 49160 | tf_op jit(solution)/shard_map/ppermute | solution.py:38
  198.5 6.6 %collective-permute-start.7 = (bf16[64,128]{1,0:T(8,128)(2,1)S(1)}, bf16[64,128]{1,0:T(8,128)(2,1)S(1)}, u32[]{:S(2)}, u32[]{:S(2)}) collective-permute-start(bf16[64,128]{1,0:T(8,128)(2,1)S(1)} %get-tuple-element.31), channel_id=1, source_target_pairs={{0,96},{16,112},{32,0},{48,16},{64,32},{80,48},{96,64},{112,80},{1... | collective-permute-start | bytes 49160 | tf_op jit(solution)/shard_map/ppermute | solution.py:38
  203.1 7.1 %collective-permute-start.6 = (bf16[64,128]{1,0:T(8,128)(2,1)S(1)}, bf16[64,128]{1,0:T(8,128)(2,1)S(1)}, u32[]{:S(2)}, u32[]{:S(2)}) collective-permute-start(bf16[64,128]{1,0:T(8,128)(2,1)S(1)} %get-tuple-element.32), channel_id=1, source_target_pairs={{0,64},{16,80},{32,96},{48,112},{64,0},{80,16},{96,32},{112,48},{1... | collective-permute-start | bytes 49160 | tf_op jit(solution)/shard_map/ppermute | solution.py:38
Sparse Core Ops, SparseCore 0:
  10.1 108.4 all-gather.2
